TPU v7x, 32 devices: a whole 2x2x4 slice. The times are simulated.
32 devices in a mesh: groups: 2 (over x), ctx: 16 (over z, y, core).
Axes of the slice: x: 2, y: 2, z: 4, core: 2. Of those that a mesh axis runs over, the one named last changes fastest.
Arguments:
- key_cache: bfloat16 [4, 16384, 128], P(None, ('groups', 'ctx')), parts along dimension 1, may hold values from -16 to 16
- value_cache: bfloat16 [4, 16384, 128], P(None, ('groups', 'ctx')), parts along dimension 1, may hold values from -6 to 6
- init_centroids: bfloat16 [4, 1024, 128], replicated, may hold values from -6 to 6
- block_clusters: int32 [4, 128], P(None, 'groups'), parts along dimension 1, may hold values from 0 to 1023, as said below
- chosen_clusters: int32 [16, 4, 32], P('groups'), parts along dimension 0, may hold values from 0 to 1023, as said below
- request_positions: int32 [16], P('groups'), parts along dimension 0, may hold values from 1 to 8192, as said below
- queries: bfloat16 [16, 4, 8, 128], P('groups'), parts along dimension 0, may hold values from -640 to 640
Outputs:
- centroids: float32 [4, 2048, 128], P(None, ('groups', 'ctx')), parts along dimension 1
- attended: bfloat16 [16, 4, 8, 128], P('groups'), parts along dimension 0
There are 2 independent parts, one for each index of `groups`. A program takes and returns all parts, laid end to end along the dimension named above; an argument that names none is the same for every part. Nothing has to cross between parts.
Inputs may be any that keep to these rules, and one draw needn't show every extreme that they name: `block_clusters`: the owner of cluster c is the ctx index c // 64. Over the 4 x 4 pairs (head, block) of one device's blocks, at most 2 pairs have clusters of one owner; 2 owners get exactly 2 pairs from every device. `chosen_clusters`: the 32 clusters of one request and head are distinct. `request_positions`: at least half of the requests see all 8192 tokens.
All inputs are finite; a program needn't handle non-finite values.
Results may differ from a plain program's by a relative error of at most 0.0078.
Values may be sent and summed in bfloat16 or wider, within the bound.
No kernel may reach another device: no remote copies, remote signals or barrier semaphores. Data moves between devices by JAX's collectives and lax.ppermute only.
A program may use at most 64 MiB of HBM per device.

v0:
```python
import math

import jax
import jax.numpy as jnp
from jax import lax
from jax.sharding import PartitionSpec as P

BLOCK = 128


SHARPNESS = 16.0
EPSILON = 1e-06
NEGATIVE = -1e30


def merged(part, axis, combine):
    gathered = jax.tree.map(lambda a: lax.all_gather(a, axis), part)

    def take(source):
        return jax.tree.map(lambda a: lax.dynamic_index_in_dim(a, source, 0, False), gathered)

    return lax.fori_loop(
        1, lax.axis_size(axis), lambda source, state: combine(state, take(source)), take(0)
    )


def to_unit(vectors):
    vectors = vectors.astype(jnp.float32)
    return (
        vectors
        * lax.rsqrt(jnp.mean(vectors * vectors, axis=-1, keepdims=True) + EPSILON)
        * vectors.shape[-1] ** (-0.5)
    )


def local_sums(key_cache, value_cache, current, with_values):
    head_count, token_count, head_dim = key_cache.shape
    cluster_count = current.shape[1]
    block_rows = math.gcd(512, token_count)
    turn_count = token_count // block_rows

    def local_advance(running, turn_index):
        unit_keys = to_unit(key_cache).astype(jnp.bfloat16)
        cosine = jnp.einsum("htd,hcd->htc", unit_keys, current, preferred_element_type=jnp.float32)
        raised = jnp.exp(SHARPNESS * (cosine - 1.0))
        weights = (raised / jnp.sum(raised, axis=2, keepdims=True)).astype(jnp.bfloat16)
        key_sums = running[0] + jnp.einsum(
            "htc,htd->hcd", weights, key_cache, preferred_element_type=jnp.float32
        )
        if with_values:
            masses = running[1] + jnp.sum(weights.astype(jnp.float32), axis=1)
            value_sums = running[2] + jnp.einsum(
                "htc,htd->hcd", weights, value_cache, preferred_element_type=jnp.float32
            )
            return ((key_sums, masses, value_sums), None)
        return ((key_sums,), None)

    start = (jnp.zeros((head_count, cluster_count, head_dim), jnp.float32),)
    if with_values:
        start = (
            start[0],
            jnp.zeros((head_count, cluster_count), jnp.float32),
            jnp.zeros((head_count, cluster_count, head_dim), jnp.float32),
        )
    running, _ = lax.scan(local_advance, start, jnp.arange(turn_count, dtype=jnp.int32))
    return running


def summary_part(queries, mean_keys, mean_values, log_mass, chosen_clusters, first_owned):
    head_dim = queries.shape[3]
    owned_ids = first_owned + jnp.arange(mean_keys.shape[1], dtype=jnp.int32)
    unpicked = jnp.logical_not(
        jnp.any(chosen_clusters[:, :, :, None] == owned_ids[None, None, None, :], axis=2)
    )
    scores = jnp.einsum(
        "rhgd,hcd->rhgc", queries, mean_keys, preferred_element_type=jnp.float32
    ) * head_dim ** (-0.5)
    scores = scores + log_mass[None, :, None, :]
    usable = unpicked[:, :, None, :]
    peak = jnp.max(jnp.where(usable, scores, NEGATIVE), axis=3)
    probability = jnp.where(usable, jnp.exp(scores - peak[..., None]), 0.0).astype(jnp.bfloat16)
    weight_sum = jnp.sum(probability.astype(jnp.float32), axis=3)
    weighted = jnp.einsum(
        "rhgc,hcd->rhgd", probability, mean_values, preferred_element_type=jnp.float32
    )
    return (peak, weight_sum, weighted)


def attend(
    queries,
    key_blocks,
    value_blocks,
    head_of,
    block_of,
    cluster_of,
    filled,
    chosen_clusters,
    request_positions,
    running,
):
    requests, head_count, group_size, head_dim = queries.shape
    slot_count, span = (key_blocks.shape[0], key_blocks.shape[1])
    per_turn = 8
    turn_count = slot_count // per_turn
    picked = jnp.take(chosen_clusters, head_of, axis=1)
    selected = filled[None, :] & jnp.any(picked == cluster_of[None, :, None], axis=2)
    score_scale = head_dim ** (-0.5)
    lane_ids = jnp.arange(span, dtype=jnp.int32)
    head_ids = jnp.arange(head_count, dtype=jnp.int32)

    def attend_advance(state, sliced):
        key_block, value_block, slot_heads, slot_blocks, slot_pick = sliced
        peak, weight_sum, weighted = state
        query_rows = jnp.take(queries, slot_heads, axis=1)
        scores = (
            jnp.einsum("rsgd,sid->rsgi", query_rows, key_block, preferred_element_type=jnp.float32)
            * score_scale
        )
        places = slot_blocks[:, None] * span + lane_ids[None, :]
        usable = slot_pick[:, :, None, None] & (
            places[None, :, None, :] < request_positions[:, None, None, None]
        )
        slot_peak = jnp.max(jnp.where(usable, scores, NEGATIVE), axis=3)
        onehot = slot_heads[:, None] == head_ids[None, :]
        candidate = jnp.max(
            jnp.where(onehot[None, :, :, None], slot_peak[:, :, None, :], NEGATIVE), axis=1
        )
        new_peak = jnp.maximum(peak, candidate)
        slot_ref = jnp.take(new_peak, slot_heads, axis=1)
        probability = jnp.where(usable, jnp.exp(scores - slot_ref[..., None]), 0.0).astype(
            jnp.bfloat16
        )
        slot_sum = jnp.sum(probability.astype(jnp.float32), axis=3)
        slot_weighted = jnp.einsum(
            "rsgi,sid->rsgd", probability, value_block, preferred_element_type=jnp.float32
        )
        rescale = jnp.exp(peak - new_peak)
        weight_sum = weight_sum * rescale + jnp.sum(
            jnp.where(onehot[None, :, :, None], slot_sum[:, :, None, :], 0.0), axis=1
        )
        weighted = weighted * rescale[..., None] + jnp.sum(
            jnp.where(onehot[None, :, :, None, None], slot_weighted[:, :, None], 0.0), axis=1
        )
        return ((new_peak, weight_sum, weighted), None)

    sliced = (
        key_blocks.reshape(turn_count, per_turn, span, head_dim),
        value_blocks.reshape(turn_count, per_turn, span, head_dim),
        head_of.reshape(turn_count, per_turn),
        block_of.reshape(turn_count, per_turn),
        jnp.transpose(selected.reshape(requests, turn_count, per_turn), (1, 0, 2)),
    )
    state, _ = lax.scan(attend_advance, running, sliced)
    return state


def combine(former, latter):
    peak = jnp.maximum(former[0], latter[0])
    left_factor = jnp.exp(former[0] - peak)
    right_factor = jnp.exp(latter[0] - peak)
    return (
        peak,
        former[1] * left_factor + latter[1] * right_factor,
        former[2] * left_factor[..., None] + latter[2] * right_factor[..., None],
    )


def body(
    key_cache,
    value_cache,
    init_centroids,
    block_clusters,
    chosen_clusters,
    request_positions,
    queries,
):
    devices = lax.axis_size("ctx")
    own_index = lax.axis_index("ctx")
    head_count, tok_dev, head_dim = key_cache.shape
    cluster_count = init_centroids.shape[1]
    per_owner = cluster_count // devices
    blk_dev = tok_dev // BLOCK
    entries = head_count * blk_dev
    start = to_unit(init_centroids).astype(jnp.bfloat16)
    (partial_value,) = local_sums(key_cache, value_cache, start, False)
    owned_part = lax.psum_scatter(partial_value, "ctx", scatter_dimension=1, tiled=True)
    current = lax.all_gather(to_unit(owned_part).astype(jnp.bfloat16), "ctx", axis=1, tiled=True)
    key_sums, masses, value_sums = local_sums(key_cache, value_cache, current, True)
    owned_keys, owned_mass, owned_values = (
        lax.psum_scatter(key_sums, "ctx", scatter_dimension=1, tiled=True),
        lax.psum_scatter(masses, "ctx", scatter_dimension=1, tiled=True),
        lax.psum_scatter(value_sums, "ctx", scatter_dimension=1, tiled=True),
    )
    centroids = to_unit(owned_keys)
    mean_keys = (owned_keys / owned_mass[..., None]).astype(jnp.bfloat16)
    mean_values = (owned_values / owned_mass[..., None]).astype(jnp.bfloat16)
    log_mass = jnp.log(owned_mass)
    running = summary_part(
        queries, mean_keys, mean_values, log_mass, chosen_clusters, own_index * per_owner
    )
    cluster_grid = jnp.transpose(
        block_clusters.reshape(head_count, devices, blk_dev), (1, 0, 2)
    ).reshape(devices, entries)
    entry_ids = jnp.arange(entries, dtype=jnp.int32)
    own_clusters = lax.dynamic_index_in_dim(cluster_grid, own_index, 0, keepdims=False)
    head_of = entry_ids // blk_dev
    block_of = own_index * blk_dev + entry_ids % blk_dev
    filled = jnp.ones((entries,), jnp.bool_)
    running = attend(
        queries,
        key_cache.reshape(entries, BLOCK, head_dim),
        value_cache.reshape(entries, BLOCK, head_dim),
        head_of,
        block_of,
        own_clusters,
        filled,
        chosen_clusters,
        request_positions,
        running,
    )
    peak, weight_sum, weighted = merged(running, "ctx", combine)
    attended = (weighted / weight_sum[..., None]).astype(jnp.bfloat16)
    return (centroids, attended)


def solution(mesh):
    placed = (
        P(None, ("groups", "ctx"), None),
        P(None, ("groups", "ctx"), None),
        P(),
        P(None, "groups"),
        P("groups", None, None),
        P("groups"),
        P("groups", None, None, None),
    )
    return jax.shard_map(
        body,
        mesh=mesh,
        in_specs=placed,
        out_specs=(P(None, ("groups", "ctx"), None), P("groups", None, None, None)),
        check_vma=False,
    )
```

profile of v0, /device:TPU:0, one launch (start us, length us, event | category | flops | bytes accessed | tf_op | source)
XLA Modules:
  0.0 389.2 jit_solution(5049722459949143035)
XLA Ops:
  7.2 1.4 fusion.32
  8.7 1.8 fusion.27
  10.6 3.7 fusion.24
  14.2 3.7 fusion.26
  18.0 64.3 %reduce-scatter.7.cloned.1.call-done = f32[4,64,128]{2,1,0:T(8,128)} async-done(((f32[4,1024,128]{2,1,0:T(8,128)}), f32[4,64,128]{2,1,0:T(8,128)}) %reduce-scatter.7.cloned.1.call-update) | async-done | bytes 131088 | tf_op jit(solution)/shard_map/reduce_scatter | solution.py:186
  83.3 1.6 multiply_convert_fusion
  85.0 37.2 %all-gather.6.cloned.1.call-done = bf16[4,1024,128]{2,1,0:T(8,128)(2,1)} async-done(((bf16[4,64,128]{2,1,0:T(8,128)(2,1)}), bf16[4,1024,128]{2,1,0:T(8,128)(2,1)}) %all-gather.6.cloned.1.call-update) | async-done | bytes 1048592 | tf_op jit(solution)/shard_map/all_gather | solution.py:187
  122.3 3.2 fusion.25
  125.5 3.4 convert_reduce_fusion.1
  129.0 1.1 copy.91
  130.2 5.2 %fusion.55 = f32[4,1024,128]{2,1,0:T(8,128)} fusion(bf16[4,512,1024]{2,1,0:T(8,128)(2,1)} %get-tuple-element.439, bf16[4,512,128]{2,1,0:T(8,128)(2,1)S(1)} %copy-done.1), kind=kOutput, calls=%fused_computation.129 | convolution fusion | flops 536870912 | bytes 6815744 | tf_op jit(solution)/shard_map/while/body/eval_jaxpr/htc,htd->hcd/dot_general | solution.py:47
  135.4 5.2 %fusion.56 = f32[4,1024,128]{2,1,0:T(8,128)} fusion(bf16[4,512,1024]{2,1,0:T(8,128)(2,1)} %get-tuple-element.439, bf16[4,512,128]{2,1,0:T(8,128)(2,1)S(1)} %copy-done.5), kind=kOutput, calls=%fused_computation.130 | convolution fusion | flops 536870912 | bytes 6815744 | tf_op jit(solution)/shard_map/while/body/eval_jaxpr/htc,htd->hcd/dot_general | solution.py:52
  142.4 42.5 %reduce-scatter.13.cloned.1.call-done = f32[64,4]{1,0:T(8,128)} async-done(((f32[1024,4]{1,0:T(8,128)}), f32[64,4]{1,0:T(8,128)}) %reduce-scatter.13.cloned.1.call-update) | async-done | bytes 1040
  185.8 63.3 %reduce-scatter.9.cloned.1.call-done = f32[4,64,128]{2,1,0:T(8,128)} async-done(((f32[4,1024,128]{2,1,0:T(8,128)}), f32[4,64,128]{2,1,0:T(8,128)}) %reduce-scatter.9.cloned.1.call-update) | async-done | bytes 131088 | tf_op jit(solution)/shard_map/reduce_scatter | solution.py:190
  249.2 1.2 select_reduce_fusion.4
  250.6 63.2 %reduce-scatter.11.cloned.1.call-done = f32[4,64,128]{2,1,0:T(8,128)} async-done(((f32[4,1024,128]{2,1,0:T(8,128)}), f32[4,64,128]{2,1,0:T(8,128)}) %reduce-scatter.11.cloned.1.call-update) | async-done | bytes 131088 | tf_op jit(solution)/shard_map/reduce_scatter | solution.py:192
  313.8 1.2 convolution_bitcast_fusion.1
  315.0 6.4 %while.11 = (s32[]{:T(128)}, f32[8,4,8]{2,0,1:T(8,128)S(1)}, f32[8,4,8]{2,0,1:T(8,128)S(1)}, f32[8,4,8,128]{3,2,1,0:T(8,128)S(1)}, s32[2,8]{1,0:T(2,128)S(1)}, /...) while((s32[]{:T(128)}, f32[8,4,8]{2,0,1:T(8,128)S(1)}, ...), condition=%wide.region_21.22_spmd.clone, body=%wide.region_15.21_spmd.clone.sunk | while | flops 34924656 | bytes 2874781 | solution.py:153
  322.1 20.2 %all-gather = f32[128,4,8]{2,0,1:T(8,128)S(1)} all-gather(f32[8,4,8]{2,0,1:T(8,128)S(1)} %get-tuple-element.281), channel_id=2, replica_groups=mesh['groups'=2,'ctx'=16] {'ctx'}, dimensions={0}, use_global_device_ids=true | all-gather | bytes 17408 | tf_op jit(solution)/shard_map/all_gather | solution.py:17
  342.4 18.5 %all-gather.1 = f32[128,4,8]{2,0,1:T(8,128)S(1)} all-gather(f32[8,4,8]{2,0,1:T(8,128)S(1)} %get-tuple-element.282), channel_id=3, replica_groups=mesh['groups'=2,'ctx'=16] {'ctx'}, dimensions={0}, use_global_device_ids=true | all-gather | bytes 17408 | tf_op jit(solution)/shard_map/all_gather | solution.py:17
  361.8 1.7 all-gather.8.cloned.1.call-done
  364.4 17.3 %while.10 = (s32[]{:T(128)}, f32[8,4,8]{2,1,0:T(4,128)S(1)}, f32[8,4,8]{2,1,0:T(4,128)S(1)}, f32[8,4,8,128]{3,2,1,0:T(8,128)S(1)}, f32[16,8,4,8]{3,1,0,2:T(8,128...) while((s32[]{:T(128)}, f32[8,4,8]{2,1,0:T(4,128)S(1)}, ...), condition=%wide.region_23.24_spmd, body=%wide.region_22.23_spmd.sunk | while | flops 99845 | bytes 407703 | solution.py:22
  365.6 1.1 fusion.71
  366.7 1.1 fusion.71
  (152 shorter events, 28.1 us)
Async XLA Ops:
  7.2 7.1 %copy-start.1 = (bf16[4,512,128]{2,1,0:T(8,128)(2,1)S(1)}, bf16[4,512,128]{2,1,0:T(8,128)(2,1)}, u32[]{:S(2)}) copy-start(bf16[4,512,128]{2,1,0:T(8,128)(2,1)} %param.11) | copy-start | bytes 1572868
  7.2 75.1 %reduce-scatter.7.cloned.1.call-start = ((), (), s32[]{:S(2)}) async-start(), calls=%async_computation.4 | async-start | bytes 2228224 | tf_op jit(solution)/shard_map/reduce_scatter | solution.py:186
  17.9 104.4 %all-gather.6.cloned.1.call-start = ((), (), s32[]{:S(2)}) async-start(), calls=%async_computation.5 | async-start | bytes 1114112 | tf_op jit(solution)/shard_map/all_gather | solution.py:187
  85.0 100.0 %reduce-scatter.13.cloned.1.call-start = ((), (), s32[]{:S(2)}) async-start(), calls=%async_computation.9 | async-start | bytes 557056
  125.5 9.9 %copy-start.5 = (bf16[4,512,128]{2,1,0:T(8,128)(2,1)S(1)}, bf16[4,512,128]{2,1,0:T(8,128)(2,1)}, u32[]{:S(2)}) copy-start(bf16[4,512,128]{2,1,0:T(8,128)(2,1)} %param.12) | copy-start | bytes 1572868
  130.1 119.1 %reduce-scatter.9.cloned.1.call-start = ((), (), s32[]{:S(2)}) async-start(), calls=%async_computation.6 | async-start | bytes 2228224 | tf_op jit(solution)/shard_map/reduce_scatter | solution.py:190
  130.1 10.6 %copy-start = (s32[8,4,32]{2,1,0:T(4,128)S(1)}, s32[8,4,32]{2,1,0:T(4,128)}, u32[]{:S(2)}) copy-start(s32[8,4,32]{2,1,0:T(4,128)} %param.15) | copy-start | bytes 12292
  130.1 10.8 %copy-start.7 = (s32[4,64]{1,0:T(4,128)S(1)}, s32[4,64]{1,0:T(4,128)}, u32[]{:S(2)}) copy-start(s32[4,64]{1,0:T(4,128)} %param.14) | copy-start | bytes 3076
  130.2 119.0 %copy-start.2 = (bf16[8,4,8,128]{3,2,1,0:T(8,128)(2,1)S(1)}, bf16[8,4,8,128]{3,2,1,0:T(8,128)(2,1)}, u32[]{:S(2)}) copy-start(bf16[8,4,8,128]{3,2,1,0:T(8,128)(2,1)} %param.17) | copy-start | bytes 196612
  135.3 179.7 %copy-start.6 = (s32[8]{0:T(128)S(1)}, s32[8]{0:T(128)}, u32[]{:S(2)}) copy-start(s32[8]{0:T(128)} %param.16) | copy-start | bytes 100
  135.4 178.5 %reduce-scatter.11.cloned.1.call-start = ((), (), s32[]{:S(2)}) async-start(), calls=%async_computation.7 | async-start | bytes 2228224 | tf_op jit(solution)/shard_map/reduce_scatter | solution.py:192
  140.6 222.8 %all-gather.8.cloned.1.call-start = ((), (), s32[]{:S(2)}) async-start(), calls=%async_computation.8 | async-start | bytes 2228224 | tf_op jit(solution)/shard_map/all_gather | solution.py:17
  315.0 45.9 %copy-start.4 = (f32[4,64,128]{2,1,0:T(8,128)S(1)}, f32[4,64,128]{2,1,0:T(8,128)}, u32[]{:S(2)}) copy-start(f32[4,64,128]{2,1,0:T(8,128)} %reduce-scatter.9.cloned.1.call-done) | copy-start | bytes 393220
  321.4 0.7 copy-start.3
Sparse Core Ops, SparseCore 0:
  18.0 64.2 reduce-scatter.6
  85.3 36.9 all-gather.5
  130.2 54.7 reduce-scatter.12
  188.6 60.5 reduce-scatter.8
  253.2 60.5 reduce-scatter.10
  322.2 41.1 all-gather.7
where the time goes:
time: 390 us; the launch traced here: 389 us
  waiting for transfers between devices  272 us (70%)
  blocking collectives  38.7 us (10%)
  other arithmetic  30.7 us (8%)
  matrix products  24.6 us (6%)
  between operations  14.4 us (4%)
  local copies, waits for them, and re-layouts  7.37 us (2%)
    reduce_scatter x1, waiting for transfers between devices, body(): lax.psum_scatter(partial_value, 'ctx', scatter_dimension=1, tiled=True)  64.3 us
    reduce_scatter x1, waiting for transfers between devices, body(): lax.psum_scatter(key_sums, 'ctx', scatter_dimension=1, tiled=True)  63.3 us
    reduce_scatter x1, waiting for transfers between devices, body(): lax.psum_scatter(value_sums, 'ctx', scatter_dimension=1, tiled=True)  63.2 us
    unnamed x7, waiting for transfers between devices  42.6 us
    all_gather x2, blocking collectives, merged(): gathered = jax.tree.map(lambda a: lax.all_gather(a, axis), part)  38.7 us
    all_gather x1, waiting for transfers between devices, body(): lax.all_gather(to_unit(owned_part).astype(jnp.bfloat16), 'ctx', axis=1, t...  37.2 us
    add x15, other arithmetic, combine(): former[2] * left_factor[..., None] + latter[2] * right_factor[..., None]  16 us
    dot_general x2, matrix products, local_advance(): jnp.einsum('htc,htd->hcd', weights, key_cache, preferred_element_type=jnp...  8.82 us
  transfers between devices with their start and end apart: 6, of which 6 were waited for; matrix products, arithmetic and copies ran while one was open for 4% of the time, Pallas kernels for 0%

commit v1 on v0

v1 whole, which is shorter than its diff:
```python
import functools
import math

import jax
import jax.numpy as jnp
from jax import lax
from jax.experimental import pallas as pl
from jax.experimental.pallas import tpu as pltpu
from jax.sharding import PartitionSpec as P

BLOCK = 128
SHARPNESS = 16.0
EPSILON = 1e-06
NEGATIVE = -1e30
F32 = jnp.float32
BF16 = jnp.bfloat16
VMEM_BYTES = 48 * 1024 * 1024
TILE = 256


def to_unit(vectors):
    vectors = vectors.astype(F32)
    return (
        vectors
        * lax.rsqrt(jnp.mean(vectors * vectors, axis=-1, keepdims=True) + EPSILON)
        * vectors.shape[-1] ** (-0.5)
    )


def dot_nt(left, right):
    return lax.dot_general(left, right, (((1,), (1,)), ((), ())), preferred_element_type=F32)


def call(kernel, outs, args, scratch=(), flops=0, scalars=0):
    in_specs = [pl.BlockSpec(memory_space=pltpu.SMEM)] * scalars
    in_specs += [pl.BlockSpec(memory_space=pltpu.VMEM)] * (len(args) - scalars)
    touched = sum(a.size * a.dtype.itemsize for a in (*args, *outs))
    return pl.pallas_call(
        kernel,
        out_shape=tuple(outs),
        in_specs=in_specs,
        out_specs=tuple(pl.BlockSpec(memory_space=pltpu.VMEM) for _ in outs),
        scratch_shapes=list(scratch),
        compiler_params=pltpu.CompilerParams(vmem_limit_bytes=VMEM_BYTES),
        cost_estimate=pl.CostEstimate(flops=flops, bytes_accessed=touched, transcendentals=0),
    )(*args)


def shape(dims, dtype):
    return jax.ShapeDtypeStruct(dims, dtype)


def fill_weights(unit_keys, pieces, raised_ref, weight_ref, first, mass_ref):
    tokens = unit_keys.shape[0]
    factor = SHARPNESS * math.log2(math.e)
    total = jnp.zeros((1, tokens), F32)
    row = 0
    tiles = []
    for piece in pieces:
        tile = min(TILE, piece.shape[0])
        for at in range(0, piece.shape[0], tile):
            raised = jnp.exp2(dot_nt(piece[at : at + tile, :], unit_keys) * factor)
            raised_ref[row : row + tile, :tokens] = raised
            total = total + jnp.sum(raised, axis=0, keepdims=True)
            tiles.append((row, tile))
            row += tile
    inverse = 1.0 / total
    for row, tile in tiles:
        weights = raised_ref[row : row + tile, :tokens] * inverse
        weight_ref[row : row + tile, first : first + tokens] = weights.astype(BF16)
        if mass_ref is not None:
            part = weights[:, :128]
            for at in range(128, tokens, 128):
                part = part + weights[:, at : at + 128]
            if first == 0:
                mass_ref[row : row + tile, :] = part
            else:
                mass_ref[row : row + tile, :] += part


def first_kernel(key_ref, cent_ref, sums_ref, unit_ref, raised_ref, weight_ref):
    unit_ref[...] = to_unit(cent_ref[...]).astype(BF16)
    keys = key_ref[...]
    fill_weights(to_unit(keys).astype(BF16), (unit_ref,), raised_ref, weight_ref, 0, None)
    rows = sums_ref.shape[0]
    tile = min(TILE, rows)
    for row in range(0, rows, tile):
        sums_ref[row : row + tile, :] = jnp.dot(
            weight_ref[row : row + tile, :], keys, preferred_element_type=F32
        )


def rest_kernel(count, *refs):
    key_refs, (unit_ref, sums_ref, keep_ref, send_ref, raised_ref, weight_ref) = (
        refs[:count],
        refs[count:],
    )
    first = 0
    for key_ref in key_refs:
        unit_keys = to_unit(key_ref[...]).astype(BF16)
        fill_weights(unit_keys, (unit_ref,), raised_ref, weight_ref, first, None)
        first += unit_keys.shape[0]
    keys = jnp.concatenate([key_ref[...] for key_ref in key_refs], axis=0)
    half = keep_ref.shape[0]
    tile = min(TILE, half)
    for row in range(0, half, tile):
        keep_ref[row : row + tile, :] = sums_ref[row : row + tile, :] + jnp.dot(
            weight_ref[row : row + tile, :], keys, preferred_element_type=F32
        )
    for row in range(half, 2 * half, tile):
        send_ref[row - half : row - half + tile, :] = (
            sums_ref[row : row + tile, :]
            + jnp.dot(weight_ref[row : row + tile, :], keys, preferred_element_type=F32)
        ).astype(BF16)


def packed_masses(row, lanes):
    count = row.shape[1]
    high = row.astype(BF16).astype(F32)
    low = row - high
    rows = []
    for part in (high, low):
        if count < lanes:
            rows.append(jnp.concatenate([part, jnp.zeros((1, lanes - count), F32)], axis=1))
        else:
            rows += [part[:, at : at + lanes] for at in range(0, count, lanes)]
    rows.append(jnp.zeros((16 - len(rows), lanes), F32))
    return jnp.concatenate(rows, axis=0).astype(BF16)


def unpacked_masses(block, count):
    block = block.astype(F32)
    lanes = block.shape[1]
    if count < lanes:
        return block[0:1, :count] + block[1:2, :count]
    rows = count // lanes
    return jnp.concatenate(
        [block[i : i + 1, :] + block[rows + i : rows + i + 1, :] for i in range(rows)], axis=1
    )


def second_kernel(count, *refs):
    key_refs, value_refs = refs[:count], refs[count : 2 * count]
    own_ref, other_ref, keep_ref, keep_mass_ref, send_ref, raised_ref, weight_ref, mass_ref = refs[
        2 * count :
    ]
    first = 0
    for key_ref in key_refs:
        unit_keys = to_unit(key_ref[...]).astype(BF16)
        fill_weights(unit_keys, (own_ref, other_ref), raised_ref, weight_ref, first, mass_ref)
        first += unit_keys.shape[0]
    pairs = jnp.concatenate(
        [jnp.concatenate([k[...], v[...]], axis=1) for k, v in zip(key_refs, value_refs)], axis=0
    )
    half, lanes = keep_ref.shape
    tile = min(TILE, half)
    for row in range(half, 2 * half, tile):
        send_ref[row - half : row - half + tile, :] = jnp.dot(
            weight_ref[row : row + tile, :], pairs, preferred_element_type=F32
        ).astype(BF16)
    for row in range(0, half, tile):
        keep_ref[row : row + tile, :] = jnp.dot(
            weight_ref[row : row + tile, :], pairs, preferred_element_type=F32
        )
    masses = jnp.sum(mass_ref[...].T, axis=0, keepdims=True)
    keep_mass_ref[...] = jnp.broadcast_to(masses[:, :half], keep_mass_ref.shape)
    send_ref[half:, :] = packed_masses(masses[:, half:], lanes)


def halve_kernel(keep_ref, mass_ref, recv_ref, keep_out_ref, mass_out_ref, send_ref):
    count, lanes = keep_ref.shape
    half = count // 2
    masses = mass_ref[0:1, :] + unpacked_masses(recv_ref[count:, :], count)
    keep_out_ref[...] = keep_ref[:half, :] + recv_ref[:half, :].astype(F32)
    mass_out_ref[...] = jnp.broadcast_to(masses[:, :half], mass_out_ref.shape)
    send_ref[:half, :] = (keep_ref[half:, :] + recv_ref[half:count, :].astype(F32)).astype(BF16)
    send_ref[half:, :] = packed_masses(masses[:, half:], lanes)


def packed_state(peak, weight_sum, weighted):
    rows, dim = weighted.shape
    lane = lax.broadcasted_iota(jnp.int32, (rows, dim), 1)
    return jnp.concatenate([weighted, jnp.where(lane < dim // 2, peak, weight_sum)], axis=1)


def softmax_part(scores, usable, values):
    peak = jnp.max(jnp.where(usable, scores, NEGATIVE), axis=1, keepdims=True)
    probability = jnp.where(usable, jnp.exp(scores - peak), 0.0).astype(BF16)
    weight_sum = jnp.sum(probability.astype(F32), axis=1, keepdims=True)
    return peak, weight_sum, jnp.dot(probability, values, preferred_element_type=F32)


def joined(former, latter):
    peak = jnp.maximum(former[0], latter[0])
    left, right = jnp.exp(former[0] - peak), jnp.exp(latter[0] - peak)
    return (
        peak,
        former[1] * left + latter[1] * right,
        former[2] * left + latter[2] * right,
    )


def unpacked_state(state):
    dim = state.shape[1] // 2
    return state[:, dim : dim + 1], state[:, dim + dim // 2 : dim + dim // 2 + 1], state[:, :dim]


def exact_kernel(count, *refs):
    key_refs, value_refs = refs[:count], refs[count : 2 * count]
    query_ref, limit_ref, out_ref = refs[2 * count :]
    queries = query_ref[...]
    rows, dim = queries.shape
    keys = jnp.concatenate([k[...] for k in key_refs], axis=0)
    values = jnp.concatenate([v[...] for v in value_refs], axis=0)
    scores = dot_nt(queries, keys) * dim ** (-0.5)
    lane = lax.broadcasted_iota(jnp.int32, (rows, BLOCK), 1)
    usable = jnp.concatenate(
        [
            jnp.where(lane < limit_ref[:, i : i + 1], 1.0, 0.0)
            for i in range(keys.shape[0] // BLOCK)
        ],
        axis=1,
    )
    out_ref[...] = packed_state(*softmax_part(scores, usable > 0.5, values))


def summary_kernel(
    keep_ref, mass_ref, recv_ref, query_ref, usable_ref, exact_ref, state_ref, cent_ref
):
    count, lanes = keep_ref.shape
    dim = lanes // 2
    masses = mass_ref[0:1, :] + unpacked_masses(recv_ref[count:, :], count)
    sums = keep_ref[...] + recv_ref[:count, :].astype(F32)
    cent_ref[...] = to_unit(sums[:, :dim])
    column = jnp.broadcast_to(masses, (dim, count)).T
    mean_keys = (sums[:, :dim] / column).astype(BF16)
    mean_values = (sums[:, dim:] / column).astype(BF16)
    scores = dot_nt(query_ref[...], mean_keys) * dim ** (-0.5) + jnp.log(masses)
    state = softmax_part(scores, usable_ref[...] > 0.5, mean_values)
    state_ref[...] = packed_state(*joined(unpacked_state(exact_ref[...]), state))


def in_order(flip, own_ref, recv_ref):
    own, recv = own_ref[...], recv_ref[...]
    return jnp.where(flip, recv, own), jnp.where(flip, own, recv)


def merge_kernel(flip_ref, own_ref, recv_ref, out_ref):
    former, latter = in_order(flip_ref[0] != 0, own_ref, recv_ref)
    out_ref[...] = packed_state(*joined(unpacked_state(former), unpacked_state(latter)))


def last_merge_kernel(scalar_ref, own_ref, recv_ref, cent_ref, *pack_refs):
    former, latter = in_order(scalar_ref[0] != 0, own_ref, recv_ref)
    _, weight_sum, weighted = joined(unpacked_state(former), unpacked_state(latter))
    attended = weighted / weight_sum
    own = scalar_ref[1]
    per_owner = cent_ref.shape[1]
    for step, pack_ref in enumerate(pack_refs):
        pack_ref[:per_owner, :] = cent_ref[own ^ step]
        pack_ref[per_owner:, :] = attended


def spread_kernel(scalar_ref, *refs):
    pack_refs, (cent_ref, out_ref) = refs[:-2], refs[-2:]
    own = scalar_ref[0]
    per_owner = cent_ref.shape[1]
    requests, _, group, dim = out_ref.shape
    for step, pack_ref in enumerate(pack_refs):
        cent_ref[own ^ step] = pack_ref[:per_owner, :]
        for r in range(requests):
            at = per_owner + r * group
            out_ref[r, own ^ step] = pack_ref[at : at + group, :].astype(BF16)


def body(
    key_cache,
    value_cache,
    init_centroids,
    block_clusters,
    chosen_clusters,
    request_positions,
    queries,
):
    devices = lax.axis_size("ctx")
    index = lax.axis_index("ctx").astype(jnp.int32)
    heads, tok_dev, dim = key_cache.shape
    clusters = init_centroids.shape[1]
    requests, _, group, _ = queries.shape
    per_owner = clusters // devices
    blk_dev = tok_dev // BLOCK
    spread = devices // heads
    levels = spread.bit_length() - 1
    if heads * spread != devices or 1 << levels != spread or heads & (heads - 1) or levels < 2:
        raise ValueError("unsupported mesh")
    head, rank = index // spread, index % spread
    half = clusters // 2
    rows = requests * group
    owned = heads * per_owner

    def over(array, bit):
        return lax.ppermute(array, "ctx", [(i, i ^ bit) for i in range(devices)])

    def pick(array, at, axis=0):
        return lax.dynamic_index_in_dim(array, at, axis, keepdims=False)

    keys = [pick(key_cache, head)]
    keys += [over(pick(key_cache, head ^ s), s * spread) for s in range(1, heads)]

    by_rank = pick(init_centroids, head).reshape(heads, spread, per_owner, dim)
    reverse = [int(format(r, f"0{levels}b")[::-1], 2) for r in range(spread)]
    cents = jnp.stack([pick(by_rank, rank ^ r, 1) for r in reverse]).reshape(clusters, dim)

    pass_flops = 4 * tok_dev * clusters * dim
    sums, unit_cents = call(
        first_kernel,
        [shape((clusters, dim), F32), shape((clusters, dim), BF16)],
        [keys[0], cents],
        [pltpu.VMEM((clusters, tok_dev), F32), pltpu.VMEM((clusters, tok_dev), BF16)],
        pass_flops,
    )
    keep, send = call(
        functools.partial(rest_kernel, heads - 1),
        [shape((half, dim), F32), shape((half, dim), BF16)],
        [*keys[1:], unit_cents, sums],
        [
            pltpu.VMEM((clusters, tok_dev), F32),
            pltpu.VMEM((clusters, (heads - 1) * tok_dev), BF16),
        ],
        pass_flops * (heads - 1),
    )

    arrived = lax.optimization_barrier((value_cache, *keys[1:]))
    later_values = arrived[0]
    values = [pick(value_cache, head)]
    values += [over(pick(later_values, head ^ s), s * spread) for s in range(1, heads)]

    for level in range(levels - 1):
        total = keep + over(send, 1 << level).astype(F32)
        if level < levels - 2:
            cut = total.shape[0] // 2
            keep, send = total[:cut], total[cut:].astype(BF16)
    rounded = total.astype(BF16)
    recv = over(rounded, 1 << (levels - 1))
    cut = rounded.shape[0] // 2
    recv = jnp.concatenate([recv[cut:], recv[:cut]])
    own_cents = to_unit(rounded.astype(F32) + recv.astype(F32)).astype(BF16)
    for level in range(levels - 2, 0, -1):
        own_cents = jnp.concatenate([own_cents, over(own_cents, 1 << level)])
    other_cents = over(own_cents, 1)

    keep, keep_mass, send = call(
        functools.partial(second_kernel, heads),
        [
            shape((half, 2 * dim), F32),
            shape((8, half), F32),
            shape((half + 16, 2 * dim), BF16),
        ],
        [*keys, *values, own_cents, other_cents],
        [
            pltpu.VMEM((clusters, tok_dev), F32),
            pltpu.VMEM((clusters, heads * tok_dev), BF16),
            pltpu.VMEM((clusters, 128), F32),
        ],
        pass_flops * heads * 3 // 2,
    )

    own_queries = pick(queries, head, 1).reshape(rows, dim)
    own_chosen = pick(chosen_clusters, head, 1)
    places = jnp.stack([head ^ s for s in range(heads)])[:, None] * spread + rank
    block_ids = (places * blk_dev + jnp.arange(blk_dev, dtype=jnp.int32)).reshape(-1)
    held = pick(pick(block_clusters, head).reshape(heads, spread, blk_dev), rank, 1)
    held = jnp.stack([pick(held, head ^ s) for s in range(heads)]).reshape(-1)
    picked = jnp.any(own_chosen[:, :, None] == held, axis=1)
    limits = jnp.where(
        picked, jnp.clip(request_positions[:, None] - block_ids * BLOCK, 0, BLOCK), 0
    )
    limits = jnp.repeat(limits, group, axis=0)
    owners = jnp.arange(heads, dtype=jnp.int32)[:, None] * spread + rank
    owned_ids = (owners * per_owner + jnp.arange(per_owner, dtype=jnp.int32)).reshape(-1)
    usable = jnp.all(own_chosen[:, :, None] != owned_ids, axis=1).astype(F32)
    usable = jnp.repeat(usable, group, axis=0)

    (exact,) = call(
        functools.partial(exact_kernel, heads),
        [shape((rows, 2 * dim), F32)],
        [*keys, *values, own_queries, limits],
        (),
        4 * rows * heads * tok_dev * dim,
    )

    for level in range(levels - 1):
        recv = over(send, 1 << level)
        count = keep.shape[0] // 2
        keep, keep_mass, send = call(
            halve_kernel,
            [
                shape((count, 2 * dim), F32),
                shape((8, count), F32),
                shape((count + 16, 2 * dim), BF16),
            ],
            [keep, keep_mass, recv],
        )
    recv = over(send, 1 << (levels - 1))
    state, centroids = call(
        summary_kernel,
        [shape((rows, 2 * dim), F32), shape((owned, dim), F32)],
        [keep, keep_mass, recv, own_queries, usable, exact],
        (),
        4 * rows * owned * dim,
    )
    for level in range(levels - 1):
        flip = ((index >> level) & 1).reshape(1)
        (state,) = call(
            merge_kernel,
            [shape((rows, 2 * dim), F32)],
            [flip, state, over(state, 1 << level)],
            scalars=1,
        )
    scalars = jnp.stack([(index >> (levels - 1)) & 1, head])
    packs = call(
        last_merge_kernel,
        [shape((per_owner + rows, dim), F32)] * heads,
        [
            scalars,
            state,
            over(state, 1 << (levels - 1)),
            centroids.reshape(heads, per_owner, dim),
        ],
        scalars=1,
    )
    packs = [packs[0]] + [over(packs[s], s * spread) for s in range(1, heads)]
    return call(
        spread_kernel,
        [shape((heads, per_owner, dim), F32), shape(queries.shape, BF16)],
        [head.reshape(1), *packs],
        scalars=1,
    )


def solution(mesh):
    placed = (
        P(None, ("groups", "ctx"), None),
        P(None, ("groups", "ctx"), None),
        P(),
        P(None, "groups"),
        P("groups", None, None),
        P("groups"),
        P("groups", None, None, None),
    )
    return jax.shard_map(
        body,
        mesh=mesh,
        in_specs=placed,
        out_specs=(P(None, ("groups", "ctx"), None), P("groups", None, None, None)),
        check_vma=False,
    )
```

time: 390 us -> 66.4 us (0.17)
  waiting for transfers between devices: 272 us -> 32.8 us
  blocking collectives: 38.7 us -> 0 us
  other arithmetic: 30.7 us -> 1.17 us
  matrix products: 24.6 us -> 0 us
  starting transfers between devices: 0.25 us -> 17.7 us
  between operations: 14.4 us -> 0.9 us
  Pallas kernels: 0 us -> 9.77 us
    reduce_scatter x3 -> x0, waiting for transfers between devices: 191 us -> none  [the longest x1 64.3 us: body(): lax.psum_scatter(partial_value, 'ctx', scatter_dimension=1, tiled=True)]
    unnamed x7 -> x0, waiting for transfers between devices: 42.6 us -> none
    all_gather x2 -> x0, waiting for transfers between devices: 38.9 us -> none  [the longest x1 37.2 us: body(): lax.all_gather(to_unit(owned_part).astype(jnp.bfloat16), 'ctx', axis=1, t...]
    all_gather x2 -> x0, blocking collectives: 38.7 us -> none  [merged(): gathered = jax.tree.map(lambda a: lax.all_gather(a, axis), part)]
    ppermute x0 -> x16, waiting for transfers between devices: none -> 32.8 us  [over(): return lax.ppermute(array, 'ctx', [(i, i ^ bit) for i in range(devices)])]
    dot_general x11 -> x0, matrix products: 24.6 us -> none  [the longest x2 8.82 us: local_advance(): jnp.einsum('htc,htd->hcd', weights, key_cache, preferred_element_type=jnp...]
    ppermute x0 -> x16, starting transfers between devices: none -> 17.7 us  [over(): return lax.ppermute(array, 'ctx', [(i, i ^ bit) for i in range(devices)])]
    add x37 -> x1, other arithmetic: 17 us -> 0.07 us  [body(): owners * per_owner + jnp.arange(per_owner, dtype=jnp.int32)]
  transfers between devices with their start and end apart: 6 -> 16, of which waited for: 6 -> 9; matrix products, arithmetic and copies ran while one was open for 4% -> 6% of each run, Pallas kernels for 0% -> 3%
where the time goes in v1:
time: 66.4 us; the launch traced here: 66.2 us
  waiting for transfers between devices  32.8 us (49%)
  starting transfers between devices  17.7 us (27%)
  Pallas kernels  9.77 us (15%)
  local copies, waits for them, and re-layouts  3.84 us (6%)
  other arithmetic  1.17 us (2%)
  between operations  0.9 us (1%)
    ppermute x16, waiting for transfers between devices, over(): return lax.ppermute(array, 'ctx', [(i, i ^ bit) for i in range(devices)])  32.8 us
    ppermute x16, starting transfers between devices, over(): return lax.ppermute(array, 'ctx', [(i, i ^ bit) for i in range(devices)])  17.7 us
    pallas_call x9, Pallas kernels, call(): pl.pallas_call(kernel, out_shape=tuple(outs), in_specs=in_specs, out_spec...  9.77 us
    dynamic_slice x4, local copies, waits for them, and re-layouts, pick(): return lax.dynamic_index_in_dim(array, at, axis, keepdims=False)  1.47 us
  transfers between devices with their start and end apart: 16, of which 9 were waited for; matrix products, arithmetic and copies ran while one was open for 6% of the time, Pallas kernels for 3%

profile of v1, /device:TPU:0, one launch (start us, length us, event | category | flops | bytes accessed | tf_op | source)
XLA Modules:
  0.0 66.2 jit_solution(15679670340290111550)
XLA Ops:
  0.7 1.2 %dynamic-slice_bitcast_fusion.4 = (bf16[512,128]{1,0:T(8,128)(2,1)S(1)}, bf16[512,128]{1,0:T(8,128)(2,1)S(1)}, bf16[512,128]{1,0:T(8,128)(2,1)S(1)}, bf16[512,128]{1,0:T(8,128)(2,1)S(1)}) fusion(bf16[4,512,128]{2,1,0:T(8,128)(2,1)} %param.7, s32[]{:T(128)S(6)} %select_n.74, s32[]{:T(128)S(6)} %select_n.72, s32[]{:T(128)S(6)} %select_n.71, s32[]{:T(128)S(6)} %select_n.73), kind=kLoop, calls=%fused_computation.11 | loop fusion | bytes 1048592 | tf_op jit(solution)/shard_map/jit(dynamic_index_in_dim)/squeeze | solution.py:305
  1.9 3.1 %collective-permute-start = (bf16[512,128]{1,0:T(8,128)(2,1)S(1)}, bf16[512,128]{1,0:T(8,128)(2,1)S(1)}, u32[]{:S(2)}, u32[]{:S(2)}) collective-permute-start(bf16[512,128]{1,0:T(8,128)(2,1)S(1)} %get-tuple-element.40), channel_id=1, source_target_pairs={{0,4},{1,5},{2,6},{3,7},{4,0},{5,1},{6,2},{7,3},{8,12},{9,13},{10,... | collective-permute-start | bytes 393224 | tf_op jit(solution)/shard_map/ppermute | solution.py:302
  5.0 2.6 %collective-permute-start.1 = (bf16[512,128]{1,0:T(8,128)(2,1)S(1)}, bf16[512,128]{1,0:T(8,128)(2,1)S(1)}, u32[]{:S(2)}, u32[]{:S(2)}) collective-permute-start(bf16[512,128]{1,0:T(8,128)(2,1)S(1)} %get-tuple-element.42), channel_id=1, source_target_pairs={{0,8},{1,9},{2,10},{3,11},{4,12},{5,13},{6,14},{7,15},{8,0},{9,1},... | collective-permute-start | bytes 393224 | tf_op jit(solution)/shard_map/ppermute | solution.py:302
  7.6 0.7 %constant_dynamic-slice_fusion.5 = s32[8,1,32]{2,1,0:T(1,128)S(1)} fusion(s32[8,4,32]{2,1,0:T(4,128)} %param.11, s32[]{:T(128)S(6)} %select_n.71), kind=kLoop, calls=%fused_computation.28 | loop fusion | bytes 2052 | tf_op jit(solution)/shard_map/jit(dynamic_index_in_dim)/dynamic_slice | solution.py:305
  9.6 1.1 %shard_map.86 = (f32[1024,128]{1,0:T(8,128)S(1)}, bf16[1024,128]{1,0:T(8,128)(2,1)S(1)}) custom-call(bf16[512,128]{1,0:T(8,128)(2,1)S(1)} %get-tuple-element.41.key_ref.refs_0_, bf16[1024,128]{1,0:T(8,128)(2,1)S(1)} %bitcast.48), custom_call_target="tpu_custom_call" | custom-call | flops 268435456 | bytes 1179648 | tf_op jit(solution)/shard_map/pallas_call | solution.py:38
  11.0 6.9 %collective-permute-done.1.refs_1_.refs_2_ = bf16[512,128]{1,0:T(8,128)(2,1)S(1)} collective-permute-done((bf16[512,128]{1,0:T(8,128)(2,1)S(1)}, bf16[512,128]{1,0:T(8,128)(2,1)S(1)}, u32[]{:S(2)}, u32[]{:S(2)}) %collective-permute-start.1) | collective-permute-done | bytes 131104 | tf_op jit(solution)/shard_map/ppermute | solution.py:302
  17.9 2.4 %shard_map.87 = (f32[512,128]{1,0:T(8,128)S(1)}, bf16[512,128]{1,0:T(8,128)(2,1)S(1)}) custom-call(bf16[512,128]{1,0:T(8,128)(2,1)S(1)} %collective-permute-done.refs_0_.refs_1_, bf16[512,128]{1,0:T(8,128)(2,1)S(1)} %collective-permute-done.1.refs_1_.refs_2_, bf16[512,128]{1,0:T(8,128)(2,1)S(1)} %collective-permute-done.2.refs_2_.refs_3_, ...), custom_call_target="tpu_custom_call" | custom-call | flops 805306368 | bytes 1572864 | tf_op jit(solution)/shard_map/pallas_call | solution.py:38
  20.5 1.2 %collective-permute-done.6 = bf16[512,128]{1,0:T(8,128)(2,1)S(1)} collective-permute-done((bf16[512,128]{1,0:T(8,128)(2,1)S(1)}, bf16[512,128]{1,0:T(8,128)(2,1)S(1)}, u32[]{:S(2)}, u32[]{:S(2)}) %collective-permute-start.6) | collective-permute-done | bytes 131104 | tf_op jit(solution)/shard_map/ppermute | solution.py:302
  21.8 1.6 %collective-permute-start.7 = (bf16[512,128]{1,0:T(8,128)(2,1)S(1)}, bf16[512,128]{1,0:T(8,128)(2,1)S(1)}, u32[]{:S(2)}, u32[]{:S(2)}) collective-permute-start(bf16[512,128]{1,0:T(8,128)(2,1)S(1)} %add_convert_fusion), channel_id=1, source_target_pairs={{0,2},{1,3},{2,0},{3,1},{4,6},{5,7},{6,4},{7,5},{8,10},{9,11},{10,... | collective-permute-start | bytes 393224 | tf_op jit(solution)/shard_map/ppermute | solution.py:302
  23.4 2.0 %collective-permute-start.3 = (bf16[512,128]{1,0:T(8,128)(2,1)S(1)}, bf16[512,128]{1,0:T(8,128)(2,1)S(1)}, u32[]{:S(2)}, u32[]{:S(2)}) collective-permute-start(bf16[512,128]{1,0:T(8,128)(2,1)S(1)} %get-tuple-element.38), channel_id=1, source_target_pairs={{0,4},{1,5},{2,6},{3,7},{4,0},{5,1},{6,2},{7,3},{8,12},{9,13},{10,... | collective-permute-start | bytes 393224 | tf_op jit(solution)/shard_map/ppermute | solution.py:302
  25.4 1.1 %collective-permute-start.4 = (bf16[512,128]{1,0:T(8,128)(2,1)S(1)}, bf16[512,128]{1,0:T(8,128)(2,1)S(1)}, u32[]{:S(2)}, u32[]{:S(2)}) collective-permute-start(bf16[512,128]{1,0:T(8,128)(2,1)S(1)} %get-tuple-element.37), channel_id=1, source_target_pairs={{0,8},{1,9},{2,10},{3,11},{4,12},{5,13},{6,14},{7,15},{8,0},{9,1},... | collective-permute-start | bytes 393224 | tf_op jit(solution)/shard_map/ppermute | solution.py:302
  26.5 1.4 %collective-permute-start.5 = (bf16[512,128]{1,0:T(8,128)(2,1)S(1)}, bf16[512,128]{1,0:T(8,128)(2,1)S(1)}, u32[]{:S(2)}, u32[]{:S(2)}) collective-permute-start(bf16[512,128]{1,0:T(8,128)(2,1)S(1)} %get-tuple-element.36), channel_id=1, source_target_pairs={{0,12},{1,13},{2,14},{3,15},{4,8},{5,9},{6,10},{7,11},{8,4},{9,5},... | collective-permute-start | bytes 393224 | tf_op jit(solution)/shard_map/ppermute | solution.py:302
  28.5 2.1 %collective-permute-done.3.refs_5_ = bf16[512,128]{1,0:T(8,128)(2,1)S(1)} collective-permute-done((bf16[512,128]{1,0:T(8,128)(2,1)S(1)}, bf16[512,128]{1,0:T(8,128)(2,1)S(1)}, u32[]{:S(2)}, u32[]{:S(2)}) %collective-permute-start.3) | collective-permute-done | bytes 131104 | tf_op jit(solution)/shard_map/ppermute | solution.py:302
  30.6 7.8 %collective-permute-done.4.refs_6_ = bf16[512,128]{1,0:T(8,128)(2,1)S(1)} collective-permute-done((bf16[512,128]{1,0:T(8,128)(2,1)S(1)}, bf16[512,128]{1,0:T(8,128)(2,1)S(1)}, u32[]{:S(2)}, u32[]{:S(2)}) %collective-permute-start.4) | collective-permute-done | bytes 131104 | tf_op jit(solution)/shard_map/ppermute | solution.py:302
  38.4 3.4 %shard_map.88 = (f32[512,256]{1,0:T(8,128)S(1)}, f32[8,512]{1,0:T(8,128)S(1)}, bf16[528,256]{1,0:T(8,128)(2,1)S(1)}) custom-call(bf16[512,128]{1,0:T(8,128)(2,1)S(1)} %get-tuple-element.41.key_ref.refs_0_, bf16[512,128]{1,0:T(8,128)(2,1)S(1)} %collective-permute-done.refs_0_.refs_1_, bf16[512,128]{1,0:T(8,128)(2,1)S(1)} %collective-permute-done.1.refs_1_.refs_2_, ...), custom_call_target="tpu_custom_call" | custom-call | flops 1610612736 | bytes 2121728 | tf_op jit(solution)/shard_map/pallas_call | solution.py:38
  42.0 1.4 %collective-permute-done.9.recv_ref = bf16[528,256]{1,0:T(8,128)(2,1)S(1)} collective-permute-done((bf16[528,256]{1,0:T(8,128)(2,1)S(1)}, bf16[528,256]{1,0:T(8,128)(2,1)S(1)}, u32[]{:S(2)}, u32[]{:S(2)}) %collective-permute-start.9) | collective-permute-done | bytes 270368 | tf_op jit(solution)/shard_map/ppermute | solution.py:302
  44.0 0.7 %dynamic-slice_bitcast_fusion.12.refs_8_.query_ref = bf16[64,128]{1,0:T(8,128)(2,1)S(1)} fusion(bf16[8,4,8,128]{3,2,1,0:T(8,128)(2,1)} %param.13, s32[]{:T(128)S(6)} %select_n.71), kind=kLoop, calls=%fused_computation.22 | loop fusion | bytes 32772 | tf_op jit(solution)/shard_map/reshape | solution.py:368
  45.5 3.8 %collective-permute-done.10.recv_ref = bf16[272,256]{1,0:T(8,128)(2,1)S(1)} collective-permute-done((bf16[272,256]{1,0:T(8,128)(2,1)S(1)}, bf16[272,256]{1,0:T(8,128)(2,1)S(1)}, u32[]{:S(2)}, u32[]{:S(2)}) %collective-permute-start.10) | collective-permute-done | bytes 139296 | tf_op jit(solution)/shard_map/ppermute | solution.py:302
  49.9 1.2 %collective-permute-done.11.recv_ref = f32[64,256]{1,0:T(8,128)S(1)} collective-permute-done((f32[64,256]{1,0:T(8,128)S(1)}, f32[64,256]{1,0:T(8,128)S(1)}, u32[]{:S(2)}, u32[]{:S(2)}) %collective-permute-start.11) | collective-permute-done | bytes 65568 | tf_op jit(solution)/shard_map/ppermute | solution.py:302
  51.9 3.7 %collective-permute-done.12.recv_ref = f32[64,256]{1,0:T(8,128)S(1)} collective-permute-done((f32[64,256]{1,0:T(8,128)S(1)}, f32[64,256]{1,0:T(8,128)S(1)}, u32[]{:S(2)}, u32[]{:S(2)}) %collective-permute-start.12) | collective-permute-done | bytes 65568 | tf_op jit(solution)/shard_map/ppermute | solution.py:302
  56.3 2.1 %collective-permute-start.13 = (f32[128,128]{1,0:T(8,128)S(1)}, f32[128,128]{1,0:T(8,128)S(1)}, u32[]{:S(2)}, u32[]{:S(2)}) collective-permute-start(f32[128,128]{1,0:T(8,128)S(1)} %get-tuple-element.33), channel_id=1, source_target_pairs={{0,4},{1,5},{2,6},{3,7},{4,0},{5,1},{6,2},{7,3},{8,12},{9,13},{10,... | collective-permute-start | bytes 196616 | tf_op jit(solution)/shard_map/ppermute | solution.py:302
  58.3 1.0 %collective-permute-start.14 = (f32[128,128]{1,0:T(8,128)S(1)}, f32[128,128]{1,0:T(8,128)S(1)}, u32[]{:S(2)}, u32[]{:S(2)}) collective-permute-start(f32[128,128]{1,0:T(8,128)S(1)} %get-tuple-element.34), channel_id=1, source_target_pairs={{0,8},{1,9},{2,10},{3,11},{4,12},{5,13},{6,14},{7,15},{8,0},{9,1},... | collective-permute-start | bytes 196616 | tf_op jit(solution)/shard_map/ppermute | solution.py:302
  59.4 1.4 %collective-permute-start.15 = (f32[128,128]{1,0:T(8,128)S(1)}, f32[128,128]{1,0:T(8,128)S(1)}, u32[]{:S(2)}, u32[]{:S(2)}) collective-permute-start(f32[128,128]{1,0:T(8,128)S(1)} %get-tuple-element.35), channel_id=1, source_target_pairs={{0,12},{1,13},{2,14},{3,15},{4,8},{5,9},{6,10},{7,11},{8,4},{9,5},... | collective-permute-start | bytes 196616 | tf_op jit(solution)/shard_map/ppermute | solution.py:302
  60.8 4.7 %collective-permute-done.14.refs_2_ = f32[128,128]{1,0:T(8,128)S(1)} collective-permute-done((f32[128,128]{1,0:T(8,128)S(1)}, f32[128,128]{1,0:T(8,128)S(1)}, u32[]{:S(2)}, u32[]{:S(2)}) %collective-permute-start.14) | collective-permute-done | bytes 65568 | tf_op jit(solution)/shard_map/ppermute | solution.py:302
  (54 shorter events, 6.6 us)
Async XLA Ops:
  0.6 7.0 %copy-start = (bf16[4,1024,128]{2,1,0:T(8,128)(2,1)S(1)}, bf16[4,1024,128]{2,1,0:T(8,128)(2,1)}, u32[]{:S(2)}) copy-start(bf16[4,1024,128]{2,1,0:T(8,128)(2,1)} %param.9) | copy-start | bytes 3145732
  1.9 9.1 %collective-permute-start = (bf16[512,128]{1,0:T(8,128)(2,1)S(1)}, bf16[512,128]{1,0:T(8,128)(2,1)S(1)}, u32[]{:S(2)}, u32[]{:S(2)}) collective-permute-start(bf16[512,128]{1,0:T(8,128)(2,1)S(1)} %get-tuple-element.40), channel_id=1, source_target_pairs={{0,4},{1,5},{2,6},{3,7},{4,0},{5,1},{6,2},{7,3},{8,12},{9,13},{10,... | collective-permute-start | bytes 393224 | tf_op jit(solution)/shard_map/ppermute | solution.py:302
  5.0 12.9 %collective-permute-start.1 = (bf16[512,128]{1,0:T(8,128)(2,1)S(1)}, bf16[512,128]{1,0:T(8,128)(2,1)S(1)}, u32[]{:S(2)}, u32[]{:S(2)}) collective-permute-start(bf16[512,128]{1,0:T(8,128)(2,1)S(1)} %get-tuple-element.42), channel_id=1, source_target_pairs={{0,8},{1,9},{2,10},{3,11},{4,12},{5,13},{6,14},{7,15},{8,0},{9,1},... | collective-permute-start | bytes 393224 | tf_op jit(solution)/shard_map/ppermute | solution.py:302
  7.6 10.3 %collective-permute-start.2 = (bf16[512,128]{1,0:T(8,128)(2,1)S(1)}, bf16[512,128]{1,0:T(8,128)(2,1)S(1)}, u32[]{:S(2)}, u32[]{:S(2)}) collective-permute-start(bf16[512,128]{1,0:T(8,128)(2,1)S(1)} %get-tuple-element.39), channel_id=1, source_target_pairs={{0,12},{1,13},{2,14},{3,15},{4,8},{5,9},{6,10},{7,11},{8,4},{9,5},... | collective-permute-start | bytes 393224 | tf_op jit(solution)/shard_map/ppermute | solution.py:302
  17.9 2.5 %copy-start.2 = (s32[8]{0:T(128)S(1)}, s32[8]{0:T(128)}, u32[]{:S(2)}) copy-start(s32[8]{0:T(128)} %param.12) | copy-start | bytes 100
  20.3 3.1 %copy-start.1 = (bf16[4,512,128]{2,1,0:T(8,128)(2,1)S(1)}, bf16[4,512,128]{2,1,0:T(8,128)(2,1)}, u32[]{:S(2)}) copy-start(bf16[4,512,128]{2,1,0:T(8,128)(2,1)} %param.8) | copy-start | bytes 1572868
  20.4 1.4 %collective-permute-start.6 = (bf16[512,128]{1,0:T(8,128)(2,1)S(1)}, bf16[512,128]{1,0:T(8,128)(2,1)S(1)}, u32[]{:S(2)}, u32[]{:S(2)}) collective-permute-start(bf16[512,128]{1,0:T(8,128)(2,1)S(1)} %get-tuple-element.23), channel_id=1, source_target_pairs={{0,1},{1,0},{2,3},{3,2},{4,5},{5,4},{6,7},{7,6},{8,9},{9,8},{10,11... | collective-permute-start | bytes 393224 | tf_op jit(solution)/shard_map/ppermute | solution.py:302
  21.8 6.1 %collective-permute-start.7 = (bf16[512,128]{1,0:T(8,128)(2,1)S(1)}, bf16[512,128]{1,0:T(8,128)(2,1)S(1)}, u32[]{:S(2)}, u32[]{:S(2)}) collective-permute-start(bf16[512,128]{1,0:T(8,128)(2,1)S(1)} %add_convert_fusion), channel_id=1, source_target_pairs={{0,2},{1,3},{2,0},{3,1},{4,6},{5,7},{6,4},{7,5},{8,10},{9,11},{10,... | collective-permute-start | bytes 393224 | tf_op jit(solution)/shard_map/ppermute | solution.py:302
  23.4 7.1 %collective-permute-start.3 = (bf16[512,128]{1,0:T(8,128)(2,1)S(1)}, bf16[512,128]{1,0:T(8,128)(2,1)S(1)}, u32[]{:S(2)}, u32[]{:S(2)}) collective-permute-start(bf16[512,128]{1,0:T(8,128)(2,1)S(1)} %get-tuple-element.38), channel_id=1, source_target_pairs={{0,4},{1,5},{2,6},{3,7},{4,0},{5,1},{6,2},{7,3},{8,12},{9,13},{10,... | collective-permute-start | bytes 393224 | tf_op jit(solution)/shard_map/ppermute | solution.py:302
  25.4 12.9 %collective-permute-start.4 = (bf16[512,128]{1,0:T(8,128)(2,1)S(1)}, bf16[512,128]{1,0:T(8,128)(2,1)S(1)}, u32[]{:S(2)}, u32[]{:S(2)}) collective-permute-start(bf16[512,128]{1,0:T(8,128)(2,1)S(1)} %get-tuple-element.37), channel_id=1, source_target_pairs={{0,8},{1,9},{2,10},{3,11},{4,12},{5,13},{6,14},{7,15},{8,0},{9,1},... | collective-permute-start | bytes 393224 | tf_op jit(solution)/shard_map/ppermute | solution.py:302
  26.5 11.9 %collective-permute-start.5 = (bf16[512,128]{1,0:T(8,128)(2,1)S(1)}, bf16[512,128]{1,0:T(8,128)(2,1)S(1)}, u32[]{:S(2)}, u32[]{:S(2)}) collective-permute-start(bf16[512,128]{1,0:T(8,128)(2,1)S(1)} %get-tuple-element.36), channel_id=1, source_target_pairs={{0,12},{1,13},{2,14},{3,15},{4,8},{5,9},{6,10},{7,11},{8,4},{9,5},... | collective-permute-start | bytes 393224 | tf_op jit(solution)/shard_map/ppermute | solution.py:302
  28.2 10.1 %collective-permute-start.8 = (bf16[512,128]{1,0:T(8,128)(2,1)S(1)}, bf16[512,128]{1,0:T(8,128)(2,1)S(1)}, u32[]{:S(2)}, u32[]{:S(2)}) collective-permute-start(bf16[512,128]{1,0:T(8,128)(2,1)S(1)} %multiply_convert_fusion.refs_8_), channel_id=1, source_target_pairs={{0,1},{1,0},{2,3},{3,2},{4,5},{5,4},{6,7},{7,6},{8,9},{9,8},{10,11... | collective-permute-start | bytes 393224 | tf_op jit(solution)/shard_map/ppermute | solution.py:302
  41.8 1.6 %collective-permute-start.9 = (bf16[528,256]{1,0:T(8,128)(2,1)S(1)}, bf16[528,256]{1,0:T(8,128)(2,1)S(1)}, u32[]{:S(2)}, u32[]{:S(2)}) collective-permute-start(bf16[528,256]{1,0:T(8,128)(2,1)S(1)} %get-tuple-element.26), channel_id=1, source_target_pairs={{0,1},{1,0},{2,3},{3,2},{4,5},{5,4},{6,7},{7,6},{8,9},{9,8},{10,11... | collective-permute-start | bytes 811016 | tf_op jit(solution)/shard_map/ppermute | solution.py:302
  43.5 5.8 %collective-permute-start.10 = (bf16[272,256]{1,0:T(8,128)(2,1)S(1)}, bf16[272,256]{1,0:T(8,128)(2,1)S(1)}, u32[]{:S(2)}, u32[]{:S(2)}) collective-permute-start(bf16[272,256]{1,0:T(8,128)(2,1)S(1)} %get-tuple-element.29), channel_id=1, source_target_pairs={{0,2},{1,3},{2,0},{3,1},{4,6},{5,7},{6,4},{7,5},{8,10},{9,11},{10,... | collective-permute-start | bytes 417800 | tf_op jit(solution)/shard_map/ppermute | solution.py:302
  49.8 1.3 %collective-permute-start.11 = (f32[64,256]{1,0:T(8,128)S(1)}, f32[64,256]{1,0:T(8,128)S(1)}, u32[]{:S(2)}, u32[]{:S(2)}) collective-permute-start(f32[64,256]{1,0:T(8,128)S(1)} %get-tuple-element.30.own_ref), channel_id=1, source_target_pairs={{0,1},{1,0},{2,3},{3,2},{4,5},{5,4},{6,7},{7,6},{8,9},{9,8},{10,11... | collective-permute-start | bytes 196616 | tf_op jit(solution)/shard_map/ppermute | solution.py:302
  51.2 4.3 %collective-permute-start.12 = (f32[64,256]{1,0:T(8,128)S(1)}, f32[64,256]{1,0:T(8,128)S(1)}, u32[]{:S(2)}, u32[]{:S(2)}) collective-permute-start(f32[64,256]{1,0:T(8,128)S(1)} %shard_map.92.own_ref), channel_id=1, source_target_pairs={{0,2},{1,3},{2,0},{3,1},{4,6},{5,7},{6,4},{7,5},{8,10},{9,11},{10,... | collective-permute-start | bytes 196616 | tf_op jit(solution)/shard_map/ppermute | solution.py:302
  56.3 4.5 %collective-permute-start.13 = (f32[128,128]{1,0:T(8,128)S(1)}, f32[128,128]{1,0:T(8,128)S(1)}, u32[]{:S(2)}, u32[]{:S(2)}) collective-permute-start(f32[128,128]{1,0:T(8,128)S(1)} %get-tuple-element.33), channel_id=1, source_target_pairs={{0,4},{1,5},{2,6},{3,7},{4,0},{5,1},{6,2},{7,3},{8,12},{9,13},{10,... | collective-permute-start | bytes 196616 | tf_op jit(solution)/shard_map/ppermute | solution.py:302
  58.3 7.1 %collective-permute-start.14 = (f32[128,128]{1,0:T(8,128)S(1)}, f32[128,128]{1,0:T(8,128)S(1)}, u32[]{:S(2)}, u32[]{:S(2)}) collective-permute-start(f32[128,128]{1,0:T(8,128)S(1)} %get-tuple-element.34), channel_id=1, source_target_pairs={{0,8},{1,9},{2,10},{3,11},{4,12},{5,13},{6,14},{7,15},{8,0},{9,1},... | collective-permute-start | bytes 196616 | tf_op jit(solution)/shard_map/ppermute | solution.py:302
  59.4 6.1 %collective-permute-start.15 = (f32[128,128]{1,0:T(8,128)S(1)}, f32[128,128]{1,0:T(8,128)S(1)}, u32[]{:S(2)}, u32[]{:S(2)}) collective-permute-start(f32[128,128]{1,0:T(8,128)S(1)} %get-tuple-element.35), channel_id=1, source_target_pairs={{0,12},{1,13},{2,14},{3,15},{4,8},{5,9},{6,10},{7,11},{8,4},{9,5},... | collective-permute-start | bytes 196616 | tf_op jit(solution)/shard_map/ppermute | solution.py:302

commit v2 on v1

--- a/solution.py
+++ b/solution.py
@@ -293,7 +293,13 @@
     levels = spread.bit_length() - 1
     if heads * spread != devices or 1 << levels != spread or heads & (heads - 1) or levels < 2:
         raise ValueError("unsupported mesh")
-    head, rank = index // spread, index % spread
+    bits = heads.bit_length() - 1
+    head_masks = [s << 1 for s in range(heads)]
+    rank_masks = [1] + [1 << (bits + level) for level in range(1, levels)]
+    rank_masks[1] |= heads
+    far = index // (2 * heads)
+    head = (index // 2) % heads ^ (far % 2) * (heads // 2)
+    rank = far * 2 + index % 2
     half = clusters // 2
     rows = requests * group
     owned = heads * per_owner
@@ -305,11 +311,14 @@
         return lax.dynamic_index_in_dim(array, at, axis, keepdims=False)
 
     keys = [pick(key_cache, head)]
-    keys += [over(pick(key_cache, head ^ s), s * spread) for s in range(1, heads)]
-
-    by_rank = pick(init_centroids, head).reshape(heads, spread, per_owner, dim)
+    keys += [over(pick(key_cache, head ^ s), head_masks[s]) for s in range(1, heads)]
+
+    blocks = pick(init_centroids, head).reshape(spread // 4, 2, heads, 2, per_owner, dim)
+    blocks = jnp.stack([blocks[:, 0], jnp.roll(blocks[:, 1], heads // 2, axis=1)], axis=1)
+    by_rank = jnp.moveaxis(blocks.reshape(spread // 2, heads, 2, per_owner, dim), 2, 1)
+    by_rank = by_rank.reshape(spread, heads, per_owner, dim)
     reverse = [int(format(r, f"0{levels}b")[::-1], 2) for r in range(spread)]
-    cents = jnp.stack([pick(by_rank, rank ^ r, 1) for r in reverse]).reshape(clusters, dim)
+    cents = jnp.stack([pick(by_rank, rank ^ r) for r in reverse]).reshape(clusters, dim)
 
     pass_flops = 4 * tok_dev * clusters * dim
     sums, unit_cents = call(
@@ -333,20 +342,20 @@
     arrived = lax.optimization_barrier((value_cache, *keys[1:]))
     later_values = arrived[0]
     values = [pick(value_cache, head)]
-    values += [over(pick(later_values, head ^ s), s * spread) for s in range(1, heads)]
+    values += [over(pick(later_values, head ^ s), head_masks[s]) for s in range(1, heads)]
 
     for level in range(levels - 1):
-        total = keep + over(send, 1 << level).astype(F32)
+        total = keep + over(send, rank_masks[level]).astype(F32)
         if level < levels - 2:
             cut = total.shape[0] // 2
             keep, send = total[:cut], total[cut:].astype(BF16)
     rounded = total.astype(BF16)
-    recv = over(rounded, 1 << (levels - 1))
+    recv = over(rounded, rank_masks[levels - 1])
     cut = rounded.shape[0] // 2
     recv = jnp.concatenate([recv[cut:], recv[:cut]])
     own_cents = to_unit(rounded.astype(F32) + recv.astype(F32)).astype(BF16)
     for level in range(levels - 2, 0, -1):
-        own_cents = jnp.concatenate([own_cents, over(own_cents, 1 << level)])
+        own_cents = jnp.concatenate([own_cents, over(own_cents, rank_masks[level])])
     other_cents = over(own_cents, 1)
 
     keep, keep_mass, send = call(
@@ -367,16 +376,17 @@
 
     own_queries = pick(queries, head, 1).reshape(rows, dim)
     own_chosen = pick(chosen_clusters, head, 1)
-    places = jnp.stack([head ^ s for s in range(heads)])[:, None] * spread + rank
+    places = jnp.stack([index ^ mask for mask in head_masks])[:, None]
     block_ids = (places * blk_dev + jnp.arange(blk_dev, dtype=jnp.int32)).reshape(-1)
-    held = pick(pick(block_clusters, head).reshape(heads, spread, blk_dev), rank, 1)
-    held = jnp.stack([pick(held, head ^ s) for s in range(heads)]).reshape(-1)
+    held = pick(block_clusters, head).reshape(devices, blk_dev)
+    held = jnp.stack([pick(held, index ^ mask) for mask in head_masks]).reshape(-1)
     picked = jnp.any(own_chosen[:, :, None] == held, axis=1)
     limits = jnp.where(
         picked, jnp.clip(request_positions[:, None] - block_ids * BLOCK, 0, BLOCK), 0
     )
     limits = jnp.repeat(limits, group, axis=0)
-    owners = jnp.arange(heads, dtype=jnp.int32)[:, None] * spread + rank
+    owners = jnp.arange(heads, dtype=jnp.int32)[:, None] ^ (far % 2) * (heads // 2)
+    owners = (far * heads + owners) * 2 + index % 2
     owned_ids = (owners * per_owner + jnp.arange(per_owner, dtype=jnp.int32)).reshape(-1)
     usable = jnp.all(own_chosen[:, :, None] != owned_ids, axis=1).astype(F32)
     usable = jnp.repeat(usable, group, axis=0)
@@ -390,7 +400,7 @@
     )
 
     for level in range(levels - 1):
-        recv = over(send, 1 << level)
+        recv = over(send, rank_masks[level])
         count = keep.shape[0] // 2
         keep, keep_mass, send = call(
             halve_kernel,
@@ -401,7 +411,7 @@
             ],
             [keep, keep_mass, recv],
         )
-    recv = over(send, 1 << (levels - 1))
+    recv = over(send, rank_masks[levels - 1])
     state, centroids = call(
         summary_kernel,
         [shape((rows, 2 * dim), F32), shape((owned, dim), F32)],
@@ -410,26 +420,26 @@
         4 * rows * owned * dim,
     )
     for level in range(levels - 1):
-        flip = ((index >> level) & 1).reshape(1)
+        flip = ((rank >> level) & 1).reshape(1)
         (state,) = call(
             merge_kernel,
             [shape((rows, 2 * dim), F32)],
-            [flip, state, over(state, 1 << level)],
+            [flip, state, over(state, rank_masks[level])],
             scalars=1,
         )
-    scalars = jnp.stack([(index >> (levels - 1)) & 1, head])
+    scalars = jnp.stack([(rank >> (levels - 1)) & 1, head])
     packs = call(
         last_merge_kernel,
         [shape((per_owner + rows, dim), F32)] * heads,
         [
             scalars,
             state,
-            over(state, 1 << (levels - 1)),
+            over(state, rank_masks[levels - 1]),
             centroids.reshape(heads, per_owner, dim),
         ],
         scalars=1,
     )
-    packs = [packs[0]] + [over(packs[s], s * spread) for s in range(1, heads)]
+    packs = [packs[0]] + [over(packs[s], head_masks[s]) for s in range(1, heads)]
     return call(
         spread_kernel,
         [shape((heads, per_owner, dim), F32), shape(queries.shape, BF16)],

time: 66.4 us -> 61.1 us (0.920)
  waiting for transfers between devices: 32.8 us -> 25 us
  starting transfers between devices: 17.7 us -> 19.9 us
    ppermute x16, waiting for transfers between devices: 32.8 us -> 25 us  [over(): return lax.ppermute(array, 'ctx', [(i, i ^ bit) for i in range(devices)])]
    ppermute x16, starting transfers between devices: 17.7 us -> 19.9 us  [over(): return lax.ppermute(array, 'ctx', [(i, i ^ bit) for i in range(devices)])]
    dynamic_slice x4 -> x5, local copies, waits for them, and re-layouts: 1.47 us -> 1.48 us  [pick(): return lax.dynamic_index_in_dim(array, at, axis, keepdims=False)]
  transfers between devices with their start and end apart: 16 -> 16, of which waited for: 9 -> 14; matrix products, arithmetic and copies ran while one was open for 6% -> 6% of each run, Pallas kernels for 3% -> 3%
where the time goes in v2:
time: 61.1 us; the launch traced here: 60.8 us
  waiting for transfers between devices  25 us (41%)
  starting transfers between devices  19.9 us (33%)
  Pallas kernels  9.76 us (16%)
  local copies, waits for them, and re-layouts  3.87 us (6%)
  other arithmetic  1.21 us (2%)
  between operations  0.96 us (2%)
    ppermute x16, waiting for transfers between devices, over(): return lax.ppermute(array, 'ctx', [(i, i ^ bit) for i in range(devices)])  25 us
    ppermute x16, starting transfers between devices, over(): return lax.ppermute(array, 'ctx', [(i, i ^ bit) for i in range(devices)])  19.9 us
    pallas_call x9, Pallas kernels, call(): pl.pallas_call(kernel, out_shape=tuple(outs), in_specs=in_specs, out_spec...  9.76 us
    dynamic_slice x5, local copies, waits for them, and re-layouts, pick(): return lax.dynamic_index_in_dim(array, at, axis, keepdims=False)  1.48 us
    squeeze x3, local copies, waits for them, and re-layouts, pick(): return lax.dynamic_index_in_dim(array, at, axis, keepdims=False)  1.25 us
  transfers between devices with their start and end apart: 16, of which 14 were waited for; matrix products, arithmetic and copies ran while one was open for 6% of the time, Pallas kernels for 3%

profile of v2, /device:TPU:0, one launch (start us, length us, event | category | flops | bytes accessed | tf_op | source)
XLA Modules:
  0.0 60.8 jit_solution(10441391372722274722)
XLA Ops:
  0.7 1.2 %dynamic-slice_bitcast_fusion.4 = (bf16[512,128]{1,0:T(8,128)(2,1)S(1)}, bf16[512,128]{1,0:T(8,128)(2,1)S(1)}, bf16[512,128]{1,0:T(8,128)(2,1)S(1)}, bf16[512,128]{1,0:T(8,128)(2,1)S(1)}) fusion(bf16[4,512,128]{2,1,0:T(8,128)(2,1)} %param.7, s32[]{:T(128)S(6)} %select_n.89, s32[]{:T(128)S(6)} %select_n.87, s32[]{:T(128)S(6)} %select_n.86, s32[]{:T(128)S(6)} %select_n.88), kind=kLoop, calls=%fused_computation.14 | loop fusion | bytes 1048592 | tf_op jit(solution)/shard_map/jit(dynamic_index_in_dim)/squeeze | solution.py:311
  1.9 3.0 %collective-permute-start = (bf16[512,128]{1,0:T(8,128)(2,1)S(1)}, bf16[512,128]{1,0:T(8,128)(2,1)S(1)}, u32[]{:S(2)}, u32[]{:S(2)}) collective-permute-start(bf16[512,128]{1,0:T(8,128)(2,1)S(1)} %get-tuple-element.40), channel_id=1, source_target_pairs={{0,2},{1,3},{2,0},{3,1},{4,6},{5,7},{6,4},{7,5},{8,10},{9,11},{10,... | collective-permute-start | bytes 393224 | tf_op jit(solution)/shard_map/ppermute | solution.py:308
  5.0 1.6 %collective-permute-start.1 = (bf16[512,128]{1,0:T(8,128)(2,1)S(1)}, bf16[512,128]{1,0:T(8,128)(2,1)S(1)}, u32[]{:S(2)}, u32[]{:S(2)}) collective-permute-start(bf16[512,128]{1,0:T(8,128)(2,1)S(1)} %get-tuple-element.42), channel_id=1, source_target_pairs={{0,4},{1,5},{2,6},{3,7},{4,0},{5,1},{6,2},{7,3},{8,12},{9,13},{10,... | collective-permute-start | bytes 393224 | tf_op jit(solution)/shard_map/ppermute | solution.py:308
  8.7 1.1 %shard_map.86 = (f32[1024,128]{1,0:T(8,128)S(1)}, bf16[1024,128]{1,0:T(8,128)(2,1)S(1)}) custom-call(bf16[512,128]{1,0:T(8,128)(2,1)S(1)} %get-tuple-element.41.key_ref.refs_0_, bf16[1024,128]{1,0:T(8,128)(2,1)S(1)} %bitcast.42), custom_call_target="tpu_custom_call" | custom-call | flops 268435456 | bytes 1179648 | tf_op jit(solution)/shard_map/pallas_call | solution.py:38
  10.1 1.3 %collective-permute-done.1.refs_1_.refs_2_ = bf16[512,128]{1,0:T(8,128)(2,1)S(1)} collective-permute-done((bf16[512,128]{1,0:T(8,128)(2,1)S(1)}, bf16[512,128]{1,0:T(8,128)(2,1)S(1)}, u32[]{:S(2)}, u32[]{:S(2)}) %collective-permute-start.1) | collective-permute-done | bytes 131104 | tf_op jit(solution)/shard_map/ppermute | solution.py:308
  11.3 1.2 %collective-permute-done.2.refs_2_.refs_3_ = bf16[512,128]{1,0:T(8,128)(2,1)S(1)} collective-permute-done((bf16[512,128]{1,0:T(8,128)(2,1)S(1)}, bf16[512,128]{1,0:T(8,128)(2,1)S(1)}, u32[]{:S(2)}, u32[]{:S(2)}) %collective-permute-start.2) | collective-permute-done | bytes 131104 | tf_op jit(solution)/shard_map/ppermute | solution.py:308
  12.5 2.4 %shard_map.87 = (f32[512,128]{1,0:T(8,128)S(1)}, bf16[512,128]{1,0:T(8,128)(2,1)S(1)}) custom-call(bf16[512,128]{1,0:T(8,128)(2,1)S(1)} %collective-permute-done.refs_0_.refs_1_, bf16[512,128]{1,0:T(8,128)(2,1)S(1)} %collective-permute-done.1.refs_1_.refs_2_, bf16[512,128]{1,0:T(8,128)(2,1)S(1)} %collective-permute-done.2.refs_2_.refs_3_, ...), custom_call_target="tpu_custom_call" | custom-call | flops 805306368 | bytes 1572864 | tf_op jit(solution)/shard_map/pallas_call | solution.py:38
  15.1 1.2 %collective-permute-done.6 = bf16[512,128]{1,0:T(8,128)(2,1)S(1)} collective-permute-done((bf16[512,128]{1,0:T(8,128)(2,1)S(1)}, bf16[512,128]{1,0:T(8,128)(2,1)S(1)}, u32[]{:S(2)}, u32[]{:S(2)}) %collective-permute-start.6) | collective-permute-done | bytes 131104 | tf_op jit(solution)/shard_map/ppermute | solution.py:308
  16.4 3.8 %collective-permute-start.7 = (bf16[512,128]{1,0:T(8,128)(2,1)S(1)}, bf16[512,128]{1,0:T(8,128)(2,1)S(1)}, u32[]{:S(2)}, u32[]{:S(2)}) collective-permute-start(bf16[512,128]{1,0:T(8,128)(2,1)S(1)} %add_convert_fusion), channel_id=1, source_target_pairs={{0,12},{1,13},{2,14},{3,15},{4,8},{5,9},{6,10},{7,11},{8,4},{9,5},... | collective-permute-start | bytes 393224 | tf_op jit(solution)/shard_map/ppermute | solution.py:308
  20.3 1.6 %collective-permute-start.3 = (bf16[512,128]{1,0:T(8,128)(2,1)S(1)}, bf16[512,128]{1,0:T(8,128)(2,1)S(1)}, u32[]{:S(2)}, u32[]{:S(2)}) collective-permute-start(bf16[512,128]{1,0:T(8,128)(2,1)S(1)} %get-tuple-element.38), channel_id=1, source_target_pairs={{0,2},{1,3},{2,0},{3,1},{4,6},{5,7},{6,4},{7,5},{8,10},{9,11},{10,... | collective-permute-start | bytes 393224 | tf_op jit(solution)/shard_map/ppermute | solution.py:308
  21.8 2.0 %collective-permute-start.5 = (bf16[512,128]{1,0:T(8,128)(2,1)S(1)}, bf16[512,128]{1,0:T(8,128)(2,1)S(1)}, u32[]{:S(2)}, u32[]{:S(2)}) collective-permute-start(bf16[512,128]{1,0:T(8,128)(2,1)S(1)} %get-tuple-element.36), channel_id=1, source_target_pairs={{0,6},{1,7},{2,4},{3,5},{4,2},{5,3},{6,0},{7,1},{8,14},{9,15},{10,... | collective-permute-start | bytes 393224 | tf_op jit(solution)/shard_map/ppermute | solution.py:308
  23.8 0.8 %collective-permute-done.7 = bf16[512,128]{1,0:T(8,128)(2,1)S(1)} collective-permute-done((bf16[512,128]{1,0:T(8,128)(2,1)S(1)}, bf16[512,128]{1,0:T(8,128)(2,1)S(1)}, u32[]{:S(2)}, u32[]{:S(2)}) %collective-permute-start.7) | collective-permute-done | bytes 131104 | tf_op jit(solution)/shard_map/ppermute | solution.py:308
  25.6 2.7 %collective-permute-done.4.refs_6_ = bf16[512,128]{1,0:T(8,128)(2,1)S(1)} collective-permute-done((bf16[512,128]{1,0:T(8,128)(2,1)S(1)}, bf16[512,128]{1,0:T(8,128)(2,1)S(1)}, u32[]{:S(2)}, u32[]{:S(2)}) %collective-permute-start.4) | collective-permute-done | bytes 131104 | tf_op jit(solution)/shard_map/ppermute | solution.py:308
  28.3 2.4 %collective-permute-done.5.refs_7_ = bf16[512,128]{1,0:T(8,128)(2,1)S(1)} collective-permute-done((bf16[512,128]{1,0:T(8,128)(2,1)S(1)}, bf16[512,128]{1,0:T(8,128)(2,1)S(1)}, u32[]{:S(2)}, u32[]{:S(2)}) %collective-permute-start.5) | collective-permute-done | bytes 131104 | tf_op jit(solution)/shard_map/ppermute | solution.py:308
  30.7 3.4 %shard_map.88 = (f32[512,256]{1,0:T(8,128)S(1)}, f32[8,512]{1,0:T(8,128)S(1)}, bf16[528,256]{1,0:T(8,128)(2,1)S(1)}) custom-call(bf16[512,128]{1,0:T(8,128)(2,1)S(1)} %get-tuple-element.41.key_ref.refs_0_, bf16[512,128]{1,0:T(8,128)(2,1)S(1)} %collective-permute-done.refs_0_.refs_1_, bf16[512,128]{1,0:T(8,128)(2,1)S(1)} %collective-permute-done.1.refs_1_.refs_2_, ...), custom_call_target="tpu_custom_call" | custom-call | flops 1610612736 | bytes 2121728 | tf_op jit(solution)/shard_map/pallas_call | solution.py:38
  34.3 1.4 %collective-permute-done.9.recv_ref = bf16[528,256]{1,0:T(8,128)(2,1)S(1)} collective-permute-done((bf16[528,256]{1,0:T(8,128)(2,1)S(1)}, bf16[528,256]{1,0:T(8,128)(2,1)S(1)}, u32[]{:S(2)}, u32[]{:S(2)}) %collective-permute-start.9) | collective-permute-done | bytes 270368 | tf_op jit(solution)/shard_map/ppermute | solution.py:308
  35.8 2.1 %collective-permute-start.10 = (bf16[272,256]{1,0:T(8,128)(2,1)S(1)}, bf16[272,256]{1,0:T(8,128)(2,1)S(1)}, u32[]{:S(2)}, u32[]{:S(2)}) collective-permute-start(bf16[272,256]{1,0:T(8,128)(2,1)S(1)} %get-tuple-element.29), channel_id=1, source_target_pairs={{0,12},{1,13},{2,14},{3,15},{4,8},{5,9},{6,10},{7,11},{8,4},{9,5},... | collective-permute-start | bytes 417800 | tf_op jit(solution)/shard_map/ppermute | solution.py:308
  39.3 4.2 %collective-permute-done.10.recv_ref = bf16[272,256]{1,0:T(8,128)(2,1)S(1)} collective-permute-done((bf16[272,256]{1,0:T(8,128)(2,1)S(1)}, bf16[272,256]{1,0:T(8,128)(2,1)S(1)}, u32[]{:S(2)}, u32[]{:S(2)}) %collective-permute-start.10) | collective-permute-done | bytes 139296 | tf_op jit(solution)/shard_map/ppermute | solution.py:308
  44.1 1.2 %collective-permute-done.11.recv_ref = f32[64,256]{1,0:T(8,128)S(1)} collective-permute-done((f32[64,256]{1,0:T(8,128)S(1)}, f32[64,256]{1,0:T(8,128)S(1)}, u32[]{:S(2)}, u32[]{:S(2)}) %collective-permute-start.11) | collective-permute-done | bytes 65568 | tf_op jit(solution)/shard_map/ppermute | solution.py:308
  45.5 2.1 %collective-permute-start.12 = (f32[64,256]{1,0:T(8,128)S(1)}, f32[64,256]{1,0:T(8,128)S(1)}, u32[]{:S(2)}, u32[]{:S(2)}) collective-permute-start(f32[64,256]{1,0:T(8,128)S(1)} %shard_map.92.own_ref), channel_id=1, source_target_pairs={{0,12},{1,13},{2,14},{3,15},{4,8},{5,9},{6,10},{7,11},{8,4},{9,5},... | collective-permute-start | bytes 196616 | tf_op jit(solution)/shard_map/ppermute | solution.py:308
  47.6 4.0 %collective-permute-done.12.recv_ref = f32[64,256]{1,0:T(8,128)S(1)} collective-permute-done((f32[64,256]{1,0:T(8,128)S(1)}, f32[64,256]{1,0:T(8,128)S(1)}, u32[]{:S(2)}, u32[]{:S(2)}) %collective-permute-start.12) | collective-permute-done | bytes 65568 | tf_op jit(solution)/shard_map/ppermute | solution.py:308
  53.1 1.8 %collective-permute-start.14 = (f32[128,128]{1,0:T(8,128)S(1)}, f32[128,128]{1,0:T(8,128)S(1)}, u32[]{:S(2)}, u32[]{:S(2)}) collective-permute-start(f32[128,128]{1,0:T(8,128)S(1)} %get-tuple-element.34), channel_id=1, source_target_pairs={{0,4},{1,5},{2,6},{3,7},{4,0},{5,1},{6,2},{7,3},{8,12},{9,13},{10,... | collective-permute-start | bytes 196616 | tf_op jit(solution)/shard_map/ppermute | solution.py:308
  54.9 1.0 %collective-permute-start.15 = (f32[128,128]{1,0:T(8,128)S(1)}, f32[128,128]{1,0:T(8,128)S(1)}, u32[]{:S(2)}, u32[]{:S(2)}) collective-permute-start(f32[128,128]{1,0:T(8,128)S(1)} %get-tuple-element.35), channel_id=1, source_target_pairs={{0,6},{1,7},{2,4},{3,5},{4,2},{5,3},{6,0},{7,1},{8,14},{9,15},{10,... | collective-permute-start | bytes 196616 | tf_op jit(solution)/shard_map/ppermute | solution.py:308
  57.4 2.7 %collective-permute-done.15.refs_3_ = f32[128,128]{1,0:T(8,128)S(1)} collective-permute-done((f32[128,128]{1,0:T(8,128)S(1)}, f32[128,128]{1,0:T(8,128)S(1)}, u32[]{:S(2)}, u32[]{:S(2)}) %collective-permute-start.15) | collective-permute-done | bytes 65568 | tf_op jit(solution)/shard_map/ppermute | solution.py:308
  (59 shorter events, 9.7 us)
Async XLA Ops:
  0.6 5.9 %copy-start = (bf16[4,1024,128]{2,1,0:T(8,128)(2,1)S(1)}, bf16[4,1024,128]{2,1,0:T(8,128)(2,1)}, u32[]{:S(2)}) copy-start(bf16[4,1024,128]{2,1,0:T(8,128)(2,1)} %param.9) | copy-start | bytes 3145732
  1.9 8.1 %collective-permute-start = (bf16[512,128]{1,0:T(8,128)(2,1)S(1)}, bf16[512,128]{1,0:T(8,128)(2,1)S(1)}, u32[]{:S(2)}, u32[]{:S(2)}) collective-permute-start(bf16[512,128]{1,0:T(8,128)(2,1)S(1)} %get-tuple-element.40), channel_id=1, source_target_pairs={{0,2},{1,3},{2,0},{3,1},{4,6},{5,7},{6,4},{7,5},{8,10},{9,11},{10,... | collective-permute-start | bytes 393224 | tf_op jit(solution)/shard_map/ppermute | solution.py:308
  5.0 6.4 %collective-permute-start.1 = (bf16[512,128]{1,0:T(8,128)(2,1)S(1)}, bf16[512,128]{1,0:T(8,128)(2,1)S(1)}, u32[]{:S(2)}, u32[]{:S(2)}) collective-permute-start(bf16[512,128]{1,0:T(8,128)(2,1)S(1)} %get-tuple-element.42), channel_id=1, source_target_pairs={{0,4},{1,5},{2,6},{3,7},{4,0},{5,1},{6,2},{7,3},{8,12},{9,13},{10,... | collective-permute-start | bytes 393224 | tf_op jit(solution)/shard_map/ppermute | solution.py:308
  6.5 6.0 %collective-permute-start.2 = (bf16[512,128]{1,0:T(8,128)(2,1)S(1)}, bf16[512,128]{1,0:T(8,128)(2,1)S(1)}, u32[]{:S(2)}, u32[]{:S(2)}) collective-permute-start(bf16[512,128]{1,0:T(8,128)(2,1)S(1)} %get-tuple-element.39), channel_id=1, source_target_pairs={{0,6},{1,7},{2,4},{3,5},{4,2},{5,3},{6,0},{7,1},{8,14},{9,15},{10,... | collective-permute-start | bytes 393224 | tf_op jit(solution)/shard_map/ppermute | solution.py:308
  12.5 2.5 %copy-start.2 = (s32[8]{0:T(128)S(1)}, s32[8]{0:T(128)}, u32[]{:S(2)}) copy-start(s32[8]{0:T(128)} %param.12) | copy-start | bytes 100
  14.9 5.3 %copy-start.1 = (bf16[4,512,128]{2,1,0:T(8,128)(2,1)S(1)}, bf16[4,512,128]{2,1,0:T(8,128)(2,1)}, u32[]{:S(2)}) copy-start(bf16[4,512,128]{2,1,0:T(8,128)(2,1)} %param.8) | copy-start | bytes 1572868
  14.9 1.4 %collective-permute-start.6 = (bf16[512,128]{1,0:T(8,128)(2,1)S(1)}, bf16[512,128]{1,0:T(8,128)(2,1)S(1)}, u32[]{:S(2)}, u32[]{:S(2)}) collective-permute-start(bf16[512,128]{1,0:T(8,128)(2,1)S(1)} %get-tuple-element.23), channel_id=1, source_target_pairs={{0,1},{1,0},{2,3},{3,2},{4,5},{5,4},{6,7},{7,6},{8,9},{9,8},{10,11... | collective-permute-start | bytes 393224 | tf_op jit(solution)/shard_map/ppermute | solution.py:308
  16.4 8.2 %collective-permute-start.7 = (bf16[512,128]{1,0:T(8,128)(2,1)S(1)}, bf16[512,128]{1,0:T(8,128)(2,1)S(1)}, u32[]{:S(2)}, u32[]{:S(2)}) collective-permute-start(bf16[512,128]{1,0:T(8,128)(2,1)S(1)} %add_convert_fusion), channel_id=1, source_target_pairs={{0,12},{1,13},{2,14},{3,15},{4,8},{5,9},{6,10},{7,11},{8,4},{9,5},... | collective-permute-start | bytes 393224 | tf_op jit(solution)/shard_map/ppermute | solution.py:308
  20.3 5.3 %collective-permute-start.3 = (bf16[512,128]{1,0:T(8,128)(2,1)S(1)}, bf16[512,128]{1,0:T(8,128)(2,1)S(1)}, u32[]{:S(2)}, u32[]{:S(2)}) collective-permute-start(bf16[512,128]{1,0:T(8,128)(2,1)S(1)} %get-tuple-element.38), channel_id=1, source_target_pairs={{0,2},{1,3},{2,0},{3,1},{4,6},{5,7},{6,4},{7,5},{8,10},{9,11},{10,... | collective-permute-start | bytes 393224 | tf_op jit(solution)/shard_map/ppermute | solution.py:308
  21.8 6.4 %collective-permute-start.4 = (bf16[512,128]{1,0:T(8,128)(2,1)S(1)}, bf16[512,128]{1,0:T(8,128)(2,1)S(1)}, u32[]{:S(2)}, u32[]{:S(2)}) collective-permute-start(bf16[512,128]{1,0:T(8,128)(2,1)S(1)} %get-tuple-element.37), channel_id=1, source_target_pairs={{0,4},{1,5},{2,6},{3,7},{4,0},{5,1},{6,2},{7,3},{8,12},{9,13},{10,... | collective-permute-start | bytes 393224 | tf_op jit(solution)/shard_map/ppermute | solution.py:308
  21.8 8.9 %collective-permute-start.5 = (bf16[512,128]{1,0:T(8,128)(2,1)S(1)}, bf16[512,128]{1,0:T(8,128)(2,1)S(1)}, u32[]{:S(2)}, u32[]{:S(2)}) collective-permute-start(bf16[512,128]{1,0:T(8,128)(2,1)S(1)} %get-tuple-element.36), channel_id=1, source_target_pairs={{0,6},{1,7},{2,4},{3,5},{4,2},{5,3},{6,0},{7,1},{8,14},{9,15},{10,... | collective-permute-start | bytes 393224 | tf_op jit(solution)/shard_map/ppermute | solution.py:308
  24.9 5.8 %collective-permute-start.8 = (bf16[512,128]{1,0:T(8,128)(2,1)S(1)}, bf16[512,128]{1,0:T(8,128)(2,1)S(1)}, u32[]{:S(2)}, u32[]{:S(2)}) collective-permute-start(bf16[512,128]{1,0:T(8,128)(2,1)S(1)} %multiply_convert_fusion.refs_8_), channel_id=1, source_target_pairs={{0,1},{1,0},{2,3},{3,2},{4,5},{5,4},{6,7},{7,6},{8,9},{9,8},{10,11... | collective-permute-start | bytes 393224 | tf_op jit(solution)/shard_map/ppermute | solution.py:308
  34.1 1.6 %collective-permute-start.9 = (bf16[528,256]{1,0:T(8,128)(2,1)S(1)}, bf16[528,256]{1,0:T(8,128)(2,1)S(1)}, u32[]{:S(2)}, u32[]{:S(2)}) collective-permute-start(bf16[528,256]{1,0:T(8,128)(2,1)S(1)} %get-tuple-element.26), channel_id=1, source_target_pairs={{0,1},{1,0},{2,3},{3,2},{4,5},{5,4},{6,7},{7,6},{8,9},{9,8},{10,11... | collective-permute-start | bytes 811016 | tf_op jit(solution)/shard_map/ppermute | solution.py:308
  35.8 7.7 %collective-permute-start.10 = (bf16[272,256]{1,0:T(8,128)(2,1)S(1)}, bf16[272,256]{1,0:T(8,128)(2,1)S(1)}, u32[]{:S(2)}, u32[]{:S(2)}) collective-permute-start(bf16[272,256]{1,0:T(8,128)(2,1)S(1)} %get-tuple-element.29), channel_id=1, source_target_pairs={{0,12},{1,13},{2,14},{3,15},{4,8},{5,9},{6,10},{7,11},{8,4},{9,5},... | collective-permute-start | bytes 417800 | tf_op jit(solution)/shard_map/ppermute | solution.py:308
  44.0 1.3 %collective-permute-start.11 = (f32[64,256]{1,0:T(8,128)S(1)}, f32[64,256]{1,0:T(8,128)S(1)}, u32[]{:S(2)}, u32[]{:S(2)}) collective-permute-start(f32[64,256]{1,0:T(8,128)S(1)} %get-tuple-element.30.own_ref), channel_id=1, source_target_pairs={{0,1},{1,0},{2,3},{3,2},{4,5},{5,4},{6,7},{7,6},{8,9},{9,8},{10,11... | collective-permute-start | bytes 196616 | tf_op jit(solution)/shard_map/ppermute | solution.py:308
  45.5 6.2 %collective-permute-start.12 = (f32[64,256]{1,0:T(8,128)S(1)}, f32[64,256]{1,0:T(8,128)S(1)}, u32[]{:S(2)}, u32[]{:S(2)}) collective-permute-start(f32[64,256]{1,0:T(8,128)S(1)} %shard_map.92.own_ref), channel_id=1, source_target_pairs={{0,12},{1,13},{2,14},{3,15},{4,8},{5,9},{6,10},{7,11},{8,4},{9,5},... | collective-permute-start | bytes 196616 | tf_op jit(solution)/shard_map/ppermute | solution.py:308
  52.4 4.3 %collective-permute-start.13 = (f32[128,128]{1,0:T(8,128)S(1)}, f32[128,128]{1,0:T(8,128)S(1)}, u32[]{:S(2)}, u32[]{:S(2)}) collective-permute-start(f32[128,128]{1,0:T(8,128)S(1)} %get-tuple-element.33), channel_id=1, source_target_pairs={{0,2},{1,3},{2,0},{3,1},{4,6},{5,7},{6,4},{7,5},{8,10},{9,11},{10,... | collective-permute-start | bytes 196616 | tf_op jit(solution)/shard_map/ppermute | solution.py:308
  53.1 4.3 %collective-permute-start.14 = (f32[128,128]{1,0:T(8,128)S(1)}, f32[128,128]{1,0:T(8,128)S(1)}, u32[]{:S(2)}, u32[]{:S(2)}) collective-permute-start(f32[128,128]{1,0:T(8,128)S(1)} %get-tuple-element.34), channel_id=1, source_target_pairs={{0,4},{1,5},{2,6},{3,7},{4,0},{5,1},{6,2},{7,3},{8,12},{9,13},{10,... | collective-permute-start | bytes 196616 | tf_op jit(solution)/shard_map/ppermute | solution.py:308
  54.9 5.2 %collective-permute-start.15 = (f32[128,128]{1,0:T(8,128)S(1)}, f32[128,128]{1,0:T(8,128)S(1)}, u32[]{:S(2)}, u32[]{:S(2)}) collective-permute-start(f32[128,128]{1,0:T(8,128)S(1)} %get-tuple-element.35), channel_id=1, source_target_pairs={{0,6},{1,7},{2,4},{3,5},{4,2},{5,3},{6,0},{7,1},{8,14},{9,15},{10,... | collective-permute-start | bytes 196616 | tf_op jit(solution)/shard_map/ppermute | solution.py:308

commit v3 on v2

--- a/solution.py
+++ b/solution.py
@@ -29,6 +29,32 @@
 
 def dot_nt(left, right):
     return lax.dot_general(left, right, (((1,), (1,)), ((), ())), preferred_element_type=F32)
+
+
+def spanned(basis, number):
+    return functools.reduce(lambda a, b: a ^ b, [m for j, m in enumerate(basis) if number >> j & 1], 0)
+
+
+def duals(head_basis, rank_basis, devices):
+    basis = [*head_basis, *rank_basis]
+    found = [
+        next(
+            f
+            for f in range(devices)
+            if all((f & m).bit_count() % 2 == (j == k) for j, m in enumerate(basis))
+        )
+        for k in range(len(basis))
+    ]
+    return found[: len(head_basis)], found[len(head_basis) :]
+
+
+def coordinates(number, masks):
+    result = 0
+    for place, mask in enumerate(masks):
+        for bit in range(mask.bit_length()):
+            if mask >> bit & 1:
+                result = result ^ ((number >> bit & 1) << place)
+    return result
 
 
 def call(kernel, outs, args, scratch=(), flops=0, scalars=0):
@@ -78,8 +104,13 @@
                 mass_ref[row : row + tile, :] += part
 
 
-def first_kernel(key_ref, cent_ref, sums_ref, unit_ref, raised_ref, weight_ref):
-    unit_ref[...] = to_unit(cent_ref[...]).astype(BF16)
+def first_kernel(
+    order_ref, key_ref, cent_ref, sums_ref, unit_ref, cents_ref, raised_ref, weight_ref
+):
+    owners, per_owner, _ = cent_ref.shape
+    for at in range(owners):
+        cents_ref[at * per_owner : (at + 1) * per_owner, :] = cent_ref[order_ref[at]].astype(F32)
+    unit_ref[...] = to_unit(cents_ref[...]).astype(BF16)
     keys = key_ref[...]
     fill_weights(to_unit(keys).astype(BF16), (unit_ref,), raised_ref, weight_ref, 0, None)
     rows = sums_ref.shape[0]
@@ -293,13 +324,16 @@
     levels = spread.bit_length() - 1
     if heads * spread != devices or 1 << levels != spread or heads & (heads - 1) or levels < 2:
         raise ValueError("unsupported mesh")
-    bits = heads.bit_length() - 1
-    head_masks = [s << 1 for s in range(heads)]
-    rank_masks = [1] + [1 << (bits + level) for level in range(1, levels)]
-    rank_masks[1] |= heads
-    far = index // (2 * heads)
-    head = (index // 2) % heads ^ (far % 2) * (heads // 2)
-    rank = far * 2 + index % 2
+    bits = devices.bit_length() - 1
+    head_bits = heads.bit_length() - 1
+    head_basis = [2 << bit for bit in range(head_bits)]
+    rank_basis = [1] + [1 << bit for bit in range(head_bits + 1, bits)]
+    rank_basis[1] |= heads
+    head_masks = [spanned(head_basis, s) for s in range(heads)]
+    rank_masks = [spanned(rank_basis, s) for s in range(spread)]
+    head_duals, rank_duals = duals(head_basis, rank_basis, devices)
+    head, rank = coordinates(index, head_duals), coordinates(index, rank_duals)
+    base = coordinates(rank, [sum(1 << j for j in range(levels) if rank_basis[j] >> bit & 1) for bit in range(bits)])
     half = clusters // 2
     rows = requests * group
     owned = heads * per_owner
@@ -313,20 +347,22 @@
     keys = [pick(key_cache, head)]
     keys += [over(pick(key_cache, head ^ s), head_masks[s]) for s in range(1, heads)]
 
-    blocks = pick(init_centroids, head).reshape(spread // 4, 2, heads, 2, per_owner, dim)
-    blocks = jnp.stack([blocks[:, 0], jnp.roll(blocks[:, 1], heads // 2, axis=1)], axis=1)
-    by_rank = jnp.moveaxis(blocks.reshape(spread // 2, heads, 2, per_owner, dim), 2, 1)
-    by_rank = by_rank.reshape(spread, heads, per_owner, dim)
-    reverse = [int(format(r, f"0{levels}b")[::-1], 2) for r in range(spread)]
-    cents = jnp.stack([pick(by_rank, rank ^ r) for r in reverse]).reshape(clusters, dim)
+    blocks = pick(init_centroids, head).reshape(devices, per_owner, dim)
+    turned = [int(format(r, f"0{levels}b")[::-1], 2) for r in range(spread)]
+    order = jnp.stack([base ^ rank_masks[r] ^ mask for r in turned for mask in head_masks])
 
     pass_flops = 4 * tok_dev * clusters * dim
     sums, unit_cents = call(
         first_kernel,
         [shape((clusters, dim), F32), shape((clusters, dim), BF16)],
-        [keys[0], cents],
-        [pltpu.VMEM((clusters, tok_dev), F32), pltpu.VMEM((clusters, tok_dev), BF16)],
+        [order, keys[0], blocks],
+        [
+            pltpu.VMEM((clusters, dim), F32),
+            pltpu.VMEM((clusters, tok_dev), F32),
+            pltpu.VMEM((clusters, tok_dev), BF16),
+        ],
         pass_flops,
+        scalars=1,
     )
     keep, send = call(
         functools.partial(rest_kernel, heads - 1),
@@ -339,23 +375,21 @@
         pass_flops * (heads - 1),
     )
 
-    arrived = lax.optimization_barrier((value_cache, *keys[1:]))
-    later_values = arrived[0]
     values = [pick(value_cache, head)]
-    values += [over(pick(later_values, head ^ s), head_masks[s]) for s in range(1, heads)]
+    values += [over(pick(value_cache, head ^ s), head_masks[s]) for s in range(1, heads)]
 
     for level in range(levels - 1):
-        total = keep + over(send, rank_masks[level]).astype(F32)
+        total = keep + over(send, rank_basis[level]).astype(F32)
         if level < levels - 2:
             cut = total.shape[0] // 2
             keep, send = total[:cut], total[cut:].astype(BF16)
     rounded = total.astype(BF16)
-    recv = over(rounded, rank_masks[levels - 1])
+    recv = over(rounded, rank_basis[levels - 1])
     cut = rounded.shape[0] // 2
     recv = jnp.concatenate([recv[cut:], recv[:cut]])
     own_cents = to_unit(rounded.astype(F32) + recv.astype(F32)).astype(BF16)
     for level in range(levels - 2, 0, -1):
-        own_cents = jnp.concatenate([own_cents, over(own_cents, rank_masks[level])])
+        own_cents = jnp.concatenate([own_cents, over(own_cents, rank_basis[level])])
     other_cents = over(own_cents, 1)
 
     keep, keep_mass, send = call(
@@ -376,8 +410,8 @@
 
     own_queries = pick(queries, head, 1).reshape(rows, dim)
     own_chosen = pick(chosen_clusters, head, 1)
-    places = jnp.stack([index ^ mask for mask in head_masks])[:, None]
-    block_ids = (places * blk_dev + jnp.arange(blk_dev, dtype=jnp.int32)).reshape(-1)
+    held_by = jnp.stack([index ^ mask for mask in head_masks])
+    block_ids = (held_by[:, None] * blk_dev + jnp.arange(blk_dev, dtype=jnp.int32)).reshape(-1)
     held = pick(block_clusters, head).reshape(devices, blk_dev)
     held = jnp.stack([pick(held, index ^ mask) for mask in head_masks]).reshape(-1)
     picked = jnp.any(own_chosen[:, :, None] == held, axis=1)
@@ -385,8 +419,7 @@
         picked, jnp.clip(request_positions[:, None] - block_ids * BLOCK, 0, BLOCK), 0
     )
     limits = jnp.repeat(limits, group, axis=0)
-    owners = jnp.arange(heads, dtype=jnp.int32)[:, None] ^ (far % 2) * (heads // 2)
-    owners = (far * heads + owners) * 2 + index % 2
+    owners = (base ^ jnp.array(head_masks, jnp.int32))[:, None]
     owned_ids = (owners * per_owner + jnp.arange(per_owner, dtype=jnp.int32)).reshape(-1)
     usable = jnp.all(own_chosen[:, :, None] != owned_ids, axis=1).astype(F32)
     usable = jnp.repeat(usable, group, axis=0)
@@ -400,7 +433,7 @@
     )
 
     for level in range(levels - 1):
-        recv = over(send, rank_masks[level])
+        recv = over(send, rank_basis[level])
         count = keep.shape[0] // 2
         keep, keep_mass, send = call(
             halve_kernel,
@@ -411,7 +444,7 @@
             ],
             [keep, keep_mass, recv],
         )
-    recv = over(send, rank_masks[levels - 1])
+    recv = over(send, rank_basis[levels - 1])
     state, centroids = call(
         summary_kernel,
         [shape((rows, 2 * dim), F32), shape((owned, dim), F32)],
@@ -424,7 +457,7 @@
         (state,) = call(
             merge_kernel,
             [shape((rows, 2 * dim), F32)],
-            [flip, state, over(state, rank_masks[level])],
+            [flip, state, over(state, rank_basis[level])],
             scalars=1,
         )
     scalars = jnp.stack([(rank >> (levels - 1)) & 1, head])
@@ -434,7 +467,7 @@
         [
             scalars,
             state,
-            over(state, rank_masks[levels - 1]),
+            over(state, rank_basis[levels - 1]),
             centroids.reshape(heads, per_owner, dim),
         ],
         scalars=1,

time: 61.1 us -> 58.7 us (0.961)
  waiting for transfers between devices: 25 us -> 18.5 us
  starting transfers between devices: 19.9 us -> 23.2 us
    ppermute x16, waiting for transfers between devices: 25 us -> 18.5 us  [over(): return lax.ppermute(array, 'ctx', [(i, i ^ bit) for i in range(devices)])]
    ppermute x16, starting transfers between devices: 19.9 us -> 23.2 us  [over(): return lax.ppermute(array, 'ctx', [(i, i ^ bit) for i in range(devices)])]
    squeeze x3 -> x2, local copies, waits for them, and re-layouts: 1.25 us -> 1.28 us  [pick(): return lax.dynamic_index_in_dim(array, at, axis, keepdims=False)]
    dynamic_slice x5 -> x4, local copies, waits for them, and re-layouts: 1.48 us -> 1.47 us  [pick(): return lax.dynamic_index_in_dim(array, at, axis, keepdims=False)]
  transfers between devices with their start and end apart: 16 -> 16, of which waited for: 14 -> 11; matrix products, arithmetic and copies ran while one was open for 6% -> 7% of each run, Pallas kernels for 3% -> 8%
where the time goes in v3:
time: 58.7 us; the launch traced here: 58.4 us
  starting transfers between devices  23.2 us (40%)
  waiting for transfers between devices  18.5 us (32%)
  Pallas kernels  10.3 us (18%)
  local copies, waits for them, and re-layouts  4.37 us (7%)
  other arithmetic  1.12 us (2%)
  between operations  0.86 us (1%)
    ppermute x16, starting transfers between devices, over(): return lax.ppermute(array, 'ctx', [(i, i ^ bit) for i in range(devices)])  23.2 us
    ppermute x16, waiting for transfers between devices, over(): return lax.ppermute(array, 'ctx', [(i, i ^ bit) for i in range(devices)])  18.5 us
    pallas_call x9, Pallas kernels, call(): pl.pallas_call(kernel, out_shape=tuple(outs), in_specs=in_specs, out_spec...  10.3 us
    dynamic_slice x4, local copies, waits for them, and re-layouts, pick(): return lax.dynamic_index_in_dim(array, at, axis, keepdims=False)  1.47 us
    squeeze x2, local copies, waits for them, and re-layouts, pick(): return lax.dynamic_index_in_dim(array, at, axis, keepdims=False)  1.28 us
  transfers between devices with their start and end apart: 16, of which 11 were waited for; matrix products, arithmetic and copies ran while one was open for 7% of the time, Pallas kernels for 8%

profile of v3, /device:TPU:0, one launch (start us, length us, event | category | flops | bytes accessed | tf_op | source)
XLA Modules:
  0.0 58.4 jit_solution(13236693600030456006)
XLA Ops:
  0.7 1.2 %dynamic-slice_bitcast_fusion.4 = (bf16[512,128]{1,0:T(8,128)(2,1)S(1)}, bf16[512,128]{1,0:T(8,128)(2,1)S(1)}, bf16[512,128]{1,0:T(8,128)(2,1)S(1)}, bf16[512,128]{1,0:T(8,128)(2,1)S(1)}) fusion(bf16[4,512,128]{2,1,0:T(8,128)(2,1)} %param.8, s32[]{:T(128)S(6)} %select_n.45, s32[]{:T(128)S(6)} %select_n.43, s32[]{:T(128)S(6)} %select_n.42, s32[]{:T(128)S(6)} %select_n.44), kind=kLoop, calls=%fused_computation.10 | loop fusion | bytes 1048592 | tf_op jit(solution)/shard_map/jit(dynamic_index_in_dim)/squeeze | solution.py:345
  1.9 3.0 %collective-permute-start = (bf16[512,128]{1,0:T(8,128)(2,1)S(1)}, bf16[512,128]{1,0:T(8,128)(2,1)S(1)}, u32[]{:S(2)}, u32[]{:S(2)}) collective-permute-start(bf16[512,128]{1,0:T(8,128)(2,1)S(1)} %get-tuple-element.39), channel_id=1, source_target_pairs={{0,2},{1,3},{2,0},{3,1},{4,6},{5,7},{6,4},{7,5},{8,10},{9,11},{10,... | collective-permute-start | bytes 393224 | tf_op jit(solution)/shard_map/ppermute | solution.py:342
  5.0 1.6 %collective-permute-start.1 = (bf16[512,128]{1,0:T(8,128)(2,1)S(1)}, bf16[512,128]{1,0:T(8,128)(2,1)S(1)}, u32[]{:S(2)}, u32[]{:S(2)}) collective-permute-start(bf16[512,128]{1,0:T(8,128)(2,1)S(1)} %get-tuple-element.41), channel_id=1, source_target_pairs={{0,4},{1,5},{2,6},{3,7},{4,0},{5,1},{6,2},{7,3},{8,12},{9,13},{10,... | collective-permute-start | bytes 393224 | tf_op jit(solution)/shard_map/ppermute | solution.py:342
  6.6 2.0 %collective-permute-start.3 = (bf16[512,128]{1,0:T(8,128)(2,1)S(1)}, bf16[512,128]{1,0:T(8,128)(2,1)S(1)}, u32[]{:S(2)}, u32[]{:S(2)}) collective-permute-start(bf16[512,128]{1,0:T(8,128)(2,1)S(1)} %get-tuple-element.35), channel_id=1, source_target_pairs={{0,2},{1,3},{2,0},{3,1},{4,6},{5,7},{6,4},{7,5},{8,10},{9,11},{10,... | collective-permute-start | bytes 393224 | tf_op jit(solution)/shard_map/ppermute | solution.py:342
  8.6 1.6 %collective-permute-start.4 = (bf16[512,128]{1,0:T(8,128)(2,1)S(1)}, bf16[512,128]{1,0:T(8,128)(2,1)S(1)}, u32[]{:S(2)}, u32[]{:S(2)}) collective-permute-start(bf16[512,128]{1,0:T(8,128)(2,1)S(1)} %get-tuple-element.37), channel_id=1, source_target_pairs={{0,4},{1,5},{2,6},{3,7},{4,0},{5,1},{6,2},{7,3},{8,12},{9,13},{10,... | collective-permute-start | bytes 393224 | tf_op jit(solution)/shard_map/ppermute | solution.py:342
  11.2 1.6 %shard_map.95 = (f32[1024,128]{1,0:T(8,128)S(1)}, bf16[1024,128]{1,0:T(8,128)(2,1)S(1)}) custom-call(s32[16]{0:T(128)S(1)} %stack.98.order_ref, bf16[512,128]{1,0:T(8,128)(2,1)S(1)} %get-tuple-element.40.key_ref.refs_0_, bf16[16,64,128]{2,1,0:T(8,128)(2,1)S(1)} %bitcast.48), custom_call_target="tpu_custom_call" | custom-call | flops 268435456 | bytes 1179712 | tf_op jit(solution)/shard_map/pallas_call | solution.py:64
  13.0 0.9 %collective-permute-done.2.refs_2_.refs_3_ = bf16[512,128]{1,0:T(8,128)(2,1)S(1)} collective-permute-done((bf16[512,128]{1,0:T(8,128)(2,1)S(1)}, bf16[512,128]{1,0:T(8,128)(2,1)S(1)}, u32[]{:S(2)}, u32[]{:S(2)}) %collective-permute-start.2) | collective-permute-done | bytes 131104 | tf_op jit(solution)/shard_map/ppermute | solution.py:342
  13.9 2.4 %shard_map.96 = (f32[512,128]{1,0:T(8,128)S(1)}, bf16[512,128]{1,0:T(8,128)(2,1)S(1)}) custom-call(bf16[512,128]{1,0:T(8,128)(2,1)S(1)} %collective-permute-done.refs_0_.refs_1_, bf16[512,128]{1,0:T(8,128)(2,1)S(1)} %collective-permute-done.1.refs_1_.refs_2_, bf16[512,128]{1,0:T(8,128)(2,1)S(1)} %collective-permute-done.2.refs_2_.refs_3_, ...), custom_call_target="tpu_custom_call" | custom-call | flops 805306368 | bytes 1572864 | tf_op jit(solution)/shard_map/pallas_call | solution.py:64
  16.4 0.7 %constant_dynamic-slice_fusion.5 = s32[8,1,32]{2,1,0:T(1,128)S(1)} fusion(s32[8,4,32]{2,1,0:T(4,128)} %param.12, s32[]{:T(128)S(6)} %select_n.42), kind=kLoop, calls=%fused_computation.24 | loop fusion | bytes 2052 | tf_op jit(solution)/shard_map/jit(dynamic_index_in_dim)/dynamic_slice | solution.py:345
  17.8 3.9 %collective-permute-start.7 = (bf16[512,128]{1,0:T(8,128)(2,1)S(1)}, bf16[512,128]{1,0:T(8,128)(2,1)S(1)}, u32[]{:S(2)}, u32[]{:S(2)}) collective-permute-start(bf16[512,128]{1,0:T(8,128)(2,1)S(1)} %add_convert_fusion), channel_id=1, source_target_pairs={{0,12},{1,13},{2,14},{3,15},{4,8},{5,9},{6,10},{7,11},{8,4},{9,5},... | collective-permute-start | bytes 393224 | tf_op jit(solution)/shard_map/ppermute | solution.py:342
  22.2 3.4 %collective-permute-done.7 = bf16[512,128]{1,0:T(8,128)(2,1)S(1)} collective-permute-done((bf16[512,128]{1,0:T(8,128)(2,1)S(1)}, bf16[512,128]{1,0:T(8,128)(2,1)S(1)}, u32[]{:S(2)}, u32[]{:S(2)}) %collective-permute-start.7) | collective-permute-done | bytes 131104 | tf_op jit(solution)/shard_map/ppermute | solution.py:342
  26.5 0.8 %collective-permute-done.8.refs_9_ = bf16[512,128]{1,0:T(8,128)(2,1)S(1)} collective-permute-done((bf16[512,128]{1,0:T(8,128)(2,1)S(1)}, bf16[512,128]{1,0:T(8,128)(2,1)S(1)}, u32[]{:S(2)}, u32[]{:S(2)}) %collective-permute-start.8) | collective-permute-done | bytes 131104 | tf_op jit(solution)/shard_map/ppermute | solution.py:342
  27.3 3.4 %shard_map.97 = (f32[512,256]{1,0:T(8,128)S(1)}, f32[8,512]{1,0:T(8,128)S(1)}, bf16[528,256]{1,0:T(8,128)(2,1)S(1)}) custom-call(bf16[512,128]{1,0:T(8,128)(2,1)S(1)} %get-tuple-element.40.key_ref.refs_0_, bf16[512,128]{1,0:T(8,128)(2,1)S(1)} %collective-permute-done.refs_0_.refs_1_, bf16[512,128]{1,0:T(8,128)(2,1)S(1)} %collective-permute-done.1.refs_1_.refs_2_, ...), custom_call_target="tpu_custom_call" | custom-call | flops 1610612736 | bytes 2121728 | tf_op jit(solution)/shard_map/pallas_call | solution.py:64
  31.1 1.2 %collective-permute-done.9.recv_ref = bf16[528,256]{1,0:T(8,128)(2,1)S(1)} collective-permute-done((bf16[528,256]{1,0:T(8,128)(2,1)S(1)}, bf16[528,256]{1,0:T(8,128)(2,1)S(1)}, u32[]{:S(2)}, u32[]{:S(2)}) %collective-permute-start.9) | collective-permute-done | bytes 270368 | tf_op jit(solution)/shard_map/ppermute | solution.py:342
  32.4 3.6 %collective-permute-start.10 = (bf16[272,256]{1,0:T(8,128)(2,1)S(1)}, bf16[272,256]{1,0:T(8,128)(2,1)S(1)}, u32[]{:S(2)}, u32[]{:S(2)}) collective-permute-start(bf16[272,256]{1,0:T(8,128)(2,1)S(1)} %get-tuple-element.27), channel_id=1, source_target_pairs={{0,12},{1,13},{2,14},{3,15},{4,8},{5,9},{6,10},{7,11},{8,4},{9,5},... | collective-permute-start | bytes 417800 | tf_op jit(solution)/shard_map/ppermute | solution.py:342
  37.4 2.7 %collective-permute-done.10.recv_ref = bf16[272,256]{1,0:T(8,128)(2,1)S(1)} collective-permute-done((bf16[272,256]{1,0:T(8,128)(2,1)S(1)}, bf16[272,256]{1,0:T(8,128)(2,1)S(1)}, u32[]{:S(2)}, u32[]{:S(2)}) %collective-permute-start.10) | collective-permute-done | bytes 139296 | tf_op jit(solution)/shard_map/ppermute | solution.py:342
  40.7 1.2 %collective-permute-done.11.recv_ref = f32[64,256]{1,0:T(8,128)S(1)} collective-permute-done((f32[64,256]{1,0:T(8,128)S(1)}, f32[64,256]{1,0:T(8,128)S(1)}, u32[]{:S(2)}, u32[]{:S(2)}) %collective-permute-start.11) | collective-permute-done | bytes 65568 | tf_op jit(solution)/shard_map/ppermute | solution.py:342
  42.1 3.6 %collective-permute-start.12 = (f32[64,256]{1,0:T(8,128)S(1)}, f32[64,256]{1,0:T(8,128)S(1)}, u32[]{:S(2)}, u32[]{:S(2)}) collective-permute-start(f32[64,256]{1,0:T(8,128)S(1)} %shard_map.101.own_ref), channel_id=1, source_target_pairs={{0,12},{1,13},{2,14},{3,15},{4,8},{5,9},{6,10},{7,11},{8,4},{9,5},... | collective-permute-start | bytes 196616 | tf_op jit(solution)/shard_map/ppermute | solution.py:342
  45.8 2.5 %collective-permute-done.12.recv_ref = f32[64,256]{1,0:T(8,128)S(1)} collective-permute-done((f32[64,256]{1,0:T(8,128)S(1)}, f32[64,256]{1,0:T(8,128)S(1)}, u32[]{:S(2)}, u32[]{:S(2)}) %collective-permute-start.12) | collective-permute-done | bytes 65568 | tf_op jit(solution)/shard_map/ppermute | solution.py:342
  49.0 1.6 %collective-permute-start.13 = (f32[128,128]{1,0:T(8,128)S(1)}, f32[128,128]{1,0:T(8,128)S(1)}, u32[]{:S(2)}, u32[]{:S(2)}) collective-permute-start(f32[128,128]{1,0:T(8,128)S(1)} %get-tuple-element.31), channel_id=1, source_target_pairs={{0,2},{1,3},{2,0},{3,1},{4,6},{5,7},{6,4},{7,5},{8,10},{9,11},{10,... | collective-permute-start | bytes 196616 | tf_op jit(solution)/shard_map/ppermute | solution.py:342
  50.6 2.0 %collective-permute-start.14 = (f32[128,128]{1,0:T(8,128)S(1)}, f32[128,128]{1,0:T(8,128)S(1)}, u32[]{:S(2)}, u32[]{:S(2)}) collective-permute-start(f32[128,128]{1,0:T(8,128)S(1)} %get-tuple-element.32), channel_id=1, source_target_pairs={{0,4},{1,5},{2,6},{3,7},{4,0},{5,1},{6,2},{7,3},{8,12},{9,13},{10,... | collective-permute-start | bytes 196616 | tf_op jit(solution)/shard_map/ppermute | solution.py:342
  52.6 0.8 %collective-permute-done.13.refs_1_ = f32[128,128]{1,0:T(8,128)S(1)} collective-permute-done((f32[128,128]{1,0:T(8,128)S(1)}, f32[128,128]{1,0:T(8,128)S(1)}, u32[]{:S(2)}, u32[]{:S(2)}) %collective-permute-start.13) | collective-permute-done | bytes 65568 | tf_op jit(solution)/shard_map/ppermute | solution.py:342
  53.3 2.0 %collective-permute-done.14.refs_2_ = f32[128,128]{1,0:T(8,128)S(1)} collective-permute-done((f32[128,128]{1,0:T(8,128)S(1)}, f32[128,128]{1,0:T(8,128)S(1)}, u32[]{:S(2)}, u32[]{:S(2)}) %collective-permute-start.14) | collective-permute-done | bytes 65568 | tf_op jit(solution)/shard_map/ppermute | solution.py:342
  55.3 2.4 %collective-permute-done.15.refs_3_ = f32[128,128]{1,0:T(8,128)S(1)} collective-permute-done((f32[128,128]{1,0:T(8,128)S(1)}, f32[128,128]{1,0:T(8,128)S(1)}, u32[]{:S(2)}, u32[]{:S(2)}) %collective-permute-start.15) | collective-permute-done | bytes 65568 | tf_op jit(solution)/shard_map/ppermute | solution.py:342
  (52 shorter events, 7.4 us)
Async XLA Ops:
  0.6 9.5 %copy-start = (bf16[4,1024,128]{2,1,0:T(8,128)(2,1)S(1)}, bf16[4,1024,128]{2,1,0:T(8,128)(2,1)}, u32[]{:S(2)}) copy-start(bf16[4,1024,128]{2,1,0:T(8,128)(2,1)} %param.10) | copy-start | bytes 3145732
  0.7 5.9 %copy-start.1 = (bf16[4,512,128]{2,1,0:T(8,128)(2,1)S(1)}, bf16[4,512,128]{2,1,0:T(8,128)(2,1)}, u32[]{:S(2)}) copy-start(bf16[4,512,128]{2,1,0:T(8,128)(2,1)} %param.9) | copy-start | bytes 1572868
  1.9 11.0 %collective-permute-start = (bf16[512,128]{1,0:T(8,128)(2,1)S(1)}, bf16[512,128]{1,0:T(8,128)(2,1)S(1)}, u32[]{:S(2)}, u32[]{:S(2)}) collective-permute-start(bf16[512,128]{1,0:T(8,128)(2,1)S(1)} %get-tuple-element.39), channel_id=1, source_target_pairs={{0,2},{1,3},{2,0},{3,1},{4,6},{5,7},{6,4},{7,5},{8,10},{9,11},{10,... | collective-permute-start | bytes 393224 | tf_op jit(solution)/shard_map/ppermute | solution.py:342
  5.0 8.0 %collective-permute-start.1 = (bf16[512,128]{1,0:T(8,128)(2,1)S(1)}, bf16[512,128]{1,0:T(8,128)(2,1)S(1)}, u32[]{:S(2)}, u32[]{:S(2)}) collective-permute-start(bf16[512,128]{1,0:T(8,128)(2,1)S(1)} %get-tuple-element.41), channel_id=1, source_target_pairs={{0,4},{1,5},{2,6},{3,7},{4,0},{5,1},{6,2},{7,3},{8,12},{9,13},{10,... | collective-permute-start | bytes 393224 | tf_op jit(solution)/shard_map/ppermute | solution.py:342
  6.6 7.4 %collective-permute-start.2 = (bf16[512,128]{1,0:T(8,128)(2,1)S(1)}, bf16[512,128]{1,0:T(8,128)(2,1)S(1)}, u32[]{:S(2)}, u32[]{:S(2)}) collective-permute-start(bf16[512,128]{1,0:T(8,128)(2,1)S(1)} %get-tuple-element.38), channel_id=1, source_target_pairs={{0,6},{1,7},{2,4},{3,5},{4,2},{5,3},{6,0},{7,1},{8,14},{9,15},{10,... | collective-permute-start | bytes 393224 | tf_op jit(solution)/shard_map/ppermute | solution.py:342
  6.6 19.9 %collective-permute-start.3 = (bf16[512,128]{1,0:T(8,128)(2,1)S(1)}, bf16[512,128]{1,0:T(8,128)(2,1)S(1)}, u32[]{:S(2)}, u32[]{:S(2)}) collective-permute-start(bf16[512,128]{1,0:T(8,128)(2,1)S(1)} %get-tuple-element.35), channel_id=1, source_target_pairs={{0,2},{1,3},{2,0},{3,1},{4,6},{5,7},{6,4},{7,5},{8,10},{9,11},{10,... | collective-permute-start | bytes 393224 | tf_op jit(solution)/shard_map/ppermute | solution.py:342
  8.6 17.9 %collective-permute-start.4 = (bf16[512,128]{1,0:T(8,128)(2,1)S(1)}, bf16[512,128]{1,0:T(8,128)(2,1)S(1)}, u32[]{:S(2)}, u32[]{:S(2)}) collective-permute-start(bf16[512,128]{1,0:T(8,128)(2,1)S(1)} %get-tuple-element.37), channel_id=1, source_target_pairs={{0,4},{1,5},{2,6},{3,7},{4,0},{5,1},{6,2},{7,3},{8,12},{9,13},{10,... | collective-permute-start | bytes 393224 | tf_op jit(solution)/shard_map/ppermute | solution.py:342
  13.0 13.6 %collective-permute-start.5 = (bf16[512,128]{1,0:T(8,128)(2,1)S(1)}, bf16[512,128]{1,0:T(8,128)(2,1)S(1)}, u32[]{:S(2)}, u32[]{:S(2)}) collective-permute-start(bf16[512,128]{1,0:T(8,128)(2,1)S(1)} %get-tuple-element.34), channel_id=1, source_target_pairs={{0,6},{1,7},{2,4},{3,5},{4,2},{5,3},{6,0},{7,1},{8,14},{9,15},{10,... | collective-permute-start | bytes 393224 | tf_op jit(solution)/shard_map/ppermute | solution.py:342
  16.3 1.4 %collective-permute-start.6 = (bf16[512,128]{1,0:T(8,128)(2,1)S(1)}, bf16[512,128]{1,0:T(8,128)(2,1)S(1)}, u32[]{:S(2)}, u32[]{:S(2)}) collective-permute-start(bf16[512,128]{1,0:T(8,128)(2,1)S(1)} %get-tuple-element.21), channel_id=1, source_target_pairs={{0,1},{1,0},{2,3},{3,2},{4,5},{5,4},{6,7},{7,6},{8,9},{9,8},{10,11... | collective-permute-start | bytes 393224 | tf_op jit(solution)/shard_map/ppermute | solution.py:342
  17.8 7.8 %collective-permute-start.7 = (bf16[512,128]{1,0:T(8,128)(2,1)S(1)}, bf16[512,128]{1,0:T(8,128)(2,1)S(1)}, u32[]{:S(2)}, u32[]{:S(2)}) collective-permute-start(bf16[512,128]{1,0:T(8,128)(2,1)S(1)} %add_convert_fusion), channel_id=1, source_target_pairs={{0,12},{1,13},{2,14},{3,15},{4,8},{5,9},{6,10},{7,11},{8,4},{9,5},... | collective-permute-start | bytes 393224 | tf_op jit(solution)/shard_map/ppermute | solution.py:342
  25.8 0.7 %copy-start.2 = (s32[8]{0:T(128)S(1)}, s32[8]{0:T(128)}, u32[]{:S(2)}) copy-start(s32[8]{0:T(128)} %param.13) | copy-start | bytes 100
  25.9 1.4 %collective-permute-start.8 = (bf16[512,128]{1,0:T(8,128)(2,1)S(1)}, bf16[512,128]{1,0:T(8,128)(2,1)S(1)}, u32[]{:S(2)}, u32[]{:S(2)}) collective-permute-start(bf16[512,128]{1,0:T(8,128)(2,1)S(1)} %multiply_convert_fusion.refs_8_), channel_id=1, source_target_pairs={{0,1},{1,0},{2,3},{3,2},{4,5},{5,4},{6,7},{7,6},{8,9},{9,8},{10,11... | collective-permute-start | bytes 393224 | tf_op jit(solution)/shard_map/ppermute | solution.py:342
  30.7 1.6 %collective-permute-start.9 = (bf16[528,256]{1,0:T(8,128)(2,1)S(1)}, bf16[528,256]{1,0:T(8,128)(2,1)S(1)}, u32[]{:S(2)}, u32[]{:S(2)}) collective-permute-start(bf16[528,256]{1,0:T(8,128)(2,1)S(1)} %get-tuple-element.24), channel_id=1, source_target_pairs={{0,1},{1,0},{2,3},{3,2},{4,5},{5,4},{6,7},{7,6},{8,9},{9,8},{10,11... | collective-permute-start | bytes 811016 | tf_op jit(solution)/shard_map/ppermute | solution.py:342
  32.4 7.7 %collective-permute-start.10 = (bf16[272,256]{1,0:T(8,128)(2,1)S(1)}, bf16[272,256]{1,0:T(8,128)(2,1)S(1)}, u32[]{:S(2)}, u32[]{:S(2)}) collective-permute-start(bf16[272,256]{1,0:T(8,128)(2,1)S(1)} %get-tuple-element.27), channel_id=1, source_target_pairs={{0,12},{1,13},{2,14},{3,15},{4,8},{5,9},{6,10},{7,11},{8,4},{9,5},... | collective-permute-start | bytes 417800 | tf_op jit(solution)/shard_map/ppermute | solution.py:342
  40.6 1.3 %collective-permute-start.11 = (f32[64,256]{1,0:T(8,128)S(1)}, f32[64,256]{1,0:T(8,128)S(1)}, u32[]{:S(2)}, u32[]{:S(2)}) collective-permute-start(f32[64,256]{1,0:T(8,128)S(1)} %get-tuple-element.28.own_ref), channel_id=1, source_target_pairs={{0,1},{1,0},{2,3},{3,2},{4,5},{5,4},{6,7},{7,6},{8,9},{9,8},{10,11... | collective-permute-start | bytes 196616 | tf_op jit(solution)/shard_map/ppermute | solution.py:342
  42.1 6.2 %collective-permute-start.12 = (f32[64,256]{1,0:T(8,128)S(1)}, f32[64,256]{1,0:T(8,128)S(1)}, u32[]{:S(2)}, u32[]{:S(2)}) collective-permute-start(f32[64,256]{1,0:T(8,128)S(1)} %shard_map.101.own_ref), channel_id=1, source_target_pairs={{0,12},{1,13},{2,14},{3,15},{4,8},{5,9},{6,10},{7,11},{8,4},{9,5},... | collective-permute-start | bytes 196616 | tf_op jit(solution)/shard_map/ppermute | solution.py:342
  49.0 4.3 %collective-permute-start.13 = (f32[128,128]{1,0:T(8,128)S(1)}, f32[128,128]{1,0:T(8,128)S(1)}, u32[]{:S(2)}, u32[]{:S(2)}) collective-permute-start(f32[128,128]{1,0:T(8,128)S(1)} %get-tuple-element.31), channel_id=1, source_target_pairs={{0,2},{1,3},{2,0},{3,1},{4,6},{5,7},{6,4},{7,5},{8,10},{9,11},{10,... | collective-permute-start | bytes 196616 | tf_op jit(solution)/shard_map/ppermute | solution.py:342
  50.6 4.7 %collective-permute-start.14 = (f32[128,128]{1,0:T(8,128)S(1)}, f32[128,128]{1,0:T(8,128)S(1)}, u32[]{:S(2)}, u32[]{:S(2)}) collective-permute-start(f32[128,128]{1,0:T(8,128)S(1)} %get-tuple-element.32), channel_id=1, source_target_pairs={{0,4},{1,5},{2,6},{3,7},{4,0},{5,1},{6,2},{7,3},{8,12},{9,13},{10,... | collective-permute-start | bytes 196616 | tf_op jit(solution)/shard_map/ppermute | solution.py:342
  52.6 5.2 %collective-permute-start.15 = (f32[128,128]{1,0:T(8,128)S(1)}, f32[128,128]{1,0:T(8,128)S(1)}, u32[]{:S(2)}, u32[]{:S(2)}) collective-permute-start(f32[128,128]{1,0:T(8,128)S(1)} %get-tuple-element.33), channel_id=1, source_target_pairs={{0,6},{1,7},{2,4},{3,5},{4,2},{5,3},{6,0},{7,1},{8,14},{9,15},{10,... | collective-permute-start | bytes 196616 | tf_op jit(solution)/shard_map/ppermute | solution.py:342

commit v4 on v3

--- a/solution.py
+++ b/solution.py
@@ -76,73 +76,93 @@
     return jax.ShapeDtypeStruct(dims, dtype)
 
 
-def fill_weights(unit_keys, pieces, raised_ref, weight_ref, first, mass_ref):
+def fill_raised(piece, unit_keys, raised_ref, row, first):
     tokens = unit_keys.shape[0]
     factor = SHARPNESS * math.log2(math.e)
     total = jnp.zeros((1, tokens), F32)
-    row = 0
-    tiles = []
-    for piece in pieces:
-        tile = min(TILE, piece.shape[0])
-        for at in range(0, piece.shape[0], tile):
-            raised = jnp.exp2(dot_nt(piece[at : at + tile, :], unit_keys) * factor)
-            raised_ref[row : row + tile, :tokens] = raised
-            total = total + jnp.sum(raised, axis=0, keepdims=True)
-            tiles.append((row, tile))
-            row += tile
-    inverse = 1.0 / total
-    for row, tile in tiles:
-        weights = raised_ref[row : row + tile, :tokens] * inverse
-        weight_ref[row : row + tile, first : first + tokens] = weights.astype(BF16)
+    tile = min(TILE, piece.shape[0])
+    for at in range(0, piece.shape[0], tile):
+        raised = jnp.exp2(dot_nt(piece[at : at + tile, :], unit_keys) * factor)
+        raised_ref[row + at : row + at + tile, first : first + tokens] = raised.astype(
+            raised_ref.dtype
+        )
+        total = total + jnp.sum(raised, axis=0, keepdims=True)
+    return total
+
+
+def fill_weights(raised_ref, inverse, weight_ref, rows, from_row, first, raised_first, mass_ref):
+    tokens = inverse.shape[1]
+    tile = min(TILE, rows)
+    for at in range(0, rows, tile):
+        raised = raised_ref[
+            from_row + at : from_row + at + tile, raised_first : raised_first + tokens
+        ]
+        weights = raised.astype(F32) * inverse
+        weight_ref[at : at + tile, first : first + tokens] = weights.astype(BF16)
         if mass_ref is not None:
             part = weights[:, :128]
-            for at in range(128, tokens, 128):
-                part = part + weights[:, at : at + 128]
+            for lane in range(128, tokens, 128):
+                part = part + weights[:, lane : lane + 128]
             if first == 0:
-                mass_ref[row : row + tile, :] = part
+                mass_ref[at : at + tile, :] = part
             else:
-                mass_ref[row : row + tile, :] += part
+                mass_ref[at : at + tile, :] += part
+
+
+def product(out_ref, weight_ref, values, sums_ref=None, row=0):
+    rows = weight_ref.shape[0]
+    tile = min(TILE, rows)
+    for at in range(0, rows, tile):
+        sums = jnp.dot(weight_ref[at : at + tile, :], values, preferred_element_type=F32)
+        if sums_ref is not None:
+            sums = sums + sums_ref[row + at : row + at + tile, :]
+        out_ref[at : at + tile, :] = sums.astype(out_ref.dtype)
 
 
 def first_kernel(
-    order_ref, key_ref, cent_ref, sums_ref, unit_ref, cents_ref, raised_ref, weight_ref
+    base_ref, order, key_ref, cent_ref, sums_ref, unit_ref, cents_ref, raised_ref, weight_ref
 ):
-    owners, per_owner, _ = cent_ref.shape
-    for at in range(owners):
-        cents_ref[at * per_owner : (at + 1) * per_owner, :] = cent_ref[order_ref[at]].astype(F32)
+    per_owner = cent_ref.shape[1]
+    for at, mask in enumerate(order):
+        cents_ref[at * per_owner : (at + 1) * per_owner, :] = cent_ref[base_ref[0] ^ mask].astype(
+            F32
+        )
     unit_ref[...] = to_unit(cents_ref[...]).astype(BF16)
     keys = key_ref[...]
-    fill_weights(to_unit(keys).astype(BF16), (unit_ref,), raised_ref, weight_ref, 0, None)
-    rows = sums_ref.shape[0]
-    tile = min(TILE, rows)
-    for row in range(0, rows, tile):
-        sums_ref[row : row + tile, :] = jnp.dot(
-            weight_ref[row : row + tile, :], keys, preferred_element_type=F32
-        )
+    inverse = 1.0 / fill_raised(unit_ref, to_unit(keys).astype(BF16), raised_ref, 0, 0)
+    fill_weights(raised_ref, inverse, weight_ref, weight_ref.shape[0], 0, 0, 0, None)
+    product(sums_ref, weight_ref, keys)
 
 
 def rest_kernel(count, *refs):
-    key_refs, (unit_ref, sums_ref, keep_ref, send_ref, raised_ref, weight_ref) = (
+    key_refs, (unit_ref, sums_ref, send_ref, keep_weight_ref, raised_ref, weight_ref) = (
         refs[:count],
         refs[count:],
     )
+    half = send_ref.shape[0]
     first = 0
     for key_ref in key_refs:
         unit_keys = to_unit(key_ref[...]).astype(BF16)
-        fill_weights(unit_keys, (unit_ref,), raised_ref, weight_ref, first, None)
+        inverse = 1.0 / fill_raised(unit_ref, unit_keys, raised_ref, 0, 0)
+        fill_weights(raised_ref, inverse, weight_ref, half, half, first, 0, None)
+        fill_weights(raised_ref, inverse, keep_weight_ref, half, 0, first, 0, None)
         first += unit_keys.shape[0]
-    keys = jnp.concatenate([key_ref[...] for key_ref in key_refs], axis=0)
-    half = keep_ref.shape[0]
-    tile = min(TILE, half)
-    for row in range(0, half, tile):
-        keep_ref[row : row + tile, :] = sums_ref[row : row + tile, :] + jnp.dot(
-            weight_ref[row : row + tile, :], keys, preferred_element_type=F32
-        )
-    for row in range(half, 2 * half, tile):
-        send_ref[row - half : row - half + tile, :] = (
-            sums_ref[row : row + tile, :]
-            + jnp.dot(weight_ref[row : row + tile, :], keys, preferred_element_type=F32)
-        ).astype(BF16)
+    product(send_ref, weight_ref, joined_rows(key_refs), sums_ref, half)
+
+
+def keep_kernel(count, *refs):
+    key_refs, (sums_ref, weight_ref, keep_ref) = refs[:count], refs[count:]
+    product(keep_ref, weight_ref, joined_rows(key_refs), sums_ref, 0)
+
+
+def joined_rows(refs):
+    return jnp.concatenate([ref[...] for ref in refs], axis=0)
+
+
+def joined_pairs(key_refs, value_refs):
+    return jnp.concatenate(
+        [jnp.concatenate([k[...], v[...]], axis=1) for k, v in zip(key_refs, value_refs)], axis=0
+    )
 
 
 def packed_masses(row, lanes):
@@ -170,32 +190,51 @@
     )
 
 
-def second_kernel(count, *refs):
-    key_refs, value_refs = refs[:count], refs[count : 2 * count]
-    own_ref, other_ref, keep_ref, keep_mass_ref, send_ref, raised_ref, weight_ref, mass_ref = refs[
-        2 * count :
-    ]
+def own_half_kernel(count, *refs):
+    key_refs, (cent_ref, unit_ref, raised_ref, total_ref) = refs[:count], refs[count:]
     first = 0
     for key_ref in key_refs:
         unit_keys = to_unit(key_ref[...]).astype(BF16)
-        fill_weights(unit_keys, (own_ref, other_ref), raised_ref, weight_ref, first, mass_ref)
-        first += unit_keys.shape[0]
-    pairs = jnp.concatenate(
-        [jnp.concatenate([k[...], v[...]], axis=1) for k, v in zip(key_refs, value_refs)], axis=0
-    )
-    half, lanes = keep_ref.shape
-    tile = min(TILE, half)
-    for row in range(half, 2 * half, tile):
-        send_ref[row - half : row - half + tile, :] = jnp.dot(
-            weight_ref[row : row + tile, :], pairs, preferred_element_type=F32
-        ).astype(BF16)
-    for row in range(0, half, tile):
-        keep_ref[row : row + tile, :] = jnp.dot(
-            weight_ref[row : row + tile, :], pairs, preferred_element_type=F32
-        )
+        tokens = unit_keys.shape[0]
+        unit_ref[first : first + tokens, :] = unit_keys
+        total = fill_raised(cent_ref, unit_keys, raised_ref, 0, first)
+        total_ref[:, first : first + tokens] = jnp.broadcast_to(total, (8, tokens))
+        first += tokens
+
+
+def other_half_kernel(count, *refs):
+    key_refs, value_refs = refs[:count], refs[count : 2 * count]
+    unit_ref, cent_ref, total_ref, send_ref, inverse_ref, raised_ref, weight_ref, mass_ref = refs[
+        2 * count :
+    ]
+    half, lanes = cent_ref.shape[0], send_ref.shape[1]
+    first = 0
+    for key_ref in key_refs:
+        tokens = key_ref.shape[0]
+        chunk = slice(first, first + tokens)
+        total = fill_raised(cent_ref, unit_ref[chunk, :], raised_ref, 0, 0)
+        inverse = 1.0 / (total_ref[0:1, chunk] + total)
+        inverse_ref[:, chunk] = jnp.broadcast_to(inverse, (8, tokens))
+        fill_weights(raised_ref, inverse, weight_ref, half, 0, first, 0, mass_ref)
+        first += tokens
     masses = jnp.sum(mass_ref[...].T, axis=0, keepdims=True)
-    keep_mass_ref[...] = jnp.broadcast_to(masses[:, :half], keep_mass_ref.shape)
-    send_ref[half:, :] = packed_masses(masses[:, half:], lanes)
+    send_ref[half:, :] = packed_masses(masses, lanes)
+    product(send_ref, weight_ref, joined_pairs(key_refs, value_refs))
+
+
+def keep_half_kernel(count, *refs):
+    key_refs, value_refs = refs[:count], refs[count : 2 * count]
+    raised_ref, inverse_ref, keep_ref, keep_mass_ref, weight_ref, mass_ref = refs[2 * count :]
+    half = keep_ref.shape[0]
+    first = 0
+    for key_ref in key_refs:
+        tokens = key_ref.shape[0]
+        inverse = inverse_ref[0:1, first : first + tokens]
+        fill_weights(raised_ref, inverse, weight_ref, half, 0, first, first, mass_ref)
+        first += tokens
+    masses = jnp.sum(mass_ref[...].T, axis=0, keepdims=True)
+    keep_mass_ref[...] = jnp.broadcast_to(masses, keep_mass_ref.shape)
+    product(keep_ref, weight_ref, joined_pairs(key_refs, value_refs))
 
 
 def halve_kernel(keep_ref, mass_ref, recv_ref, keep_out_ref, mass_out_ref, send_ref):
@@ -236,23 +275,55 @@
     return state[:, dim : dim + 1], state[:, dim + dim // 2 : dim + dim // 2 + 1], state[:, :dim]
 
 
-def exact_kernel(count, *refs):
-    key_refs, value_refs = refs[:count], refs[count : 2 * count]
-    query_ref, limit_ref, out_ref = refs[2 * count :]
-    queries = query_ref[...]
-    rows, dim = queries.shape
-    keys = jnp.concatenate([k[...] for k in key_refs], axis=0)
-    values = jnp.concatenate([v[...] for v in value_refs], axis=0)
-    scores = dot_nt(queries, keys) * dim ** (-0.5)
+def exact_kernel(count, head_masks, owned_by, per_owner, *refs):
+    scalar_refs, key_refs, value_refs = (
+        refs[:5],
+        refs[5 : 5 + count],
+        refs[5 + count : 5 + 2 * count],
+    )
+    head_ref, index_ref, base_ref, position_ref, cluster_ref = scalar_refs
+    query_ref, chosen_ref, out_ref, own_query_ref, usable_ref = refs[5 + 2 * count :]
+    head, index, base = head_ref[0], index_ref[0], base_ref[0]
+    requests, _, group, dim = query_ref.shape
+    rows = requests * group
+    for r in range(requests):
+        own_query_ref[r * group : (r + 1) * group, :] = query_ref[r, head].astype(F32)
+    queries = own_query_ref[...].astype(BF16)
+    ksel = chosen_ref.shape[2]
+    chosen = jnp.concatenate(
+        [
+            jnp.broadcast_to(chosen_ref[r, pl.ds(head, 1), :], (group, ksel))
+            for r in range(requests)
+        ],
+        axis=0,
+    )
+    positions = jnp.concatenate(
+        [jnp.full((group, 1), position_ref[r], jnp.int32) for r in range(requests)], axis=0
+    )
     lane = lax.broadcasted_iota(jnp.int32, (rows, BLOCK), 1)
-    usable = jnp.concatenate(
-        [
-            jnp.where(lane < limit_ref[:, i : i + 1], 1.0, 0.0)
-            for i in range(keys.shape[0] // BLOCK)
-        ],
-        axis=1,
-    )
-    out_ref[...] = packed_state(*softmax_part(scores, usable > 0.5, values))
+    blocks = key_refs[0].shape[0] // BLOCK
+    parts = []
+    for mask in head_masks:
+        for block in range(blocks):
+            at = (index ^ mask) * blocks + block
+            picked = jnp.max(
+                jnp.where(chosen == cluster_ref[head, at], 1, 0).astype(F32), axis=1, keepdims=True
+            )
+            limit = jnp.where(picked > 0.5, positions - at * BLOCK, 0)
+            parts.append(jnp.where(lane < limit, 1.0, 0.0))
+    scores = dot_nt(queries, joined_rows(key_refs)) * dim ** (-0.5)
+    usable = jnp.concatenate(parts, axis=1) > 0.5
+    out_ref[...] = packed_state(*softmax_part(scores, usable, joined_rows(value_refs)))
+    owned = usable_ref.shape[1]
+    place = lax.broadcasted_iota(jnp.int32, (rows, owned), 1)
+    ids = place
+    for part, mask in enumerate(owned_by):
+        shift = (base ^ mask) * per_owner - part * per_owner
+        ids = jnp.where((place >= part * per_owner) & (place < (part + 1) * per_owner), place + shift, ids)
+    free = jnp.ones((rows, owned), F32)
+    for k in range(ksel):
+        free = jnp.where(chosen[:, k : k + 1] == ids, 0.0, free)
+    usable_ref[...] = free
 
 
 def summary_kernel(
@@ -266,7 +337,8 @@
     column = jnp.broadcast_to(masses, (dim, count)).T
     mean_keys = (sums[:, :dim] / column).astype(BF16)
     mean_values = (sums[:, dim:] / column).astype(BF16)
-    scores = dot_nt(query_ref[...], mean_keys) * dim ** (-0.5) + jnp.log(masses)
+    queries = query_ref[...].astype(BF16)
+    scores = dot_nt(queries, mean_keys) * dim ** (-0.5) + jnp.log(masses)
     state = softmax_part(scores, usable_ref[...] > 0.5, mean_values)
     state_ref[...] = packed_state(*joined(unpacked_state(exact_ref[...]), state))
 
@@ -281,11 +353,11 @@
     out_ref[...] = packed_state(*joined(unpacked_state(former), unpacked_state(latter)))
 
 
-def last_merge_kernel(scalar_ref, own_ref, recv_ref, cent_ref, *pack_refs):
-    former, latter = in_order(scalar_ref[0] != 0, own_ref, recv_ref)
+def last_merge_kernel(flip_ref, head_ref, own_ref, recv_ref, cent_ref, *pack_refs):
+    former, latter = in_order(flip_ref[0] != 0, own_ref, recv_ref)
     _, weight_sum, weighted = joined(unpacked_state(former), unpacked_state(latter))
     attended = weighted / weight_sum
-    own = scalar_ref[1]
+    own = head_ref[0]
     per_owner = cent_ref.shape[1]
     for step, pack_ref in enumerate(pack_refs):
         pack_ref[:per_owner, :] = cent_ref[own ^ step]
@@ -319,7 +391,6 @@
     clusters = init_centroids.shape[1]
     requests, _, group, _ = queries.shape
     per_owner = clusters // devices
-    blk_dev = tok_dev // BLOCK
     spread = devices // heads
     levels = spread.bit_length() - 1
     if heads * spread != devices or 1 << levels != spread or heads & (heads - 1) or levels < 2:
@@ -349,13 +420,14 @@
 
     blocks = pick(init_centroids, head).reshape(devices, per_owner, dim)
     turned = [int(format(r, f"0{levels}b")[::-1], 2) for r in range(spread)]
-    order = jnp.stack([base ^ rank_masks[r] ^ mask for r in turned for mask in head_masks])
+    order = [rank_masks[r] ^ mask for r in turned for mask in head_masks]
+    scalar_base = base.reshape(1)
 
     pass_flops = 4 * tok_dev * clusters * dim
     sums, unit_cents = call(
-        first_kernel,
+        lambda base_ref, *refs: first_kernel(base_ref, order, *refs),
         [shape((clusters, dim), F32), shape((clusters, dim), BF16)],
-        [order, keys[0], blocks],
+        [scalar_base, keys[0], blocks],
         [
             pltpu.VMEM((clusters, dim), F32),
             pltpu.VMEM((clusters, tok_dev), F32),
@@ -364,20 +436,28 @@
         pass_flops,
         scalars=1,
     )
-    keep, send = call(
+    values = [pick(value_cache, head)]
+    values += [over(pick(value_cache, head ^ s), head_masks[s]) for s in range(1, heads)]
+
+    send, keep_weights = call(
         functools.partial(rest_kernel, heads - 1),
-        [shape((half, dim), F32), shape((half, dim), BF16)],
+        [shape((half, dim), BF16), shape((half, (heads - 1) * tok_dev), BF16)],
         [*keys[1:], unit_cents, sums],
         [
             pltpu.VMEM((clusters, tok_dev), F32),
-            pltpu.VMEM((clusters, (heads - 1) * tok_dev), BF16),
+            pltpu.VMEM((half, (heads - 1) * tok_dev), BF16),
         ],
         pass_flops * (heads - 1),
     )
-
-    values = [pick(value_cache, head)]
-    values += [over(pick(value_cache, head ^ s), head_masks[s]) for s in range(1, heads)]
-
+    (keep,) = call(
+        functools.partial(keep_kernel, heads - 1),
+        [shape((half, dim), F32)],
+        [*keys[1:], sums, keep_weights],
+        (),
+        pass_flops * (heads - 1) // 4,
+    )
+
+    keep, values[1], values[2], values[3] = lax.optimization_barrier((keep, values[1], values[2], values[3]))
     for level in range(levels - 1):
         total = keep + over(send, rank_basis[level]).astype(F32)
         if level < levels - 2:
@@ -392,44 +472,47 @@
         own_cents = jnp.concatenate([own_cents, over(own_cents, rank_basis[level])])
     other_cents = over(own_cents, 1)
 
-    keep, keep_mass, send = call(
-        functools.partial(second_kernel, heads),
+    tokens = heads * tok_dev
+    unit_keys, raised, total = call(
+        functools.partial(own_half_kernel, heads),
+        [shape((tokens, dim), BF16), shape((half, tokens), BF16), shape((8, tokens), F32)],
+        [*keys, own_cents],
+        (),
+        pass_flops * heads // 4,
+    )
+    half_scratch = [pltpu.VMEM((half, tokens), BF16), pltpu.VMEM((half, 128), F32)]
+    send, inverse = call(
+        functools.partial(other_half_kernel, heads),
+        [shape((half + 16, 2 * dim), BF16), shape((8, tokens), F32)],
+        [*keys, *values, unit_keys, other_cents, total],
+        [pltpu.VMEM((half, tok_dev), F32), *half_scratch],
+        pass_flops * heads * 3 // 4,
+    )
+    keep, keep_mass = call(
+        functools.partial(keep_half_kernel, heads),
+        [shape((half, 2 * dim), F32), shape((8, half), F32)],
+        [*keys, *values, raised, inverse],
+        half_scratch,
+        pass_flops * heads // 2,
+    )
+
+    exact, own_queries, usable = call(
+        functools.partial(exact_kernel, heads, head_masks, head_masks, per_owner),
+        [shape((rows, 2 * dim), F32), shape((rows, dim), F32), shape((rows, owned), F32)],
         [
-            shape((half, 2 * dim), F32),
-            shape((8, half), F32),
-            shape((half + 16, 2 * dim), BF16),
+            head.reshape(1),
+            index.reshape(1),
+            scalar_base,
+            request_positions,
+            block_clusters,
+            *keys,
+            *values,
+            queries,
+            chosen_clusters,
         ],
-        [*keys, *values, own_cents, other_cents],
-        [
-            pltpu.VMEM((clusters, tok_dev), F32),
-            pltpu.VMEM((clusters, heads * tok_dev), BF16),
-            pltpu.VMEM((clusters, 128), F32),
-        ],
-        pass_flops * heads * 3 // 2,
-    )
-
-    own_queries = pick(queries, head, 1).reshape(rows, dim)
-    own_chosen = pick(chosen_clusters, head, 1)
-    held_by = jnp.stack([index ^ mask for mask in head_masks])
-    block_ids = (held_by[:, None] * blk_dev + jnp.arange(blk_dev, dtype=jnp.int32)).reshape(-1)
-    held = pick(block_clusters, head).reshape(devices, blk_dev)
-    held = jnp.stack([pick(held, index ^ mask) for mask in head_masks]).reshape(-1)
-    picked = jnp.any(own_chosen[:, :, None] == held, axis=1)
-    limits = jnp.where(
-        picked, jnp.clip(request_positions[:, None] - block_ids * BLOCK, 0, BLOCK), 0
-    )
-    limits = jnp.repeat(limits, group, axis=0)
-    owners = (base ^ jnp.array(head_masks, jnp.int32))[:, None]
-    owned_ids = (owners * per_owner + jnp.arange(per_owner, dtype=jnp.int32)).reshape(-1)
-    usable = jnp.all(own_chosen[:, :, None] != owned_ids, axis=1).astype(F32)
-    usable = jnp.repeat(usable, group, axis=0)
-
-    (exact,) = call(
-        functools.partial(exact_kernel, heads),
-        [shape((rows, 2 * dim), F32)],
-        [*keys, *values, own_queries, limits],
         (),
         4 * rows * heads * tok_dev * dim,
+        scalars=5,
     )
 
     for level in range(levels - 1):
@@ -460,17 +543,18 @@
             [flip, state, over(state, rank_basis[level])],
             scalars=1,
         )
-    scalars = jnp.stack([(rank >> (levels - 1)) & 1, head])
+    flip = ((rank >> (levels - 1)) & 1).reshape(1)
     packs = call(
         last_merge_kernel,
         [shape((per_owner + rows, dim), F32)] * heads,
         [
-            scalars,
+            flip,
+            head.reshape(1),
             state,
             over(state, rank_basis[levels - 1]),
             centroids.reshape(heads, per_owner, dim),
         ],
-        scalars=1,
+        scalars=2,
     )
     packs = [packs[0]] + [over(packs[s], head_masks[s]) for s in range(1, heads)]
     return call(

time: 58.7 us -> 56 us (0.954)
  local copies, waits for them, and re-layouts: 4.37 us -> 2.41 us
  other arithmetic: 1.12 us -> 0.33 us
    dynamic_slice x4 -> x1, local copies, waits for them, and re-layouts: 1.47 us -> 0.02 us  [pick(): return lax.dynamic_index_in_dim(array, at, axis, keepdims=False)]
    squeeze x2, local copies, waits for them, and re-layouts: 1.28 us -> 2.35 us  [pick(): return lax.dynamic_index_in_dim(array, at, axis, keepdims=False)]
    reshape x4 -> x0, local copies, waits for them, and re-layouts: 0.81 us -> none  [the longest x1 0.72 us: body(): own_queries = pick(queries, head, 1).reshape(rows, dim)]
    pallas_call x9 -> x12, Pallas kernels: 10.3 us -> 10.5 us  [call(): pl.pallas_call(kernel, out_shape=tuple(outs), in_specs=in_specs, out_spec...]
  transfers between devices with their start and end apart: 16 -> 16, of which waited for: 11 -> 12; matrix products, arithmetic and copies ran while one was open for 7% -> 2% of each run, Pallas kernels for 8% -> 13%
where the time goes in v4:
time: 56 us; the launch traced here: 55.9 us
  starting transfers between devices  23.1 us (41%)
  waiting for transfers between devices  18.7 us (33%)
  Pallas kernels  10.5 us (19%)
  local copies, waits for them, and re-layouts  2.41 us (4%)
  between operations  0.87 us (2%)
    ppermute x16, starting transfers between devices, over(): return lax.ppermute(array, 'ctx', [(i, i ^ bit) for i in range(devices)])  23.1 us
    ppermute x16, waiting for transfers between devices, over(): return lax.ppermute(array, 'ctx', [(i, i ^ bit) for i in range(devices)])  18.7 us
    pallas_call x12, Pallas kernels, call(): pl.pallas_call(kernel, out_shape=tuple(outs), in_specs=in_specs, out_spec...  10.5 us
    squeeze x2, local copies, waits for them, and re-layouts, pick(): return lax.dynamic_index_in_dim(array, at, axis, keepdims=False)  2.35 us
  transfers between devices with their start and end apart: 16, of which 12 were waited for; matrix products, arithmetic and copies ran while one was open for 2% of the time, Pallas kernels for 13%

profile of v4, /device:TPU:0, one launch (start us, length us, event | category | flops | bytes accessed | tf_op | source)
XLA Modules:
  0.0 55.9 jit_solution(13902759152463415529)
XLA Ops:
  0.7 1.2 %dynamic-slice_bitcast_fusion.4 = (bf16[512,128]{1,0:T(8,128)(2,1)S(1)}, bf16[512,128]{1,0:T(8,128)(2,1)S(1)}, bf16[512,128]{1,0:T(8,128)(2,1)S(1)}, bf16[512,128]{1,0:T(8,128)(2,1)S(1)}) fusion(bf16[4,512,128]{2,1,0:T(8,128)(2,1)} %param.7, s32[]{:T(128)S(6)} %select_n.22, s32[]{:T(128)S(6)} %select_n.20, s32[]{:T(128)S(6)} %select_n.19, s32[]{:T(128)S(6)} %select_n.21), kind=kLoop, calls=%fused_computation.9 | loop fusion | bytes 1048592 | tf_op jit(solution)/shard_map/jit(dynamic_index_in_dim)/squeeze | solution.py:416
  1.9 3.0 %collective-permute-start = (bf16[512,128]{1,0:T(8,128)(2,1)S(1)}, bf16[512,128]{1,0:T(8,128)(2,1)S(1)}, u32[]{:S(2)}, u32[]{:S(2)}) collective-permute-start(bf16[512,128]{1,0:T(8,128)(2,1)S(1)} %get-tuple-element.61), channel_id=1, source_target_pairs={{0,2},{1,3},{2,0},{3,1},{4,6},{5,7},{6,4},{7,5},{8,10},{9,11},{10,... | collective-permute-start | bytes 393224 | tf_op jit(solution)/shard_map/ppermute | solution.py:413
  4.9 1.6 %collective-permute-start.1 = (bf16[512,128]{1,0:T(8,128)(2,1)S(1)}, bf16[512,128]{1,0:T(8,128)(2,1)S(1)}, u32[]{:S(2)}, u32[]{:S(2)}) collective-permute-start(bf16[512,128]{1,0:T(8,128)(2,1)S(1)} %get-tuple-element.63), channel_id=1, source_target_pairs={{0,4},{1,5},{2,6},{3,7},{4,0},{5,1},{6,2},{7,3},{8,12},{9,13},{10,... | collective-permute-start | bytes 393224 | tf_op jit(solution)/shard_map/ppermute | solution.py:413
  6.5 1.1 %dynamic-slice_bitcast_fusion = (bf16[512,128]{1,0:T(8,128)(2,1)S(1)}, bf16[512,128]{1,0:T(8,128)(2,1)S(1)}, bf16[512,128]{1,0:T(8,128)(2,1)S(1)}, bf16[512,128]{1,0:T(8,128)(2,1)S(1)}) fusion(bf16[4,512,128]{2,1,0:T(8,128)(2,1)} %param.8, s32[]{:T(128)S(6)} %select_n.22, s32[]{:T(128)S(6)} %select_n.20, s32[]{:T(128)S(6)} %select_n.19, s32[]{:T(128)S(6)} %select_n.21), kind=kLoop, calls=%fused_computation.5 | loop fusion | bytes 1048592 | tf_op jit(solution)/shard_map/jit(dynamic_index_in_dim)/squeeze | solution.py:416
  7.7 2.0 %collective-permute-start.3 = (bf16[512,128]{1,0:T(8,128)(2,1)S(1)}, bf16[512,128]{1,0:T(8,128)(2,1)S(1)}, u32[]{:S(2)}, u32[]{:S(2)}) collective-permute-start(bf16[512,128]{1,0:T(8,128)(2,1)S(1)} %get-tuple-element.57), channel_id=1, source_target_pairs={{0,2},{1,3},{2,0},{3,1},{4,6},{5,7},{6,4},{7,5},{8,10},{9,11},{10,... | collective-permute-start | bytes 393224 | tf_op jit(solution)/shard_map/ppermute | solution.py:413
  9.6 1.6 %collective-permute-start.4 = (bf16[512,128]{1,0:T(8,128)(2,1)S(1)}, bf16[512,128]{1,0:T(8,128)(2,1)S(1)}, u32[]{:S(2)}, u32[]{:S(2)}) collective-permute-start(bf16[512,128]{1,0:T(8,128)(2,1)S(1)} %get-tuple-element.59), channel_id=1, source_target_pairs={{0,4},{1,5},{2,6},{3,7},{4,0},{5,1},{6,2},{7,3},{8,12},{9,13},{10,... | collective-permute-start | bytes 393224 | tf_op jit(solution)/shard_map/ppermute | solution.py:413
  11.2 1.1 %shard_map.86 = (f32[1024,128]{1,0:T(8,128)S(1)}, bf16[1024,128]{1,0:T(8,128)(2,1)S(1)}) custom-call(s32[1]{0:T(128)} %bitcast.8.base_ref.refs_2_, bf16[512,128]{1,0:T(8,128)(2,1)S(1)} %get-tuple-element.62.refs_0_.refs_5_, bf16[16,64,128]{2,1,0:T(8,128)(2,1)S(1)} %bitcast.23), custom_call_target="tpu_custom_call" | custom-call | flops 268435456 | bytes 1179652 | tf_op jit(solution)/shard_map/pallas_call | solution.py:64
  12.5 1.4 %collective-permute-done.2.refs_2_.refs_3_.refs_8_ = bf16[512,128]{1,0:T(8,128)(2,1)S(1)} collective-permute-done((bf16[512,128]{1,0:T(8,128)(2,1)S(1)}, bf16[512,128]{1,0:T(8,128)(2,1)S(1)}, u32[]{:S(2)}, u32[]{:S(2)}) %collective-permute-start.2) | collective-permute-done | bytes 131104 | tf_op jit(solution)/shard_map/ppermute | solution.py:413
  13.9 2.2 %shard_map.87 = (bf16[512,128]{1,0:T(8,128)(2,1)S(1)}, bf16[512,1536]{1,0:T(8,128)(2,1)S(1)}) custom-call(bf16[512,128]{1,0:T(8,128)(2,1)S(1)} %collective-permute-done.refs_0_.refs_1_.refs_6_, bf16[512,128]{1,0:T(8,128)(2,1)S(1)} %collective-permute-done.1.refs_1_.refs_2_.refs_7_, bf16[512,128]{1,0:T(8,128)(2,1)S(1)} %collective-permute-done.2.refs_2_.refs_3_.refs_8_, ...), custom_call_target="tpu_custom_call" | custom-call | flops 805306368 | bytes 2883584 | tf_op jit(solution)/shard_map/pallas_call | solution.py:64
  16.9 1.4 %collective-permute-done.5.refs_7_.refs_12_ = bf16[512,128]{1,0:T(8,128)(2,1)S(1)} collective-permute-done((bf16[512,128]{1,0:T(8,128)(2,1)S(1)}, bf16[512,128]{1,0:T(8,128)(2,1)S(1)}, u32[]{:S(2)}, u32[]{:S(2)}) %collective-permute-start.5) | collective-permute-done | bytes 131104 | tf_op jit(solution)/shard_map/ppermute | solution.py:413
  18.3 3.6 %collective-permute-start.7 = (bf16[512,128]{1,0:T(8,128)(2,1)S(1)}, bf16[512,128]{1,0:T(8,128)(2,1)S(1)}, u32[]{:S(2)}, u32[]{:S(2)}) collective-permute-start(bf16[512,128]{1,0:T(8,128)(2,1)S(1)} %add_convert_fusion), channel_id=1, source_target_pairs={{0,12},{1,13},{2,14},{3,15},{4,8},{5,9},{6,10},{7,11},{8,4},{9,5},... | collective-permute-start | bytes 393224 | tf_op jit(solution)/shard_map/ppermute | solution.py:413
  22.0 3.4 %collective-permute-done.7 = bf16[512,128]{1,0:T(8,128)(2,1)S(1)} collective-permute-done((bf16[512,128]{1,0:T(8,128)(2,1)S(1)}, bf16[512,128]{1,0:T(8,128)(2,1)S(1)}, u32[]{:S(2)}, u32[]{:S(2)}) %collective-permute-start.7) | collective-permute-done | bytes 131104 | tf_op jit(solution)/shard_map/ppermute | solution.py:413
  25.8 1.0 %shard_map.89 = (bf16[2048,128]{1,0:T(8,128)(2,1)S(1)}, bf16[512,2048]{1,0:T(8,128)(2,1)S(1)}, f32[8,2048]{1,0:T(8,128)S(1)}) custom-call(bf16[512,128]{1,0:T(8,128)(2,1)S(1)} %get-tuple-element.62.refs_0_.refs_5_, bf16[512,128]{1,0:T(8,128)(2,1)S(1)} %collective-permute-done.refs_0_.refs_1_.refs_6_, ...), custom_call_target="tpu_custom_call" | custom-call | flops 268435456 | bytes 3342336 | tf_op jit(solution)/shard_map/pallas_call | solution.py:64
  27.1 1.5 %shard_map.90 = (bf16[528,256]{1,0:T(8,128)(2,1)S(1)}, f32[8,2048]{1,0:T(8,128)S(1)}) custom-call(bf16[512,128]{1,0:T(8,128)(2,1)S(1)} %get-tuple-element.62.refs_0_.refs_5_, bf16[512,128]{1,0:T(8,128)(2,1)S(1)} %collective-permute-done.refs_0_.refs_1_.refs_6_, bf16[512,128]{1,0:T(8,128)(2,1)S(1)} %collective-permute-done.1.refs_1_.refs_2_.refs_7_, ...), custom_call_target="tpu_custom_call" | custom-call | flops 805306368 | bytes 2105344 | tf_op jit(solution)/shard_map/pallas_call | solution.py:64
  30.3 3.6 %collective-permute-start.10 = (bf16[272,256]{1,0:T(8,128)(2,1)S(1)}, bf16[272,256]{1,0:T(8,128)(2,1)S(1)}, u32[]{:S(2)}, u32[]{:S(2)}) collective-permute-start(bf16[272,256]{1,0:T(8,128)(2,1)S(1)} %get-tuple-element.46), channel_id=1, source_target_pairs={{0,12},{1,13},{2,14},{3,15},{4,8},{5,9},{6,10},{7,11},{8,4},{9,5},... | collective-permute-start | bytes 417800 | tf_op jit(solution)/shard_map/ppermute | solution.py:413
  34.0 1.6 %shard_map.93 = (f32[64,256]{1,0:T(8,128)S(1)}, f32[64,128]{1,0:T(8,128)S(1)}, f32[64,256]{1,0:T(8,128)S(1)}) custom-call(s32[1]{0:T(128)} %bitcast.refs_0_.head_ref.scalar_ref, s32[1]{0:T(128)} %bitcast.13.refs_1_, s32[1]{0:T(128)} %bitcast.8.base_ref.refs_2_, s32[8]{0:T(128)S(1)} %copy-done.4, s32[4,64]{1,0:T(4,128)S(1)} %copy-done.3, ...), custom_call_target="tpu_custom_call" | custom-call | flops 67108864 | bytes 1283116 | tf_op jit(solution)/shard_map/pallas_call | solution.py:64
  35.6 2.5 %collective-permute-done.10.recv_ref = bf16[272,256]{1,0:T(8,128)(2,1)S(1)} collective-permute-done((bf16[272,256]{1,0:T(8,128)(2,1)S(1)}, bf16[272,256]{1,0:T(8,128)(2,1)S(1)}, u32[]{:S(2)}, u32[]{:S(2)}) %collective-permute-start.10) | collective-permute-done | bytes 139296 | tf_op jit(solution)/shard_map/ppermute | solution.py:413
  38.7 1.2 %collective-permute-done.11.recv_ref = f32[64,256]{1,0:T(8,128)S(1)} collective-permute-done((f32[64,256]{1,0:T(8,128)S(1)}, f32[64,256]{1,0:T(8,128)S(1)}, u32[]{:S(2)}, u32[]{:S(2)}) %collective-permute-start.11) | collective-permute-done | bytes 65568 | tf_op jit(solution)/shard_map/ppermute | solution.py:413
  40.1 3.6 %collective-permute-start.12 = (f32[64,256]{1,0:T(8,128)S(1)}, f32[64,256]{1,0:T(8,128)S(1)}, u32[]{:S(2)}, u32[]{:S(2)}) collective-permute-start(f32[64,256]{1,0:T(8,128)S(1)} %shard_map.95.own_ref), channel_id=1, source_target_pairs={{0,12},{1,13},{2,14},{3,15},{4,8},{5,9},{6,10},{7,11},{8,4},{9,5},... | collective-permute-start | bytes 196616 | tf_op jit(solution)/shard_map/ppermute | solution.py:413
  43.7 2.6 %collective-permute-done.12.recv_ref = f32[64,256]{1,0:T(8,128)S(1)} collective-permute-done((f32[64,256]{1,0:T(8,128)S(1)}, f32[64,256]{1,0:T(8,128)S(1)}, u32[]{:S(2)}, u32[]{:S(2)}) %collective-permute-start.12) | collective-permute-done | bytes 65568 | tf_op jit(solution)/shard_map/ppermute | solution.py:413
  46.4 1.6 %collective-permute-start.13 = (f32[128,128]{1,0:T(8,128)S(1)}, f32[128,128]{1,0:T(8,128)S(1)}, u32[]{:S(2)}, u32[]{:S(2)}) collective-permute-start(f32[128,128]{1,0:T(8,128)S(1)} %get-tuple-element.53), channel_id=1, source_target_pairs={{0,2},{1,3},{2,0},{3,1},{4,6},{5,7},{6,4},{7,5},{8,10},{9,11},{10,... | collective-permute-start | bytes 196616 | tf_op jit(solution)/shard_map/ppermute | solution.py:413
  48.0 2.0 %collective-permute-start.14 = (f32[128,128]{1,0:T(8,128)S(1)}, f32[128,128]{1,0:T(8,128)S(1)}, u32[]{:S(2)}, u32[]{:S(2)}) collective-permute-start(f32[128,128]{1,0:T(8,128)S(1)} %get-tuple-element.54), channel_id=1, source_target_pairs={{0,4},{1,5},{2,6},{3,7},{4,0},{5,1},{6,2},{7,3},{8,12},{9,13},{10,... | collective-permute-start | bytes 196616 | tf_op jit(solution)/shard_map/ppermute | solution.py:413
  50.8 1.9 %collective-permute-done.14.refs_2_ = f32[128,128]{1,0:T(8,128)S(1)} collective-permute-done((f32[128,128]{1,0:T(8,128)S(1)}, f32[128,128]{1,0:T(8,128)S(1)}, u32[]{:S(2)}, u32[]{:S(2)}) %collective-permute-start.14) | collective-permute-done | bytes 65568 | tf_op jit(solution)/shard_map/ppermute | solution.py:413
  52.7 2.5 %collective-permute-done.15.refs_3_ = f32[128,128]{1,0:T(8,128)S(1)} collective-permute-done((f32[128,128]{1,0:T(8,128)S(1)}, f32[128,128]{1,0:T(8,128)S(1)}, u32[]{:S(2)}, u32[]{:S(2)}) %collective-permute-start.15) | collective-permute-done | bytes 65568 | tf_op jit(solution)/shard_map/ppermute | solution.py:413
  (38 shorter events, 5.7 us)
Async XLA Ops:
  0.6 10.6 %copy-start = (bf16[4,1024,128]{2,1,0:T(8,128)(2,1)S(1)}, bf16[4,1024,128]{2,1,0:T(8,128)(2,1)}, u32[]{:S(2)}) copy-start(bf16[4,1024,128]{2,1,0:T(8,128)(2,1)} %param.9) | copy-start | bytes 3145732
  1.9 10.5 %collective-permute-start = (bf16[512,128]{1,0:T(8,128)(2,1)S(1)}, bf16[512,128]{1,0:T(8,128)(2,1)S(1)}, u32[]{:S(2)}, u32[]{:S(2)}) collective-permute-start(bf16[512,128]{1,0:T(8,128)(2,1)S(1)} %get-tuple-element.61), channel_id=1, source_target_pairs={{0,2},{1,3},{2,0},{3,1},{4,6},{5,7},{6,4},{7,5},{8,10},{9,11},{10,... | collective-permute-start | bytes 393224 | tf_op jit(solution)/shard_map/ppermute | solution.py:413
  4.9 7.5 %collective-permute-start.1 = (bf16[512,128]{1,0:T(8,128)(2,1)S(1)}, bf16[512,128]{1,0:T(8,128)(2,1)S(1)}, u32[]{:S(2)}, u32[]{:S(2)}) collective-permute-start(bf16[512,128]{1,0:T(8,128)(2,1)S(1)} %get-tuple-element.63), channel_id=1, source_target_pairs={{0,4},{1,5},{2,6},{3,7},{4,0},{5,1},{6,2},{7,3},{8,12},{9,13},{10,... | collective-permute-start | bytes 393224 | tf_op jit(solution)/shard_map/ppermute | solution.py:413
  6.5 7.4 %collective-permute-start.2 = (bf16[512,128]{1,0:T(8,128)(2,1)S(1)}, bf16[512,128]{1,0:T(8,128)(2,1)S(1)}, u32[]{:S(2)}, u32[]{:S(2)}) collective-permute-start(bf16[512,128]{1,0:T(8,128)(2,1)S(1)} %get-tuple-element.60), channel_id=1, source_target_pairs={{0,6},{1,7},{2,4},{3,5},{4,2},{5,3},{6,0},{7,1},{8,14},{9,15},{10,... | collective-permute-start | bytes 393224 | tf_op jit(solution)/shard_map/ppermute | solution.py:413
  7.7 9.1 %collective-permute-start.3 = (bf16[512,128]{1,0:T(8,128)(2,1)S(1)}, bf16[512,128]{1,0:T(8,128)(2,1)S(1)}, u32[]{:S(2)}, u32[]{:S(2)}) collective-permute-start(bf16[512,128]{1,0:T(8,128)(2,1)S(1)} %get-tuple-element.57), channel_id=1, source_target_pairs={{0,2},{1,3},{2,0},{3,1},{4,6},{5,7},{6,4},{7,5},{8,10},{9,11},{10,... | collective-permute-start | bytes 393224 | tf_op jit(solution)/shard_map/ppermute | solution.py:413
  9.6 7.3 %collective-permute-start.4 = (bf16[512,128]{1,0:T(8,128)(2,1)S(1)}, bf16[512,128]{1,0:T(8,128)(2,1)S(1)}, u32[]{:S(2)}, u32[]{:S(2)}) collective-permute-start(bf16[512,128]{1,0:T(8,128)(2,1)S(1)} %get-tuple-element.59), channel_id=1, source_target_pairs={{0,4},{1,5},{2,6},{3,7},{4,0},{5,1},{6,2},{7,3},{8,12},{9,13},{10,... | collective-permute-start | bytes 393224 | tf_op jit(solution)/shard_map/ppermute | solution.py:413
  12.4 5.9 %collective-permute-start.5 = (bf16[512,128]{1,0:T(8,128)(2,1)S(1)}, bf16[512,128]{1,0:T(8,128)(2,1)S(1)}, u32[]{:S(2)}, u32[]{:S(2)}) collective-permute-start(bf16[512,128]{1,0:T(8,128)(2,1)S(1)} %get-tuple-element.56), channel_id=1, source_target_pairs={{0,6},{1,7},{2,4},{3,5},{4,2},{5,3},{6,0},{7,1},{8,14},{9,15},{10,... | collective-permute-start | bytes 393224 | tf_op jit(solution)/shard_map/ppermute | solution.py:413
  16.1 2.2 %collective-permute-start.6 = (bf16[512,128]{1,0:T(8,128)(2,1)S(1)}, bf16[512,128]{1,0:T(8,128)(2,1)S(1)}, u32[]{:S(2)}, u32[]{:S(2)}) collective-permute-start(bf16[512,128]{1,0:T(8,128)(2,1)S(1)} %get-tuple-element.36), channel_id=1, source_target_pairs={{0,1},{1,0},{2,3},{3,2},{4,5},{5,4},{6,7},{7,6},{8,9},{9,8},{10,11... | collective-permute-start | bytes 393224 | tf_op jit(solution)/shard_map/ppermute | solution.py:413
  18.3 7.0 %collective-permute-start.7 = (bf16[512,128]{1,0:T(8,128)(2,1)S(1)}, bf16[512,128]{1,0:T(8,128)(2,1)S(1)}, u32[]{:S(2)}, u32[]{:S(2)}) collective-permute-start(bf16[512,128]{1,0:T(8,128)(2,1)S(1)} %add_convert_fusion), channel_id=1, source_target_pairs={{0,12},{1,13},{2,14},{3,15},{4,8},{5,9},{6,10},{7,11},{8,4},{9,5},... | collective-permute-start | bytes 393224 | tf_op jit(solution)/shard_map/ppermute | solution.py:413
  25.7 1.4 %collective-permute-start.8 = (bf16[512,128]{1,0:T(8,128)(2,1)S(1)}, bf16[512,128]{1,0:T(8,128)(2,1)S(1)}, u32[]{:S(2)}, u32[]{:S(2)}) collective-permute-start(bf16[512,128]{1,0:T(8,128)(2,1)S(1)} %multiply_convert_fusion.refs_4_), channel_id=1, source_target_pairs={{0,1},{1,0},{2,3},{3,2},{4,5},{5,4},{6,7},{7,6},{8,9},{9,8},{10,11... | collective-permute-start | bytes 393224 | tf_op jit(solution)/shard_map/ppermute | solution.py:413
  28.6 5.3 %copy-start.1 = (bf16[8,4,8,128]{3,2,1,0:T(8,128)(2,1)S(1)}, bf16[8,4,8,128]{3,2,1,0:T(8,128)(2,1)}, u32[]{:S(2)}) copy-start(bf16[8,4,8,128]{3,2,1,0:T(8,128)(2,1)} %refs_13_.1) | copy-start | bytes 196612
  28.6 5.3 %copy-start.2 = (s32[8,4,32]{2,1,0:T(4,128)S(1)}, s32[8,4,32]{2,1,0:T(4,128)}, u32[]{:S(2)}) copy-start(s32[8,4,32]{2,1,0:T(4,128)} %refs_14_.1) | copy-start | bytes 12292
  28.7 5.3 %copy-start.3 = (s32[4,64]{1,0:T(4,128)S(1)}, s32[4,64]{1,0:T(4,128)}, u32[]{:S(2)}) copy-start(s32[4,64]{1,0:T(4,128)} %refs_4_.1) | copy-start | bytes 3076
  28.7 5.3 %copy-start.4 = (s32[8]{0:T(128)S(1)}, s32[8]{0:T(128)}, u32[]{:S(2)}) copy-start(s32[8]{0:T(128)} %refs_3_.1) | copy-start | bytes 100
  28.7 1.6 %collective-permute-start.9 = (bf16[528,256]{1,0:T(8,128)(2,1)S(1)}, bf16[528,256]{1,0:T(8,128)(2,1)S(1)}, u32[]{:S(2)}, u32[]{:S(2)}) collective-permute-start(bf16[528,256]{1,0:T(8,128)(2,1)S(1)} %get-tuple-element.43), channel_id=1, source_target_pairs={{0,1},{1,0},{2,3},{3,2},{4,5},{5,4},{6,7},{7,6},{8,9},{9,8},{10,11... | collective-permute-start | bytes 811016 | tf_op jit(solution)/shard_map/ppermute | solution.py:413
  30.3 7.7 %collective-permute-start.10 = (bf16[272,256]{1,0:T(8,128)(2,1)S(1)}, bf16[272,256]{1,0:T(8,128)(2,1)S(1)}, u32[]{:S(2)}, u32[]{:S(2)}) collective-permute-start(bf16[272,256]{1,0:T(8,128)(2,1)S(1)} %get-tuple-element.46), channel_id=1, source_target_pairs={{0,12},{1,13},{2,14},{3,15},{4,8},{5,9},{6,10},{7,11},{8,4},{9,5},... | collective-permute-start | bytes 417800 | tf_op jit(solution)/shard_map/ppermute | solution.py:413
  38.6 1.3 %collective-permute-start.11 = (f32[64,256]{1,0:T(8,128)S(1)}, f32[64,256]{1,0:T(8,128)S(1)}, u32[]{:S(2)}, u32[]{:S(2)}) collective-permute-start(f32[64,256]{1,0:T(8,128)S(1)} %get-tuple-element.50.own_ref), channel_id=1, source_target_pairs={{0,1},{1,0},{2,3},{3,2},{4,5},{5,4},{6,7},{7,6},{8,9},{9,8},{10,11... | collective-permute-start | bytes 196616 | tf_op jit(solution)/shard_map/ppermute | solution.py:413
  40.1 6.2 %collective-permute-start.12 = (f32[64,256]{1,0:T(8,128)S(1)}, f32[64,256]{1,0:T(8,128)S(1)}, u32[]{:S(2)}, u32[]{:S(2)}) collective-permute-start(f32[64,256]{1,0:T(8,128)S(1)} %shard_map.95.own_ref), channel_id=1, source_target_pairs={{0,12},{1,13},{2,14},{3,15},{4,8},{5,9},{6,10},{7,11},{8,4},{9,5},... | collective-permute-start | bytes 196616 | tf_op jit(solution)/shard_map/ppermute | solution.py:413
  46.4 4.3 %collective-permute-start.13 = (f32[128,128]{1,0:T(8,128)S(1)}, f32[128,128]{1,0:T(8,128)S(1)}, u32[]{:S(2)}, u32[]{:S(2)}) collective-permute-start(f32[128,128]{1,0:T(8,128)S(1)} %get-tuple-element.53), channel_id=1, source_target_pairs={{0,2},{1,3},{2,0},{3,1},{4,6},{5,7},{6,4},{7,5},{8,10},{9,11},{10,... | collective-permute-start | bytes 196616 | tf_op jit(solution)/shard_map/ppermute | solution.py:413
  48.0 4.7 %collective-permute-start.14 = (f32[128,128]{1,0:T(8,128)S(1)}, f32[128,128]{1,0:T(8,128)S(1)}, u32[]{:S(2)}, u32[]{:S(2)}) collective-permute-start(f32[128,128]{1,0:T(8,128)S(1)} %get-tuple-element.54), channel_id=1, source_target_pairs={{0,4},{1,5},{2,6},{3,7},{4,0},{5,1},{6,2},{7,3},{8,12},{9,13},{10,... | collective-permute-start | bytes 196616 | tf_op jit(solution)/shard_map/ppermute | solution.py:413
  50.0 5.2 %collective-permute-start.15 = (f32[128,128]{1,0:T(8,128)S(1)}, f32[128,128]{1,0:T(8,128)S(1)}, u32[]{:S(2)}, u32[]{:S(2)}) collective-permute-start(f32[128,128]{1,0:T(8,128)S(1)} %get-tuple-element.55), channel_id=1, source_target_pairs={{0,6},{1,7},{2,4},{3,5},{4,2},{5,3},{6,0},{7,1},{8,14},{9,15},{10,... | collective-permute-start | bytes 196616 | tf_op jit(solution)/shard_map/ppermute | solution.py:413

commit v5 on v4

--- a/solution.py
+++ b/solution.py
@@ -120,7 +120,16 @@
 
 
 def first_kernel(
-    base_ref, order, key_ref, cent_ref, sums_ref, unit_ref, cents_ref, raised_ref, weight_ref
+    base_ref,
+    order,
+    key_ref,
+    cent_ref,
+    sums_ref,
+    keep_weight_ref,
+    unit_ref,
+    cents_ref,
+    raised_ref,
+    weight_ref,
 ):
     per_owner = cent_ref.shape[1]
     for at, mask in enumerate(order):
@@ -128,31 +137,22 @@
             F32
         )
     unit_ref[...] = to_unit(cents_ref[...]).astype(BF16)
+    pass_chunk(key_ref, unit_ref, None, sums_ref, keep_weight_ref, raised_ref, weight_ref)
+
+
+def pass_chunk(key_ref, unit_ref, before_ref, sums_ref, keep_weight_ref, raised_ref, weight_ref):
     keys = key_ref[...]
+    half = sums_ref.shape[0]
     inverse = 1.0 / fill_raised(unit_ref, to_unit(keys).astype(BF16), raised_ref, 0, 0)
-    fill_weights(raised_ref, inverse, weight_ref, weight_ref.shape[0], 0, 0, 0, None)
-    product(sums_ref, weight_ref, keys)
-
-
-def rest_kernel(count, *refs):
-    key_refs, (unit_ref, sums_ref, send_ref, keep_weight_ref, raised_ref, weight_ref) = (
-        refs[:count],
-        refs[count:],
-    )
-    half = send_ref.shape[0]
-    first = 0
-    for key_ref in key_refs:
-        unit_keys = to_unit(key_ref[...]).astype(BF16)
-        inverse = 1.0 / fill_raised(unit_ref, unit_keys, raised_ref, 0, 0)
-        fill_weights(raised_ref, inverse, weight_ref, half, half, first, 0, None)
-        fill_weights(raised_ref, inverse, keep_weight_ref, half, 0, first, 0, None)
-        first += unit_keys.shape[0]
-    product(send_ref, weight_ref, joined_rows(key_refs), sums_ref, half)
+    fill_weights(raised_ref, inverse, weight_ref, half, half, 0, 0, None)
+    fill_weights(raised_ref, inverse, keep_weight_ref, half, 0, 0, 0, None)
+    product(sums_ref, weight_ref, keys, before_ref)
 
 
 def keep_kernel(count, *refs):
-    key_refs, (sums_ref, weight_ref, keep_ref) = refs[:count], refs[count:]
-    product(keep_ref, weight_ref, joined_rows(key_refs), sums_ref, 0)
+    key_refs, weight_refs, keep_ref = refs[:count], refs[count : 2 * count], refs[-1]
+    weights = jnp.concatenate([ref[...] for ref in weight_refs], axis=1)
+    keep_ref[...] = jnp.dot(weights, joined_rows(key_refs), preferred_element_type=F32)
 
 
 def joined_rows(refs):
@@ -249,8 +249,13 @@
 
 def packed_state(peak, weight_sum, weighted):
     rows, dim = weighted.shape
-    lane = lax.broadcasted_iota(jnp.int32, (rows, dim), 1)
-    return jnp.concatenate([weighted, jnp.where(lane < dim // 2, peak, weight_sum)], axis=1)
+    lines = [
+        jnp.concatenate(
+            [jnp.broadcast_to(column, (rows, dim)), jnp.zeros((dim - rows, dim), F32)], axis=0
+        ).T[0:1, :]
+        for column in (peak, weight_sum)
+    ]
+    return jnp.concatenate([weighted, *lines, jnp.zeros((6, dim), F32)], axis=0)
 
 
 def softmax_part(scores, usable, values):
@@ -271,8 +276,13 @@
 
 
 def unpacked_state(state):
-    dim = state.shape[1] // 2
-    return state[:, dim : dim + 1], state[:, dim + dim // 2 : dim + dim // 2 + 1], state[:, :dim]
+    dim = state.shape[1]
+    rows = state.shape[0] - 8
+    columns = [
+        jnp.broadcast_to(state[rows + at : rows + at + 1, :], (dim, dim)).T[:rows, :]
+        for at in range(2)
+    ]
+    return columns[0], columns[1], state[:rows, :]
 
 
 def exact_kernel(count, head_masks, owned_by, per_owner, *refs):
@@ -353,27 +363,29 @@
     out_ref[...] = packed_state(*joined(unpacked_state(former), unpacked_state(latter)))
 
 
-def last_merge_kernel(flip_ref, head_ref, own_ref, recv_ref, cent_ref, *pack_refs):
+def last_merge_kernel(flip_ref, head_ref, own_ref, recv_ref, cent_ref, attended_ref, *pack_refs):
     former, latter = in_order(flip_ref[0] != 0, own_ref, recv_ref)
     _, weight_sum, weighted = joined(unpacked_state(former), unpacked_state(latter))
-    attended = weighted / weight_sum
+    attended = (weighted / weight_sum).astype(BF16)
+    attended_ref[...] = attended
+    rows = attended.shape[0]
+    for step, pack_ref in enumerate(pack_refs, 1):
+        pack_ref[:rows, :] = attended
+        pack_ref[rows:, :] = cent_ref[head_ref[0] ^ step].astype(BF16)
+
+
+def spread_kernel(head_ref, own_cent_ref, attended_ref, *refs):
+    pack_refs, (cent_ref, out_ref) = refs[:-2], refs[-2:]
     own = head_ref[0]
-    per_owner = cent_ref.shape[1]
-    for step, pack_ref in enumerate(pack_refs):
-        pack_ref[:per_owner, :] = cent_ref[own ^ step]
-        pack_ref[per_owner:, :] = attended
-
-
-def spread_kernel(scalar_ref, *refs):
-    pack_refs, (cent_ref, out_ref) = refs[:-2], refs[-2:]
-    own = scalar_ref[0]
-    per_owner = cent_ref.shape[1]
-    requests, _, group, dim = out_ref.shape
-    for step, pack_ref in enumerate(pack_refs):
-        cent_ref[own ^ step] = pack_ref[:per_owner, :]
+    requests, _, group, _ = out_ref.shape
+    rows = requests * group
+    cent_ref[own] = own_cent_ref[own]
+    for step, pack_ref in enumerate((attended_ref, *pack_refs)):
+        attended = pack_ref[:rows, :].astype(F32)
+        if step:
+            cent_ref[own ^ step] = pack_ref[rows:, :].astype(F32)
         for r in range(requests):
-            at = per_owner + r * group
-            out_ref[r, own ^ step] = pack_ref[at : at + group, :].astype(BF16)
+            out_ref[r, own ^ step] = attended[r * group : (r + 1) * group, :].astype(BF16)
 
 
 def body(
@@ -424,40 +436,41 @@
     scalar_base = base.reshape(1)
 
     pass_flops = 4 * tok_dev * clusters * dim
-    sums, unit_cents = call(
+    chunk_scratch = [pltpu.VMEM((clusters, tok_dev), F32), pltpu.VMEM((half, tok_dev), BF16)]
+    sums, keep_weights, unit_cents = call(
         lambda base_ref, *refs: first_kernel(base_ref, order, *refs),
-        [shape((clusters, dim), F32), shape((clusters, dim), BF16)],
+        [
+            shape((half, dim), F32),
+            shape((half, tok_dev), BF16),
+            shape((clusters, dim), BF16),
+        ],
         [scalar_base, keys[0], blocks],
-        [
-            pltpu.VMEM((clusters, dim), F32),
-            pltpu.VMEM((clusters, tok_dev), F32),
-            pltpu.VMEM((clusters, tok_dev), BF16),
-        ],
+        [pltpu.VMEM((clusters, dim), F32), *chunk_scratch],
         pass_flops,
         scalars=1,
     )
     values = [pick(value_cache, head)]
     values += [over(pick(value_cache, head ^ s), head_masks[s]) for s in range(1, heads)]
 
-    send, keep_weights = call(
-        functools.partial(rest_kernel, heads - 1),
-        [shape((half, dim), BF16), shape((half, (heads - 1) * tok_dev), BF16)],
-        [*keys[1:], unit_cents, sums],
-        [
-            pltpu.VMEM((clusters, tok_dev), F32),
-            pltpu.VMEM((half, (heads - 1) * tok_dev), BF16),
-        ],
-        pass_flops * (heads - 1),
-    )
+    keep_weights = [keep_weights]
+    for step in range(1, heads):
+        sums, kept = call(
+            pass_chunk,
+            [shape((half, dim), F32 if step < heads - 1 else BF16), shape((half, tok_dev), BF16)],
+            [keys[step], unit_cents, sums],
+            chunk_scratch,
+            pass_flops,
+        )
+        keep_weights.append(kept)
+    send = sums
     (keep,) = call(
-        functools.partial(keep_kernel, heads - 1),
+        functools.partial(keep_kernel, heads),
         [shape((half, dim), F32)],
-        [*keys[1:], sums, keep_weights],
+        [*keys, *keep_weights],
         (),
-        pass_flops * (heads - 1) // 4,
-    )
-
-    keep, values[1], values[2], values[3] = lax.optimization_barrier((keep, values[1], values[2], values[3]))
+        pass_flops * heads // 4,
+    )
+    keep, values[1], values[2] = lax.optimization_barrier((keep, values[1], values[2]))
     for level in range(levels - 1):
         total = keep + over(send, rank_basis[level]).astype(F32)
         if level < levels - 2:
@@ -498,7 +511,7 @@
 
     exact, own_queries, usable = call(
         functools.partial(exact_kernel, heads, head_masks, head_masks, per_owner),
-        [shape((rows, 2 * dim), F32), shape((rows, dim), F32), shape((rows, owned), F32)],
+        [shape((rows + 8, dim), F32), shape((rows, dim), F32), shape((rows, owned), F32)],
         [
             head.reshape(1),
             index.reshape(1),
@@ -530,7 +543,7 @@
     recv = over(send, rank_basis[levels - 1])
     state, centroids = call(
         summary_kernel,
-        [shape((rows, 2 * dim), F32), shape((owned, dim), F32)],
+        [shape((rows + 8, dim), F32), shape((owned, dim), F32)],
         [keep, keep_mass, recv, own_queries, usable, exact],
         (),
         4 * rows * owned * dim,
@@ -539,28 +552,23 @@
         flip = ((rank >> level) & 1).reshape(1)
         (state,) = call(
             merge_kernel,
-            [shape((rows, 2 * dim), F32)],
+            [shape((rows + 8, dim), F32)],
             [flip, state, over(state, rank_basis[level])],
             scalars=1,
         )
     flip = ((rank >> (levels - 1)) & 1).reshape(1)
-    packs = call(
+    centroids = centroids.reshape(heads, per_owner, dim)
+    attended, *packs = call(
         last_merge_kernel,
-        [shape((per_owner + rows, dim), F32)] * heads,
-        [
-            flip,
-            head.reshape(1),
-            state,
-            over(state, rank_basis[levels - 1]),
-            centroids.reshape(heads, per_owner, dim),
-        ],
+        [shape((rows, dim), BF16)] + [shape((rows + per_owner, dim), BF16)] * (heads - 1),
+        [flip, head.reshape(1), state, over(state, rank_basis[levels - 1]), centroids],
         scalars=2,
     )
-    packs = [packs[0]] + [over(packs[s], head_masks[s]) for s in range(1, heads)]
+    packs = [over(pack, head_masks[step]) for step, pack in enumerate(packs, 1)]
     return call(
         spread_kernel,
         [shape((heads, per_owner, dim), F32), shape(queries.shape, BF16)],
-        [head.reshape(1), *packs],
+        [head.reshape(1), centroids, attended, *packs],
         scalars=1,
     )
 

time: 56 us -> 54 us (0.964)
  starting transfers between devices: 23.1 us -> 20.5 us
  Pallas kernels: 10.5 us -> 11.3 us
    ppermute x16, starting transfers between devices: 23.1 us -> 20.5 us  [over(): return lax.ppermute(array, 'ctx', [(i, i ^ bit) for i in range(devices)])]
    pallas_call x12 -> x14, Pallas kernels: 10.5 us -> 11.3 us  [call(): pl.pallas_call(kernel, out_shape=tuple(outs), in_specs=in_specs, out_spec...]
  transfers between devices with their start and end apart: 16 -> 16, of which waited for: 12 -> 10; matrix products, arithmetic and copies ran while one was open for 2% -> 3% of each run, Pallas kernels for 13% -> 15%
where the time goes in v5:
time: 54 us; the launch traced here: 53.9 us
  starting transfers between devices  20.5 us (38%)
  waiting for transfers between devices  18.4 us (34%)
  Pallas kernels  11.3 us (21%)
  local copies, waits for them, and re-layouts  2.41 us (4%)
  between operations  0.91 us (2%)
    ppermute x16, starting transfers between devices, over(): return lax.ppermute(array, 'ctx', [(i, i ^ bit) for i in range(devices)])  20.5 us
    ppermute x16, waiting for transfers between devices, over(): return lax.ppermute(array, 'ctx', [(i, i ^ bit) for i in range(devices)])  18.4 us
    pallas_call x14, Pallas kernels, call(): pl.pallas_call(kernel, out_shape=tuple(outs), in_specs=in_specs, out_spec...  11.3 us
    squeeze x2, local copies, waits for them, and re-layouts, pick(): return lax.dynamic_index_in_dim(array, at, axis, keepdims=False)  2.35 us
  transfers between devices with their start and end apart: 16, of which 10 were waited for; matrix products, arithmetic and copies ran while one was open for 3% of the time, Pallas kernels for 15%

profile of v5, /device:TPU:0, one launch (start us, length us, event | category | flops | bytes accessed | tf_op | source)
XLA Modules:
  0.0 53.9 jit_solution(5701020813226425812)
XLA Ops:
  0.7 1.2 %dynamic-slice_bitcast_fusion.4 = (bf16[512,128]{1,0:T(8,128)(2,1)S(1)}, bf16[512,128]{1,0:T(8,128)(2,1)S(1)}, bf16[512,128]{1,0:T(8,128)(2,1)S(1)}, bf16[512,128]{1,0:T(8,128)(2,1)S(1)}) fusion(bf16[4,512,128]{2,1,0:T(8,128)(2,1)} %param.7, s32[]{:T(128)S(6)} %select_n.22, s32[]{:T(128)S(6)} %select_n.20, s32[]{:T(128)S(6)} %select_n.19, s32[]{:T(128)S(6)} %select_n.21), kind=kLoop, calls=%fused_computation.9 | loop fusion | bytes 1048592 | tf_op jit(solution)/shard_map/jit(dynamic_index_in_dim)/squeeze | solution.py:428
  1.9 3.0 %collective-permute-start = (bf16[512,128]{1,0:T(8,128)(2,1)S(1)}, bf16[512,128]{1,0:T(8,128)(2,1)S(1)}, u32[]{:S(2)}, u32[]{:S(2)}) collective-permute-start(bf16[512,128]{1,0:T(8,128)(2,1)S(1)} %get-tuple-element.69), channel_id=1, source_target_pairs={{0,2},{1,3},{2,0},{3,1},{4,6},{5,7},{6,4},{7,5},{8,10},{9,11},{10,... | collective-permute-start | bytes 393224 | tf_op jit(solution)/shard_map/ppermute | solution.py:425
  4.9 1.6 %collective-permute-start.1 = (bf16[512,128]{1,0:T(8,128)(2,1)S(1)}, bf16[512,128]{1,0:T(8,128)(2,1)S(1)}, u32[]{:S(2)}, u32[]{:S(2)}) collective-permute-start(bf16[512,128]{1,0:T(8,128)(2,1)S(1)} %get-tuple-element.71), channel_id=1, source_target_pairs={{0,4},{1,5},{2,6},{3,7},{4,0},{5,1},{6,2},{7,3},{8,12},{9,13},{10,... | collective-permute-start | bytes 393224 | tf_op jit(solution)/shard_map/ppermute | solution.py:425
  6.5 1.1 %dynamic-slice_bitcast_fusion = (bf16[512,128]{1,0:T(8,128)(2,1)S(1)}, bf16[512,128]{1,0:T(8,128)(2,1)S(1)}, bf16[512,128]{1,0:T(8,128)(2,1)S(1)}, bf16[512,128]{1,0:T(8,128)(2,1)S(1)}) fusion(bf16[4,512,128]{2,1,0:T(8,128)(2,1)} %param.8, s32[]{:T(128)S(6)} %select_n.22, s32[]{:T(128)S(6)} %select_n.20, s32[]{:T(128)S(6)} %select_n.19, s32[]{:T(128)S(6)} %select_n.21), kind=kLoop, calls=%fused_computation.5 | loop fusion | bytes 1048592 | tf_op jit(solution)/shard_map/jit(dynamic_index_in_dim)/squeeze | solution.py:428
  7.7 2.0 %collective-permute-start.3 = (bf16[512,128]{1,0:T(8,128)(2,1)S(1)}, bf16[512,128]{1,0:T(8,128)(2,1)S(1)}, u32[]{:S(2)}, u32[]{:S(2)}) collective-permute-start(bf16[512,128]{1,0:T(8,128)(2,1)S(1)} %get-tuple-element.65), channel_id=1, source_target_pairs={{0,2},{1,3},{2,0},{3,1},{4,6},{5,7},{6,4},{7,5},{8,10},{9,11},{10,... | collective-permute-start | bytes 393224 | tf_op jit(solution)/shard_map/ppermute | solution.py:425
  9.6 1.6 %collective-permute-start.4 = (bf16[512,128]{1,0:T(8,128)(2,1)S(1)}, bf16[512,128]{1,0:T(8,128)(2,1)S(1)}, u32[]{:S(2)}, u32[]{:S(2)}) collective-permute-start(bf16[512,128]{1,0:T(8,128)(2,1)S(1)} %get-tuple-element.67), channel_id=1, source_target_pairs={{0,4},{1,5},{2,6},{3,7},{4,0},{5,1},{6,2},{7,3},{8,12},{9,13},{10,... | collective-permute-start | bytes 393224 | tf_op jit(solution)/shard_map/ppermute | solution.py:425
  11.2 1.0 %shard_map.86 = (f32[512,128]{1,0:T(8,128)S(1)}, bf16[512,512]{1,0:T(8,128)(2,1)S(1)}, bf16[1024,128]{1,0:T(8,128)(2,1)S(1)}) custom-call(s32[1]{0:T(128)} %bitcast.6.base_ref.refs_2_, bf16[512,128]{1,0:T(8,128)(2,1)S(1)} %get-tuple-element.70.refs_0_.refs_5_, bf16[16,64,128]{2,1,0:T(8,128)(2,1)S(1)} %bitcast.25), custom_call_target="tpu_custom_call" | custom-call | flops 268435456 | bytes 1441796 | tf_op jit(solution)/shard_map/pallas_call | solution.py:64
  12.3 1.0 %shard_map.87 = (f32[512,128]{1,0:T(8,128)S(1)}, bf16[512,512]{1,0:T(8,128)(2,1)S(1)}) custom-call(bf16[512,128]{1,0:T(8,128)(2,1)S(1)} %collective-permute-done.key_ref.refs_1_.refs_6_, bf16[1024,128]{1,0:T(8,128)(2,1)S(1)} %get-tuple-element.34.unit_ref, f32[512,128]{1,0:T(8,128)S(1)} %get-tuple-element.35.before_ref), custom_call_target="tpu_custom_call" | custom-call | flops 268435456 | bytes 1441792 | tf_op jit(solution)/shard_map/pallas_call | solution.py:64
  13.3 1.0 %shard_map.88 = (f32[512,128]{1,0:T(8,128)S(1)}, bf16[512,512]{1,0:T(8,128)(2,1)S(1)}) custom-call(bf16[512,128]{1,0:T(8,128)(2,1)S(1)} %collective-permute-done.1.key_ref.refs_2_.refs_7_, bf16[1024,128]{1,0:T(8,128)(2,1)S(1)} %get-tuple-element.34.unit_ref, f32[512,128]{1,0:T(8,128)S(1)} %get-tuple-element.37.before_ref), custom_call_target="tpu_custom_call" | custom-call | flops 268435456 | bytes 1441792 | tf_op jit(solution)/shard_map/pallas_call | solution.py:64
  14.3 1.0 %shard_map.89 = (bf16[512,128]{1,0:T(8,128)(2,1)S(1)}, bf16[512,512]{1,0:T(8,128)(2,1)S(1)}) custom-call(bf16[512,128]{1,0:T(8,128)(2,1)S(1)} %collective-permute-done.2.key_ref.refs_3_.refs_8_, bf16[1024,128]{1,0:T(8,128)(2,1)S(1)} %get-tuple-element.34.unit_ref, f32[512,128]{1,0:T(8,128)S(1)} %get-tuple-element.39.before_ref), custom_call_target="tpu_custom_call" | custom-call | flops 268435456 | bytes 1310720 | tf_op jit(solution)/shard_map/pallas_call | solution.py:64
  16.8 3.4 %collective-permute-start.7 = (bf16[512,128]{1,0:T(8,128)(2,1)S(1)}, bf16[512,128]{1,0:T(8,128)(2,1)S(1)}, u32[]{:S(2)}, u32[]{:S(2)}) collective-permute-start(bf16[512,128]{1,0:T(8,128)(2,1)S(1)} %add_convert_fusion), channel_id=1, source_target_pairs={{0,12},{1,13},{2,14},{3,15},{4,8},{5,9},{6,10},{7,11},{8,4},{9,5},... | collective-permute-start | bytes 393224 | tf_op jit(solution)/shard_map/ppermute | solution.py:425
  20.7 4.3 %collective-permute-done.7 = bf16[512,128]{1,0:T(8,128)(2,1)S(1)} collective-permute-done((bf16[512,128]{1,0:T(8,128)(2,1)S(1)}, bf16[512,128]{1,0:T(8,128)(2,1)S(1)}, u32[]{:S(2)}, u32[]{:S(2)}) %collective-permute-start.7) | collective-permute-done | bytes 131104 | tf_op jit(solution)/shard_map/ppermute | solution.py:425
  25.4 1.0 %shard_map.91 = (bf16[2048,128]{1,0:T(8,128)(2,1)S(1)}, bf16[512,2048]{1,0:T(8,128)(2,1)S(1)}, f32[8,2048]{1,0:T(8,128)S(1)}) custom-call(bf16[512,128]{1,0:T(8,128)(2,1)S(1)} %get-tuple-element.70.refs_0_.refs_5_, bf16[512,128]{1,0:T(8,128)(2,1)S(1)} %collective-permute-done.key_ref.refs_1_.refs_6_, ...), custom_call_target="tpu_custom_call" | custom-call | flops 268435456 | bytes 3342336 | tf_op jit(solution)/shard_map/pallas_call | solution.py:64
  26.5 1.4 %collective-permute-done.5.refs_7_.refs_12_ = bf16[512,128]{1,0:T(8,128)(2,1)S(1)} collective-permute-done((bf16[512,128]{1,0:T(8,128)(2,1)S(1)}, bf16[512,128]{1,0:T(8,128)(2,1)S(1)}, u32[]{:S(2)}, u32[]{:S(2)}) %collective-permute-start.5) | collective-permute-done | bytes 131104 | tf_op jit(solution)/shard_map/ppermute | solution.py:425
  27.8 1.5 %shard_map.92 = (bf16[528,256]{1,0:T(8,128)(2,1)S(1)}, f32[8,2048]{1,0:T(8,128)S(1)}) custom-call(bf16[512,128]{1,0:T(8,128)(2,1)S(1)} %get-tuple-element.70.refs_0_.refs_5_, bf16[512,128]{1,0:T(8,128)(2,1)S(1)} %collective-permute-done.key_ref.refs_1_.refs_6_, bf16[512,128]{1,0:T(8,128)(2,1)S(1)} %collective-permute-done.1.key_ref.refs_2_.refs_7_, ...), custom_call_target="tpu_custom_call" | custom-call | flops 805306368 | bytes 2105344 | tf_op jit(solution)/shard_map/pallas_call | solution.py:64
  31.1 2.3 %collective-permute-start.10 = (bf16[272,256]{1,0:T(8,128)(2,1)S(1)}, bf16[272,256]{1,0:T(8,128)(2,1)S(1)}, u32[]{:S(2)}, u32[]{:S(2)}) collective-permute-start(bf16[272,256]{1,0:T(8,128)(2,1)S(1)} %get-tuple-element.54), channel_id=1, source_target_pairs={{0,12},{1,13},{2,14},{3,15},{4,8},{5,9},{6,10},{7,11},{8,4},{9,5},... | collective-permute-start | bytes 417800 | tf_op jit(solution)/shard_map/ppermute | solution.py:425
  33.4 1.7 %shard_map.95 = (f32[72,128]{1,0:T(8,128)S(1)}, f32[64,128]{1,0:T(8,128)S(1)}, f32[64,256]{1,0:T(8,128)S(1)}) custom-call(s32[1]{0:T(128)} %bitcast.refs_0_.head_ref, s32[1]{0:T(128)} %bitcast.11.refs_1_, s32[1]{0:T(128)} %bitcast.6.base_ref.refs_2_, s32[8]{0:T(128)S(1)} %copy-done.4, s32[4,64]{1,0:T(4,128)S(1)} %copy-done.3, ...), custom_call_target="tpu_custom_call" | custom-call | flops 67108864 | bytes 1254444 | tf_op jit(solution)/shard_map/pallas_call | solution.py:64
  35.2 3.6 %collective-permute-done.10.recv_ref = bf16[272,256]{1,0:T(8,128)(2,1)S(1)} collective-permute-done((bf16[272,256]{1,0:T(8,128)(2,1)S(1)}, bf16[272,256]{1,0:T(8,128)(2,1)S(1)}, u32[]{:S(2)}, u32[]{:S(2)}) %collective-permute-start.10) | collective-permute-done | bytes 139296 | tf_op jit(solution)/shard_map/ppermute | solution.py:425
  39.3 1.2 %collective-permute-done.11.recv_ref = f32[72,128]{1,0:T(8,128)S(1)} collective-permute-done((f32[72,128]{1,0:T(8,128)S(1)}, f32[72,128]{1,0:T(8,128)S(1)}, u32[]{:S(2)}, u32[]{:S(2)}) %collective-permute-start.11) | collective-permute-done | bytes 36896 | tf_op jit(solution)/shard_map/ppermute | solution.py:425
  40.7 2.4 %collective-permute-start.12 = (f32[72,128]{1,0:T(8,128)S(1)}, f32[72,128]{1,0:T(8,128)S(1)}, u32[]{:S(2)}, u32[]{:S(2)}) collective-permute-start(f32[72,128]{1,0:T(8,128)S(1)} %shard_map.97.own_ref), channel_id=1, source_target_pairs={{0,12},{1,13},{2,14},{3,15},{4,8},{5,9},{6,10},{7,11},{8,4},{9,5},... | collective-permute-start | bytes 110600 | tf_op jit(solution)/shard_map/ppermute | solution.py:425
  43.0 3.4 %collective-permute-done.12.recv_ref = f32[72,128]{1,0:T(8,128)S(1)} collective-permute-done((f32[72,128]{1,0:T(8,128)S(1)}, f32[72,128]{1,0:T(8,128)S(1)}, u32[]{:S(2)}, u32[]{:S(2)}) %collective-permute-start.12) | collective-permute-done | bytes 36896 | tf_op jit(solution)/shard_map/ppermute | solution.py:425
  47.4 0.9 %collective-permute-start.14 = (bf16[128,128]{1,0:T(8,128)(2,1)S(1)}, bf16[128,128]{1,0:T(8,128)(2,1)S(1)}, u32[]{:S(2)}, u32[]{:S(2)}) collective-permute-start(bf16[128,128]{1,0:T(8,128)(2,1)S(1)} %get-tuple-element.62), channel_id=1, source_target_pairs={{0,4},{1,5},{2,6},{3,7},{4,0},{5,1},{6,2},{7,3},{8,12},{9,13},{10,... | collective-permute-start | bytes 98312 | tf_op jit(solution)/shard_map/ppermute | solution.py:425
  48.4 1.8 %collective-permute-start.15 = (bf16[128,128]{1,0:T(8,128)(2,1)S(1)}, bf16[128,128]{1,0:T(8,128)(2,1)S(1)}, u32[]{:S(2)}, u32[]{:S(2)}) collective-permute-start(bf16[128,128]{1,0:T(8,128)(2,1)S(1)} %get-tuple-element.63), channel_id=1, source_target_pairs={{0,6},{1,7},{2,4},{3,5},{4,2},{5,3},{6,0},{7,1},{8,14},{9,15},{10,... | collective-permute-start | bytes 98312 | tf_op jit(solution)/shard_map/ppermute | solution.py:425
  51.4 1.8 %collective-permute-done.15.refs_2_ = bf16[128,128]{1,0:T(8,128)(2,1)S(1)} collective-permute-done((bf16[128,128]{1,0:T(8,128)(2,1)S(1)}, bf16[128,128]{1,0:T(8,128)(2,1)S(1)}, u32[]{:S(2)}, u32[]{:S(2)}) %collective-permute-start.15) | collective-permute-done | bytes 32800 | tf_op jit(solution)/shard_map/ppermute | solution.py:425
  (40 shorter events, 7.6 us)
Async XLA Ops:
  0.6 10.6 %copy-start = (bf16[4,1024,128]{2,1,0:T(8,128)(2,1)S(1)}, bf16[4,1024,128]{2,1,0:T(8,128)(2,1)}, u32[]{:S(2)}) copy-start(bf16[4,1024,128]{2,1,0:T(8,128)(2,1)} %param.9) | copy-start | bytes 3145732
  1.9 10.4 %collective-permute-start = (bf16[512,128]{1,0:T(8,128)(2,1)S(1)}, bf16[512,128]{1,0:T(8,128)(2,1)S(1)}, u32[]{:S(2)}, u32[]{:S(2)}) collective-permute-start(bf16[512,128]{1,0:T(8,128)(2,1)S(1)} %get-tuple-element.69), channel_id=1, source_target_pairs={{0,2},{1,3},{2,0},{3,1},{4,6},{5,7},{6,4},{7,5},{8,10},{9,11},{10,... | collective-permute-start | bytes 393224 | tf_op jit(solution)/shard_map/ppermute | solution.py:425
  4.9 8.4 %collective-permute-start.1 = (bf16[512,128]{1,0:T(8,128)(2,1)S(1)}, bf16[512,128]{1,0:T(8,128)(2,1)S(1)}, u32[]{:S(2)}, u32[]{:S(2)}) collective-permute-start(bf16[512,128]{1,0:T(8,128)(2,1)S(1)} %get-tuple-element.71), channel_id=1, source_target_pairs={{0,4},{1,5},{2,6},{3,7},{4,0},{5,1},{6,2},{7,3},{8,12},{9,13},{10,... | collective-permute-start | bytes 393224 | tf_op jit(solution)/shard_map/ppermute | solution.py:425
  6.5 7.8 %collective-permute-start.2 = (bf16[512,128]{1,0:T(8,128)(2,1)S(1)}, bf16[512,128]{1,0:T(8,128)(2,1)S(1)}, u32[]{:S(2)}, u32[]{:S(2)}) collective-permute-start(bf16[512,128]{1,0:T(8,128)(2,1)S(1)} %get-tuple-element.68), channel_id=1, source_target_pairs={{0,6},{1,7},{2,4},{3,5},{4,2},{5,3},{6,0},{7,1},{8,14},{9,15},{10,... | collective-permute-start | bytes 393224 | tf_op jit(solution)/shard_map/ppermute | solution.py:425
  7.7 8.5 %collective-permute-start.3 = (bf16[512,128]{1,0:T(8,128)(2,1)S(1)}, bf16[512,128]{1,0:T(8,128)(2,1)S(1)}, u32[]{:S(2)}, u32[]{:S(2)}) collective-permute-start(bf16[512,128]{1,0:T(8,128)(2,1)S(1)} %get-tuple-element.65), channel_id=1, source_target_pairs={{0,2},{1,3},{2,0},{3,1},{4,6},{5,7},{6,4},{7,5},{8,10},{9,11},{10,... | collective-permute-start | bytes 393224 | tf_op jit(solution)/shard_map/ppermute | solution.py:425
  9.6 6.5 %collective-permute-start.4 = (bf16[512,128]{1,0:T(8,128)(2,1)S(1)}, bf16[512,128]{1,0:T(8,128)(2,1)S(1)}, u32[]{:S(2)}, u32[]{:S(2)}) collective-permute-start(bf16[512,128]{1,0:T(8,128)(2,1)S(1)} %get-tuple-element.67), channel_id=1, source_target_pairs={{0,4},{1,5},{2,6},{3,7},{4,0},{5,1},{6,2},{7,3},{8,12},{9,13},{10,... | collective-permute-start | bytes 393224 | tf_op jit(solution)/shard_map/ppermute | solution.py:425
  15.3 1.4 %collective-permute-start.6 = (bf16[512,128]{1,0:T(8,128)(2,1)S(1)}, bf16[512,128]{1,0:T(8,128)(2,1)S(1)}, u32[]{:S(2)}, u32[]{:S(2)}) collective-permute-start(bf16[512,128]{1,0:T(8,128)(2,1)S(1)} %get-tuple-element.44), channel_id=1, source_target_pairs={{0,1},{1,0},{2,3},{3,2},{4,5},{5,4},{6,7},{7,6},{8,9},{9,8},{10,11... | collective-permute-start | bytes 393224 | tf_op jit(solution)/shard_map/ppermute | solution.py:425
  16.8 8.3 %collective-permute-start.7 = (bf16[512,128]{1,0:T(8,128)(2,1)S(1)}, bf16[512,128]{1,0:T(8,128)(2,1)S(1)}, u32[]{:S(2)}, u32[]{:S(2)}) collective-permute-start(bf16[512,128]{1,0:T(8,128)(2,1)S(1)} %add_convert_fusion), channel_id=1, source_target_pairs={{0,12},{1,13},{2,14},{3,15},{4,8},{5,9},{6,10},{7,11},{8,4},{9,5},... | collective-permute-start | bytes 393224 | tf_op jit(solution)/shard_map/ppermute | solution.py:425
  20.2 7.7 %collective-permute-start.5 = (bf16[512,128]{1,0:T(8,128)(2,1)S(1)}, bf16[512,128]{1,0:T(8,128)(2,1)S(1)}, u32[]{:S(2)}, u32[]{:S(2)}) collective-permute-start(bf16[512,128]{1,0:T(8,128)(2,1)S(1)} %get-tuple-element.64), channel_id=1, source_target_pairs={{0,6},{1,7},{2,4},{3,5},{4,2},{5,3},{6,0},{7,1},{8,14},{9,15},{10,... | collective-permute-start | bytes 393224 | tf_op jit(solution)/shard_map/ppermute | solution.py:425
  25.3 2.5 %collective-permute-start.8 = (bf16[512,128]{1,0:T(8,128)(2,1)S(1)}, bf16[512,128]{1,0:T(8,128)(2,1)S(1)}, u32[]{:S(2)}, u32[]{:S(2)}) collective-permute-start(bf16[512,128]{1,0:T(8,128)(2,1)S(1)} %multiply_convert_fusion.refs_4_), channel_id=1, source_target_pairs={{0,1},{1,0},{2,3},{3,2},{4,5},{5,4},{6,7},{7,6},{8,9},{9,8},{10,11... | collective-permute-start | bytes 393224 | tf_op jit(solution)/shard_map/ppermute | solution.py:425
  29.4 4.0 %copy-start.1 = (bf16[8,4,8,128]{3,2,1,0:T(8,128)(2,1)S(1)}, bf16[8,4,8,128]{3,2,1,0:T(8,128)(2,1)}, u32[]{:S(2)}) copy-start(bf16[8,4,8,128]{3,2,1,0:T(8,128)(2,1)} %refs_13_.1) | copy-start | bytes 196612
  29.4 4.0 %copy-start.2 = (s32[8,4,32]{2,1,0:T(4,128)S(1)}, s32[8,4,32]{2,1,0:T(4,128)}, u32[]{:S(2)}) copy-start(s32[8,4,32]{2,1,0:T(4,128)} %refs_14_.1) | copy-start | bytes 12292
  29.4 4.0 %copy-start.3 = (s32[4,64]{1,0:T(4,128)S(1)}, s32[4,64]{1,0:T(4,128)}, u32[]{:S(2)}) copy-start(s32[4,64]{1,0:T(4,128)} %refs_4_.1) | copy-start | bytes 3076
  29.4 4.0 %copy-start.4 = (s32[8]{0:T(128)S(1)}, s32[8]{0:T(128)}, u32[]{:S(2)}) copy-start(s32[8]{0:T(128)} %refs_3_.1) | copy-start | bytes 100
  29.4 1.6 %collective-permute-start.9 = (bf16[528,256]{1,0:T(8,128)(2,1)S(1)}, bf16[528,256]{1,0:T(8,128)(2,1)S(1)}, u32[]{:S(2)}, u32[]{:S(2)}) collective-permute-start(bf16[528,256]{1,0:T(8,128)(2,1)S(1)} %get-tuple-element.51), channel_id=1, source_target_pairs={{0,1},{1,0},{2,3},{3,2},{4,5},{5,4},{6,7},{7,6},{8,9},{9,8},{10,11... | collective-permute-start | bytes 811016 | tf_op jit(solution)/shard_map/ppermute | solution.py:425
  31.1 7.7 %collective-permute-start.10 = (bf16[272,256]{1,0:T(8,128)(2,1)S(1)}, bf16[272,256]{1,0:T(8,128)(2,1)S(1)}, u32[]{:S(2)}, u32[]{:S(2)}) collective-permute-start(bf16[272,256]{1,0:T(8,128)(2,1)S(1)} %get-tuple-element.54), channel_id=1, source_target_pairs={{0,12},{1,13},{2,14},{3,15},{4,8},{5,9},{6,10},{7,11},{8,4},{9,5},... | collective-permute-start | bytes 417800 | tf_op jit(solution)/shard_map/ppermute | solution.py:425
  39.3 1.2 %collective-permute-start.11 = (f32[72,128]{1,0:T(8,128)S(1)}, f32[72,128]{1,0:T(8,128)S(1)}, u32[]{:S(2)}, u32[]{:S(2)}) collective-permute-start(f32[72,128]{1,0:T(8,128)S(1)} %get-tuple-element.59.own_ref), channel_id=1, source_target_pairs={{0,1},{1,0},{2,3},{3,2},{4,5},{5,4},{6,7},{7,6},{8,9},{9,8},{10,11... | collective-permute-start | bytes 110600 | tf_op jit(solution)/shard_map/ppermute | solution.py:425
  40.7 5.8 %collective-permute-start.12 = (f32[72,128]{1,0:T(8,128)S(1)}, f32[72,128]{1,0:T(8,128)S(1)}, u32[]{:S(2)}, u32[]{:S(2)}) collective-permute-start(f32[72,128]{1,0:T(8,128)S(1)} %shard_map.97.own_ref), channel_id=1, source_target_pairs={{0,12},{1,13},{2,14},{3,15},{4,8},{5,9},{6,10},{7,11},{8,4},{9,5},... | collective-permute-start | bytes 110600 | tf_op jit(solution)/shard_map/ppermute | solution.py:425
  46.6 4.3 %collective-permute-start.13 = (bf16[128,128]{1,0:T(8,128)(2,1)S(1)}, bf16[128,128]{1,0:T(8,128)(2,1)S(1)}, u32[]{:S(2)}, u32[]{:S(2)}) collective-permute-start(bf16[128,128]{1,0:T(8,128)(2,1)S(1)} %get-tuple-element.61), channel_id=1, source_target_pairs={{0,2},{1,3},{2,0},{3,1},{4,6},{5,7},{6,4},{7,5},{8,10},{9,11},{10,... | collective-permute-start | bytes 98312 | tf_op jit(solution)/shard_map/ppermute | solution.py:425
  47.4 3.9 %collective-permute-start.14 = (bf16[128,128]{1,0:T(8,128)(2,1)S(1)}, bf16[128,128]{1,0:T(8,128)(2,1)S(1)}, u32[]{:S(2)}, u32[]{:S(2)}) collective-permute-start(bf16[128,128]{1,0:T(8,128)(2,1)S(1)} %get-tuple-element.62), channel_id=1, source_target_pairs={{0,4},{1,5},{2,6},{3,7},{4,0},{5,1},{6,2},{7,3},{8,12},{9,13},{10,... | collective-permute-start | bytes 98312 | tf_op jit(solution)/shard_map/ppermute | solution.py:425
  48.4 4.8 %collective-permute-start.15 = (bf16[128,128]{1,0:T(8,128)(2,1)S(1)}, bf16[128,128]{1,0:T(8,128)(2,1)S(1)}, u32[]{:S(2)}, u32[]{:S(2)}) collective-permute-start(bf16[128,128]{1,0:T(8,128)(2,1)S(1)} %get-tuple-element.63), channel_id=1, source_target_pairs={{0,6},{1,7},{2,4},{3,5},{4,2},{5,3},{6,0},{7,1},{8,14},{9,15},{10,... | collective-permute-start | bytes 98312 | tf_op jit(solution)/shard_map/ppermute | solution.py:425

commit v6 on v5

--- a/solution.py
+++ b/solution.py
@@ -190,6 +190,14 @@
     )
 
 
+def cents_kernel(own_ref, recv_ref, out_ref):
+    half = own_ref.shape[0] // 2
+    for at in (0, half):
+        recv = recv_ref[half - at : 2 * half - at, :]
+        sums = own_ref[at : at + half, :].astype(F32) + recv.astype(F32)
+        out_ref[at : at + half, :] = to_unit(sums).astype(BF16)
+
+
 def own_half_kernel(count, *refs):
     key_refs, (cent_ref, unit_ref, raised_ref, total_ref) = refs[:count], refs[count:]
     first = 0
@@ -203,38 +211,53 @@
 
 
 def other_half_kernel(count, *refs):
-    key_refs, value_refs = refs[:count], refs[count : 2 * count]
-    unit_ref, cent_ref, total_ref, send_ref, inverse_ref, raised_ref, weight_ref, mass_ref = refs[
-        2 * count :
-    ]
-    half, lanes = cent_ref.shape[0], send_ref.shape[1]
+    pair_refs, refs = refs[: 2 * count], refs[2 * count :]
+    unit_ref, cent_ref, total_ref, send_ref, inverse_ref, early_ref = refs[:6]
+    raised_ref, weight_ref, mass_ref = refs[6:]
+    rows, lanes = early_ref.shape[0], send_ref.shape[1]
     first = 0
-    for key_ref in key_refs:
+    for key_ref in pair_refs[:count]:
         tokens = key_ref.shape[0]
         chunk = slice(first, first + tokens)
         total = fill_raised(cent_ref, unit_ref[chunk, :], raised_ref, 0, 0)
         inverse = 1.0 / (total_ref[0:1, chunk] + total)
         inverse_ref[:, chunk] = jnp.broadcast_to(inverse, (8, tokens))
-        fill_weights(raised_ref, inverse, weight_ref, half, 0, first, 0, mass_ref)
+        fill_weights(raised_ref, inverse, weight_ref, rows, rows, first, 0, mass_ref)
+        early_ref[:, chunk] = raised_ref[:rows, :tokens].astype(BF16)
         first += tokens
     masses = jnp.sum(mass_ref[...].T, axis=0, keepdims=True)
-    send_ref[half:, :] = packed_masses(masses, lanes)
-    product(send_ref, weight_ref, joined_pairs(key_refs, value_refs))
-
-
-def keep_half_kernel(count, *refs):
-    key_refs, value_refs = refs[:count], refs[count : 2 * count]
-    raised_ref, inverse_ref, keep_ref, keep_mass_ref, weight_ref, mass_ref = refs[2 * count :]
-    half = keep_ref.shape[0]
+    send_ref[rows:, :] = packed_masses(masses, lanes)
+    product(send_ref, weight_ref, joined_pairs(pair_refs[:count], pair_refs[count:]))
+
+
+def part_kernel(count, row, to_send, *refs):
+    pair_refs, refs = refs[: 2 * count], refs[2 * count :]
+    raised_ref, inverse_ref, refs = refs[0], refs[1], refs[2:]
+    out_ref, (weight_ref, mass_ref) = refs[0], refs[-2:]
+    rows = weight_ref.shape[0]
     first = 0
-    for key_ref in key_refs:
+    for key_ref in pair_refs[:count]:
         tokens = key_ref.shape[0]
         inverse = inverse_ref[0:1, first : first + tokens]
-        fill_weights(raised_ref, inverse, weight_ref, half, 0, first, first, mass_ref)
+        fill_weights(raised_ref, inverse, weight_ref, rows, row, first, first, mass_ref)
         first += tokens
     masses = jnp.sum(mass_ref[...].T, axis=0, keepdims=True)
-    keep_mass_ref[...] = jnp.broadcast_to(masses, keep_mass_ref.shape)
-    product(keep_ref, weight_ref, joined_pairs(key_refs, value_refs))
+    if to_send:
+        out_ref[rows:, :] = packed_masses(masses, out_ref.shape[1])
+    else:
+        refs[1][...] = jnp.broadcast_to(masses, refs[1].shape)
+    product(out_ref, weight_ref, joined_pairs(pair_refs[:count], pair_refs[count:]))
+
+
+def both_kernel(to_send, keep_ref, mass_ref, recv_ref, out_ref, *refs):
+    count, lanes = keep_ref.shape
+    masses = mass_ref[0:1, :] + unpacked_masses(recv_ref[count:, :], count)
+    sums = keep_ref[...] + recv_ref[:count, :].astype(F32)
+    out_ref[:count, :] = sums.astype(out_ref.dtype)
+    if to_send:
+        out_ref[count:, :] = packed_masses(masses, lanes)
+    else:
+        refs[0][...] = jnp.broadcast_to(masses, refs[0].shape)
 
 
 def halve_kernel(keep_ref, mass_ref, recv_ref, keep_out_ref, mass_out_ref, send_ref):
@@ -427,8 +450,9 @@
     def pick(array, at, axis=0):
         return lax.dynamic_index_in_dim(array, at, axis, keepdims=False)
 
-    keys = [pick(key_cache, head)]
-    keys += [over(pick(key_cache, head ^ s), head_masks[s]) for s in range(1, heads)]
+    slices = [pick(cache, head ^ s) for cache in (key_cache, value_cache) for s in range(heads)]
+    slices = lax.optimization_barrier(tuple(slices))
+    keys = [slices[0]] + [over(slices[s], head_masks[s]) for s in range(1, heads)]
 
     blocks = pick(init_centroids, head).reshape(devices, per_owner, dim)
     turned = [int(format(r, f"0{levels}b")[::-1], 2) for r in range(spread)]
@@ -449,8 +473,7 @@
         pass_flops,
         scalars=1,
     )
-    values = [pick(value_cache, head)]
-    values += [over(pick(value_cache, head ^ s), head_masks[s]) for s in range(1, heads)]
+    values = [slices[heads]] + [over(slices[heads + s], head_masks[s]) for s in range(1, heads)]
 
     keep_weights = [keep_weights]
     for step in range(1, heads):
@@ -470,7 +493,7 @@
         (),
         pass_flops * heads // 4,
     )
-    keep, values[1], values[2] = lax.optimization_barrier((keep, values[1], values[2]))
+    keep, values[3] = lax.optimization_barrier((keep, values[3]))
     for level in range(levels - 1):
         total = keep + over(send, rank_basis[level]).astype(F32)
         if level < levels - 2:
@@ -478,9 +501,7 @@
             keep, send = total[:cut], total[cut:].astype(BF16)
     rounded = total.astype(BF16)
     recv = over(rounded, rank_basis[levels - 1])
-    cut = rounded.shape[0] // 2
-    recv = jnp.concatenate([recv[cut:], recv[:cut]])
-    own_cents = to_unit(rounded.astype(F32) + recv.astype(F32)).astype(BF16)
+    (own_cents,) = call(cents_kernel, [shape(rounded.shape, BF16)], [rounded, recv])
     for level in range(levels - 2, 0, -1):
         own_cents = jnp.concatenate([own_cents, over(own_cents, rank_basis[level])])
     other_cents = over(own_cents, 1)
@@ -493,21 +514,42 @@
         (),
         pass_flops * heads // 4,
     )
-    half_scratch = [pltpu.VMEM((half, tokens), BF16), pltpu.VMEM((half, 128), F32)]
-    send, inverse = call(
+    part = half // 2
+    part_scratch = [pltpu.VMEM((part, tokens), BF16), pltpu.VMEM((part, 128), F32)]
+    sent = shape((part + 16, 2 * dim), BF16)
+    kept = [shape((part, 2 * dim), F32), shape((8, part), F32)]
+    send, inverse, early = call(
         functools.partial(other_half_kernel, heads),
-        [shape((half + 16, 2 * dim), BF16), shape((8, tokens), F32)],
+        [sent, shape((8, tokens), F32), shape((part, tokens), BF16)],
         [*keys, *values, unit_keys, other_cents, total],
-        [pltpu.VMEM((half, tok_dev), F32), *half_scratch],
-        pass_flops * heads * 3 // 4,
+        [pltpu.VMEM((half, tok_dev), F32), *part_scratch],
+        pass_flops * heads // 2,
+    )
+    later = call(
+        functools.partial(part_kernel, heads, part, False),
+        kept,
+        [*keys, *values, raised, inverse],
+        part_scratch,
+        pass_flops * heads // 4,
+    )
+    recv = over(send, 1)
+    (send,) = call(functools.partial(both_kernel, True), [sent], [*later, recv])
+    (early_send,) = call(
+        functools.partial(part_kernel, heads, 0, True),
+        [sent],
+        [*keys, *values, early, inverse],
+        part_scratch,
+        pass_flops * heads // 4,
     )
     keep, keep_mass = call(
-        functools.partial(keep_half_kernel, heads),
-        [shape((half, 2 * dim), F32), shape((8, half), F32)],
+        functools.partial(part_kernel, heads, 0, False),
+        kept,
         [*keys, *values, raised, inverse],
-        half_scratch,
-        pass_flops * heads // 2,
-    )
+        part_scratch,
+        pass_flops * heads // 4,
+    )
+    early_recv = over(early_send, 1)
+    keep, keep_mass = call(functools.partial(both_kernel, False), kept, [keep, keep_mass, early_recv])
 
     exact, own_queries, usable = call(
         functools.partial(exact_kernel, heads, head_masks, head_masks, per_owner),
@@ -528,7 +570,7 @@
         scalars=5,
     )
 
-    for level in range(levels - 1):
+    for level in range(1, levels - 1):
         recv = over(send, rank_basis[level])
         count = keep.shape[0] // 2
         keep, keep_mass, send = call(

time: 54 us -> 53.8 us (level)
  starting transfers between devices: 20.5 us -> 23.4 us
  waiting for transfers between devices: 18.4 us -> 15.7 us
  local copies, waits for them, and re-layouts: 2.41 us -> 1.49 us
  Pallas kernels: 11.3 us -> 12.1 us
    ppermute x16 -> x17, starting transfers between devices: 20.5 us -> 23.4 us  [over(): return lax.ppermute(array, 'ctx', [(i, i ^ bit) for i in range(devices)])]
    ppermute x16 -> x17, waiting for transfers between devices: 18.4 us -> 15.7 us  [over(): return lax.ppermute(array, 'ctx', [(i, i ^ bit) for i in range(devices)])]
    squeeze x2 -> x1, local copies, waits for them, and re-layouts: 2.35 us -> 1.43 us  [pick(): return lax.dynamic_index_in_dim(array, at, axis, keepdims=False)]
    pallas_call x14 -> x18, Pallas kernels: 11.3 us -> 12.1 us  [call(): pl.pallas_call(kernel, out_shape=tuple(outs), in_specs=in_specs, out_spec...]
  transfers between devices with their start and end apart: 16 -> 17, of which waited for: 10 -> 10; matrix products, arithmetic and copies ran while one was open for 3% -> 0% of each run, Pallas kernels for 15% -> 17%
where the time goes in v6:
time: 53.8 us; the launch traced here: 53.7 us
  starting transfers between devices  23.4 us (43%)
  waiting for transfers between devices  15.7 us (29%)
  Pallas kernels  12.1 us (22%)
  local copies, waits for them, and re-layouts  1.49 us (3%)
  between operations  0.92 us (2%)
    ppermute x17, starting transfers between devices, over(): return lax.ppermute(array, 'ctx', [(i, i ^ bit) for i in range(devices)])  23.4 us
    ppermute x17, waiting for transfers between devices, over(): return lax.ppermute(array, 'ctx', [(i, i ^ bit) for i in range(devices)])  15.7 us
    pallas_call x18, Pallas kernels, call(): pl.pallas_call(kernel, out_shape=tuple(outs), in_specs=in_specs, out_spec...  12.1 us
    squeeze x1, local copies, waits for them, and re-layouts, pick(): return lax.dynamic_index_in_dim(array, at, axis, keepdims=False)  1.43 us
  transfers between devices with their start and end apart: 17, of which 10 were waited for; matrix products, arithmetic and copies ran while one was open for 0% of the time, Pallas kernels for 17%

profile of v6, /device:TPU:0, one launch (start us, length us, event | category | flops | bytes accessed | tf_op | source)
XLA Modules:
  0.0 53.7 jit_solution(14259384291703599747)
XLA Ops:
  0.7 1.4 %dynamic-slice_bitcast_fusion = (bf16[512,128]{1,0:T(8,128)(2,1)S(1)}, bf16[512,128]{1,0:T(8,128)(2,1)S(1)}, bf16[512,128]{1,0:T(8,128)(2,1)S(1)}, bf16[512,128]...) fusion(bf16[4,512,128]{2,1,0:T(8,128)(2,1)} %param.8, ...), kind=kLoop, calls=%fused_computation.1 | loop fusion | bytes 2097168 | tf_op jit(solution)/shard_map/jit(dynamic_index_in_dim)/squeeze | solution.py:451
  2.1 3.0 %collective-permute-start = (bf16[512,128]{1,0:T(8,128)(2,1)S(1)}, bf16[512,128]{1,0:T(8,128)(2,1)S(1)}, u32[]{:S(2)}, u32[]{:S(2)}) collective-permute-start(bf16[512,128]{1,0:T(8,128)(2,1)S(1)} %get-tuple-element.43), channel_id=1, source_target_pairs={{0,2},{1,3},{2,0},{3,1},{4,6},{5,7},{6,4},{7,5},{8,10},{9,11},{10,... | collective-permute-start | bytes 393224 | tf_op jit(solution)/shard_map/ppermute | solution.py:448
  5.2 1.6 %collective-permute-start.1 = (bf16[512,128]{1,0:T(8,128)(2,1)S(1)}, bf16[512,128]{1,0:T(8,128)(2,1)S(1)}, u32[]{:S(2)}, u32[]{:S(2)}) collective-permute-start(bf16[512,128]{1,0:T(8,128)(2,1)S(1)} %get-tuple-element.44), channel_id=1, source_target_pairs={{0,4},{1,5},{2,6},{3,7},{4,0},{5,1},{6,2},{7,3},{8,12},{9,13},{10,... | collective-permute-start | bytes 393224 | tf_op jit(solution)/shard_map/ppermute | solution.py:448
  6.7 2.9 %collective-permute-start.5 = (bf16[512,128]{1,0:T(8,128)(2,1)S(1)}, bf16[512,128]{1,0:T(8,128)(2,1)S(1)}, u32[]{:S(2)}, u32[]{:S(2)}) collective-permute-start(bf16[512,128]{1,0:T(8,128)(2,1)S(1)} %get-tuple-element.57), channel_id=1, source_target_pairs={{0,6},{1,7},{2,4},{3,5},{4,2},{5,3},{6,0},{7,1},{8,14},{9,15},{10,... | collective-permute-start | bytes 393224 | tf_op jit(solution)/shard_map/ppermute | solution.py:448
  9.7 1.0 %shard_map.86 = (f32[512,128]{1,0:T(8,128)S(1)}, bf16[512,512]{1,0:T(8,128)(2,1)S(1)}, bf16[1024,128]{1,0:T(8,128)(2,1)S(1)}) custom-call(s32[1]{0:T(128)} %bitcast.9.base_ref.refs_2_, bf16[512,128]{1,0:T(8,128)(2,1)S(1)} %get-tuple-element.42.refs_0_.refs_5_, bf16[16,64,128]{2,1,0:T(8,128)(2,1)S(1)} %bitcast.25), custom_call_target="tpu_custom_call" | custom-call | flops 268435456 | bytes 1441796 | tf_op jit(solution)/shard_map/pallas_call | solution.py:64
  10.8 1.0 %shard_map.87 = (f32[512,128]{1,0:T(8,128)S(1)}, bf16[512,512]{1,0:T(8,128)(2,1)S(1)}) custom-call(bf16[512,128]{1,0:T(8,128)(2,1)S(1)} %collective-permute-done.key_ref.refs_1_.refs_6_, bf16[1024,128]{1,0:T(8,128)(2,1)S(1)} %get-tuple-element.50.unit_ref, f32[512,128]{1,0:T(8,128)S(1)} %get-tuple-element.51.before_ref), custom_call_target="tpu_custom_call" | custom-call | flops 268435456 | bytes 1441792 | tf_op jit(solution)/shard_map/pallas_call | solution.py:64
  11.8 1.0 %shard_map.88 = (f32[512,128]{1,0:T(8,128)S(1)}, bf16[512,512]{1,0:T(8,128)(2,1)S(1)}) custom-call(bf16[512,128]{1,0:T(8,128)(2,1)S(1)} %collective-permute-done.1.key_ref.refs_2_.refs_7_, bf16[1024,128]{1,0:T(8,128)(2,1)S(1)} %get-tuple-element.50.unit_ref, f32[512,128]{1,0:T(8,128)S(1)} %get-tuple-element.53.before_ref), custom_call_target="tpu_custom_call" | custom-call | flops 268435456 | bytes 1441792 | tf_op jit(solution)/shard_map/pallas_call | solution.py:64
  12.8 1.3 %collective-permute-done.2.key_ref.refs_3_.refs_8_ = bf16[512,128]{1,0:T(8,128)(2,1)S(1)} collective-permute-done((bf16[512,128]{1,0:T(8,128)(2,1)S(1)}, bf16[512,128]{1,0:T(8,128)(2,1)S(1)}, u32[]{:S(2)}, u32[]{:S(2)}) %collective-permute-start.2) | collective-permute-done | bytes 131104 | tf_op jit(solution)/shard_map/ppermute | solution.py:448
  16.5 3.9 %collective-permute-start.7 = (bf16[512,128]{1,0:T(8,128)(2,1)S(1)}, bf16[512,128]{1,0:T(8,128)(2,1)S(1)}, u32[]{:S(2)}, u32[]{:S(2)}) collective-permute-start(bf16[512,128]{1,0:T(8,128)(2,1)S(1)} %add_convert_fusion.own_ref), channel_id=1, source_target_pairs={{0,12},{1,13},{2,14},{3,15},{4,8},{5,9},{6,10},{7,11},{8,4},{9,5},... | collective-permute-start | bytes 393224 | tf_op jit(solution)/shard_map/ppermute | solution.py:448
  20.4 1.5 %collective-permute-start.3 = (bf16[512,128]{1,0:T(8,128)(2,1)S(1)}, bf16[512,128]{1,0:T(8,128)(2,1)S(1)}, u32[]{:S(2)}, u32[]{:S(2)}) collective-permute-start(bf16[512,128]{1,0:T(8,128)(2,1)S(1)} %get-tuple-element.47), channel_id=1, source_target_pairs={{0,2},{1,3},{2,0},{3,1},{4,6},{5,7},{6,4},{7,5},{8,10},{9,11},{10,... | collective-permute-start | bytes 393224 | tf_op jit(solution)/shard_map/ppermute | solution.py:448
  21.9 2.8 %collective-permute-done.7.recv_ref = bf16[512,128]{1,0:T(8,128)(2,1)S(1)} collective-permute-done((bf16[512,128]{1,0:T(8,128)(2,1)S(1)}, bf16[512,128]{1,0:T(8,128)(2,1)S(1)}, u32[]{:S(2)}, u32[]{:S(2)}) %collective-permute-start.7) | collective-permute-done | bytes 131104 | tf_op jit(solution)/shard_map/ppermute | solution.py:448
  25.0 1.0 %shard_map.92 = (bf16[2048,128]{1,0:T(8,128)(2,1)S(1)}, bf16[512,2048]{1,0:T(8,128)(2,1)S(1)}, f32[8,2048]{1,0:T(8,128)S(1)}) custom-call(bf16[512,128]{1,0:T(8,128)(2,1)S(1)} %get-tuple-element.42.refs_0_.refs_5_, bf16[512,128]{1,0:T(8,128)(2,1)S(1)} %collective-permute-done.key_ref.refs_1_.refs_6_, ...), custom_call_target="tpu_custom_call" | custom-call | flops 268435456 | bytes 3342336 | tf_op jit(solution)/shard_map/pallas_call | solution.py:64
  26.0 1.2 %collective-permute-done.4.refs_6_.refs_11_ = bf16[512,128]{1,0:T(8,128)(2,1)S(1)} collective-permute-done((bf16[512,128]{1,0:T(8,128)(2,1)S(1)}, bf16[512,128]{1,0:T(8,128)(2,1)S(1)}, u32[]{:S(2)}, u32[]{:S(2)}) %collective-permute-start.4) | collective-permute-done | bytes 131104 | tf_op jit(solution)/shard_map/ppermute | solution.py:448
  27.2 1.3 %shard_map.93 = (bf16[272,256]{1,0:T(8,128)(2,1)S(1)}, f32[8,2048]{1,0:T(8,128)S(1)}, bf16[256,2048]{1,0:T(8,128)(2,1)S(1)}) custom-call(bf16[512,128]{1,0:T(8,128)(2,1)S(1)} %get-tuple-element.42.refs_0_.refs_5_, bf16[512,128]{1,0:T(8,128)(2,1)S(1)} %collective-permute-done.key_ref.refs_1_.refs_6_, ...), custom_call_target="tpu_custom_call" | custom-call | flops 536870912 | bytes 3022848 | tf_op jit(solution)/shard_map/pallas_call | solution.py:64
  30.3 3.0 %collective-permute-start.11 = (bf16[272,256]{1,0:T(8,128)(2,1)S(1)}, bf16[272,256]{1,0:T(8,128)(2,1)S(1)}, u32[]{:S(2)}, u32[]{:S(2)}) collective-permute-start(bf16[272,256]{1,0:T(8,128)(2,1)S(1)} %shard_map.98), channel_id=1, source_target_pairs={{0,12},{1,13},{2,14},{3,15},{4,8},{5,9},{6,10},{7,11},{8,4},{9,5},... | collective-permute-start | bytes 417800 | tf_op jit(solution)/shard_map/ppermute | solution.py:448
  33.3 1.8 %shard_map.99 = (f32[72,128]{1,0:T(8,128)S(1)}, f32[64,128]{1,0:T(8,128)S(1)}, f32[64,256]{1,0:T(8,128)S(1)}) custom-call(s32[1]{0:T(128)} %bitcast.refs_0_.head_ref, s32[1]{0:T(128)} %bitcast.11.refs_1_, s32[1]{0:T(128)} %bitcast.9.base_ref.refs_2_, s32[8]{0:T(128)S(1)} %copy-done.4, s32[4,64]{1,0:T(4,128)S(1)} %copy-done.3, ...), custom_call_target="tpu_custom_call" | custom-call | flops 67108864 | bytes 1254444 | tf_op jit(solution)/shard_map/pallas_call | solution.py:64
  35.6 2.2 %collective-permute-done.11.recv_ref = bf16[272,256]{1,0:T(8,128)(2,1)S(1)} collective-permute-done((bf16[272,256]{1,0:T(8,128)(2,1)S(1)}, bf16[272,256]{1,0:T(8,128)(2,1)S(1)}, u32[]{:S(2)}, u32[]{:S(2)}) %collective-permute-start.11) | collective-permute-done | bytes 139296 | tf_op jit(solution)/shard_map/ppermute | solution.py:448
  38.4 1.2 %collective-permute-done.12.recv_ref = f32[72,128]{1,0:T(8,128)S(1)} collective-permute-done((f32[72,128]{1,0:T(8,128)S(1)}, f32[72,128]{1,0:T(8,128)S(1)}, u32[]{:S(2)}, u32[]{:S(2)}) %collective-permute-start.12) | collective-permute-done | bytes 36896 | tf_op jit(solution)/shard_map/ppermute | solution.py:448
  39.8 3.2 %collective-permute-start.13 = (f32[72,128]{1,0:T(8,128)S(1)}, f32[72,128]{1,0:T(8,128)S(1)}, u32[]{:S(2)}, u32[]{:S(2)}) collective-permute-start(f32[72,128]{1,0:T(8,128)S(1)} %shard_map.101.own_ref), channel_id=1, source_target_pairs={{0,12},{1,13},{2,14},{3,15},{4,8},{5,9},{6,10},{7,11},{8,4},{9,5},... | collective-permute-start | bytes 110600 | tf_op jit(solution)/shard_map/ppermute | solution.py:448
  42.9 2.6 %collective-permute-done.13.recv_ref = f32[72,128]{1,0:T(8,128)S(1)} collective-permute-done((f32[72,128]{1,0:T(8,128)S(1)}, f32[72,128]{1,0:T(8,128)S(1)}, u32[]{:S(2)}, u32[]{:S(2)}) %collective-permute-start.13) | collective-permute-done | bytes 36896 | tf_op jit(solution)/shard_map/ppermute | solution.py:448
  45.7 1.5 %collective-permute-start.14 = (bf16[128,128]{1,0:T(8,128)(2,1)S(1)}, bf16[128,128]{1,0:T(8,128)(2,1)S(1)}, u32[]{:S(2)}, u32[]{:S(2)}) collective-permute-start(bf16[128,128]{1,0:T(8,128)(2,1)S(1)} %get-tuple-element.79), channel_id=1, source_target_pairs={{0,2},{1,3},{2,0},{3,1},{4,6},{5,7},{6,4},{7,5},{8,10},{9,11},{10,... | collective-permute-start | bytes 98312 | tf_op jit(solution)/shard_map/ppermute | solution.py:448
  48.2 1.1 %collective-permute-start.16 = (bf16[128,128]{1,0:T(8,128)(2,1)S(1)}, bf16[128,128]{1,0:T(8,128)(2,1)S(1)}, u32[]{:S(2)}, u32[]{:S(2)}) collective-permute-start(bf16[128,128]{1,0:T(8,128)(2,1)S(1)} %get-tuple-element.81), channel_id=1, source_target_pairs={{0,6},{1,7},{2,4},{3,5},{4,2},{5,3},{6,0},{7,1},{8,14},{9,15},{10,... | collective-permute-start | bytes 98312 | tf_op jit(solution)/shard_map/ppermute | solution.py:448
  49.7 1.4 %collective-permute-done.15.refs_1_ = bf16[128,128]{1,0:T(8,128)(2,1)S(1)} collective-permute-done((bf16[128,128]{1,0:T(8,128)(2,1)S(1)}, bf16[128,128]{1,0:T(8,128)(2,1)S(1)}, u32[]{:S(2)}, u32[]{:S(2)}) %collective-permute-start.15) | collective-permute-done | bytes 32800 | tf_op jit(solution)/shard_map/ppermute | solution.py:448
  51.1 1.9 %collective-permute-done.16.refs_2_ = bf16[128,128]{1,0:T(8,128)(2,1)S(1)} collective-permute-done((bf16[128,128]{1,0:T(8,128)(2,1)S(1)}, bf16[128,128]{1,0:T(8,128)(2,1)S(1)}, u32[]{:S(2)}, u32[]{:S(2)}) %collective-permute-start.16) | collective-permute-done | bytes 32800 | tf_op jit(solution)/shard_map/ppermute | solution.py:448
  (41 shorter events, 7.9 us)
Async XLA Ops:
  0.6 9.0 %copy-start = (bf16[4,1024,128]{2,1,0:T(8,128)(2,1)S(1)}, bf16[4,1024,128]{2,1,0:T(8,128)(2,1)}, u32[]{:S(2)}) copy-start(bf16[4,1024,128]{2,1,0:T(8,128)(2,1)} %param.9) | copy-start | bytes 3145732
  2.1 8.6 %collective-permute-start = (bf16[512,128]{1,0:T(8,128)(2,1)S(1)}, bf16[512,128]{1,0:T(8,128)(2,1)S(1)}, u32[]{:S(2)}, u32[]{:S(2)}) collective-permute-start(bf16[512,128]{1,0:T(8,128)(2,1)S(1)} %get-tuple-element.43), channel_id=1, source_target_pairs={{0,2},{1,3},{2,0},{3,1},{4,6},{5,7},{6,4},{7,5},{8,10},{9,11},{10,... | collective-permute-start | bytes 393224 | tf_op jit(solution)/shard_map/ppermute | solution.py:448
  5.2 6.6 %collective-permute-start.1 = (bf16[512,128]{1,0:T(8,128)(2,1)S(1)}, bf16[512,128]{1,0:T(8,128)(2,1)S(1)}, u32[]{:S(2)}, u32[]{:S(2)}) collective-permute-start(bf16[512,128]{1,0:T(8,128)(2,1)S(1)} %get-tuple-element.44), channel_id=1, source_target_pairs={{0,4},{1,5},{2,6},{3,7},{4,0},{5,1},{6,2},{7,3},{8,12},{9,13},{10,... | collective-permute-start | bytes 393224 | tf_op jit(solution)/shard_map/ppermute | solution.py:448
  6.7 7.3 %collective-permute-start.2 = (bf16[512,128]{1,0:T(8,128)(2,1)S(1)}, bf16[512,128]{1,0:T(8,128)(2,1)S(1)}, u32[]{:S(2)}, u32[]{:S(2)}) collective-permute-start(bf16[512,128]{1,0:T(8,128)(2,1)S(1)} %get-tuple-element.45), channel_id=1, source_target_pairs={{0,6},{1,7},{2,4},{3,5},{4,2},{5,3},{6,0},{7,1},{8,14},{9,15},{10,... | collective-permute-start | bytes 393224 | tf_op jit(solution)/shard_map/ppermute | solution.py:448
  6.7 9.1 %collective-permute-start.5 = (bf16[512,128]{1,0:T(8,128)(2,1)S(1)}, bf16[512,128]{1,0:T(8,128)(2,1)S(1)}, u32[]{:S(2)}, u32[]{:S(2)}) collective-permute-start(bf16[512,128]{1,0:T(8,128)(2,1)S(1)} %get-tuple-element.57), channel_id=1, source_target_pairs={{0,6},{1,7},{2,4},{3,5},{4,2},{5,3},{6,0},{7,1},{8,14},{9,15},{10,... | collective-permute-start | bytes 393224 | tf_op jit(solution)/shard_map/ppermute | solution.py:448
  15.1 1.4 %collective-permute-start.6 = (bf16[512,128]{1,0:T(8,128)(2,1)S(1)}, bf16[512,128]{1,0:T(8,128)(2,1)S(1)}, u32[]{:S(2)}, u32[]{:S(2)}) collective-permute-start(bf16[512,128]{1,0:T(8,128)(2,1)S(1)} %get-tuple-element.60), channel_id=1, source_target_pairs={{0,1},{1,0},{2,3},{3,2},{4,5},{5,4},{6,7},{7,6},{8,9},{9,8},{10,11... | collective-permute-start | bytes 393224 | tf_op jit(solution)/shard_map/ppermute | solution.py:448
  16.5 8.2 %collective-permute-start.7 = (bf16[512,128]{1,0:T(8,128)(2,1)S(1)}, bf16[512,128]{1,0:T(8,128)(2,1)S(1)}, u32[]{:S(2)}, u32[]{:S(2)}) collective-permute-start(bf16[512,128]{1,0:T(8,128)(2,1)S(1)} %add_convert_fusion.own_ref), channel_id=1, source_target_pairs={{0,12},{1,13},{2,14},{3,15},{4,8},{5,9},{6,10},{7,11},{8,4},{9,5},... | collective-permute-start | bytes 393224 | tf_op jit(solution)/shard_map/ppermute | solution.py:448
  20.4 5.6 %collective-permute-start.3 = (bf16[512,128]{1,0:T(8,128)(2,1)S(1)}, bf16[512,128]{1,0:T(8,128)(2,1)S(1)}, u32[]{:S(2)}, u32[]{:S(2)}) collective-permute-start(bf16[512,128]{1,0:T(8,128)(2,1)S(1)} %get-tuple-element.47), channel_id=1, source_target_pairs={{0,2},{1,3},{2,0},{3,1},{4,6},{5,7},{6,4},{7,5},{8,10},{9,11},{10,... | collective-permute-start | bytes 393224 | tf_op jit(solution)/shard_map/ppermute | solution.py:448
  21.9 5.3 %collective-permute-start.4 = (bf16[512,128]{1,0:T(8,128)(2,1)S(1)}, bf16[512,128]{1,0:T(8,128)(2,1)S(1)}, u32[]{:S(2)}, u32[]{:S(2)}) collective-permute-start(bf16[512,128]{1,0:T(8,128)(2,1)S(1)} %get-tuple-element.48), channel_id=1, source_target_pairs={{0,4},{1,5},{2,6},{3,7},{4,0},{5,1},{6,2},{7,3},{8,12},{9,13},{10,... | collective-permute-start | bytes 393224 | tf_op jit(solution)/shard_map/ppermute | solution.py:448
  24.9 2.3 %collective-permute-start.8 = (bf16[512,128]{1,0:T(8,128)(2,1)S(1)}, bf16[512,128]{1,0:T(8,128)(2,1)S(1)}, u32[]{:S(2)}, u32[]{:S(2)}) collective-permute-start(bf16[512,128]{1,0:T(8,128)(2,1)S(1)} %shard_map.91.refs_4_), channel_id=1, source_target_pairs={{0,1},{1,0},{2,3},{3,2},{4,5},{5,4},{6,7},{7,6},{8,9},{9,8},{10,11... | collective-permute-start | bytes 393224 | tf_op jit(solution)/shard_map/ppermute | solution.py:448
  28.5 1.7 %collective-permute-start.10 = (bf16[272,256]{1,0:T(8,128)(2,1)S(1)}, bf16[272,256]{1,0:T(8,128)(2,1)S(1)}, u32[]{:S(2)}, u32[]{:S(2)}) collective-permute-start(bf16[272,256]{1,0:T(8,128)(2,1)S(1)} %get-tuple-element.72), channel_id=1, source_target_pairs={{0,1},{1,0},{2,3},{3,2},{4,5},{5,4},{6,7},{7,6},{8,9},{9,8},{10,11... | collective-permute-start | bytes 417800 | tf_op jit(solution)/shard_map/ppermute | solution.py:448
  29.1 4.2 %copy-start.1 = (bf16[8,4,8,128]{3,2,1,0:T(8,128)(2,1)S(1)}, bf16[8,4,8,128]{3,2,1,0:T(8,128)(2,1)}, u32[]{:S(2)}) copy-start(bf16[8,4,8,128]{3,2,1,0:T(8,128)(2,1)} %refs_13_.1) | copy-start | bytes 196612
  29.1 4.1 %copy-start.2 = (s32[8,4,32]{2,1,0:T(4,128)S(1)}, s32[8,4,32]{2,1,0:T(4,128)}, u32[]{:S(2)}) copy-start(s32[8,4,32]{2,1,0:T(4,128)} %refs_14_.1) | copy-start | bytes 12292
  29.1 4.1 %copy-start.3 = (s32[4,64]{1,0:T(4,128)S(1)}, s32[4,64]{1,0:T(4,128)}, u32[]{:S(2)}) copy-start(s32[4,64]{1,0:T(4,128)} %refs_4_.1) | copy-start | bytes 3076
  29.2 4.1 %copy-start.4 = (s32[8]{0:T(128)S(1)}, s32[8]{0:T(128)}, u32[]{:S(2)}) copy-start(s32[8]{0:T(128)} %refs_3_.1) | copy-start | bytes 100
  29.2 6.4 %collective-permute-start.9 = (bf16[272,256]{1,0:T(8,128)(2,1)S(1)}, bf16[272,256]{1,0:T(8,128)(2,1)S(1)}, u32[]{:S(2)}, u32[]{:S(2)}) collective-permute-start(bf16[272,256]{1,0:T(8,128)(2,1)S(1)} %shard_map.95), channel_id=1, source_target_pairs={{0,1},{1,0},{2,3},{3,2},{4,5},{5,4},{6,7},{7,6},{8,9},{9,8},{10,11... | collective-permute-start | bytes 417800 | tf_op jit(solution)/shard_map/ppermute | solution.py:448
  30.3 7.6 %collective-permute-start.11 = (bf16[272,256]{1,0:T(8,128)(2,1)S(1)}, bf16[272,256]{1,0:T(8,128)(2,1)S(1)}, u32[]{:S(2)}, u32[]{:S(2)}) collective-permute-start(bf16[272,256]{1,0:T(8,128)(2,1)S(1)} %shard_map.98), channel_id=1, source_target_pairs={{0,12},{1,13},{2,14},{3,15},{4,8},{5,9},{6,10},{7,11},{8,4},{9,5},... | collective-permute-start | bytes 417800 | tf_op jit(solution)/shard_map/ppermute | solution.py:448
  38.4 1.2 %collective-permute-start.12 = (f32[72,128]{1,0:T(8,128)S(1)}, f32[72,128]{1,0:T(8,128)S(1)}, u32[]{:S(2)}, u32[]{:S(2)}) collective-permute-start(f32[72,128]{1,0:T(8,128)S(1)} %get-tuple-element.77.own_ref), channel_id=1, source_target_pairs={{0,1},{1,0},{2,3},{3,2},{4,5},{5,4},{6,7},{7,6},{8,9},{9,8},{10,11... | collective-permute-start | bytes 110600 | tf_op jit(solution)/shard_map/ppermute | solution.py:448
  39.8 5.8 %collective-permute-start.13 = (f32[72,128]{1,0:T(8,128)S(1)}, f32[72,128]{1,0:T(8,128)S(1)}, u32[]{:S(2)}, u32[]{:S(2)}) collective-permute-start(f32[72,128]{1,0:T(8,128)S(1)} %shard_map.101.own_ref), channel_id=1, source_target_pairs={{0,12},{1,13},{2,14},{3,15},{4,8},{5,9},{6,10},{7,11},{8,4},{9,5},... | collective-permute-start | bytes 110600 | tf_op jit(solution)/shard_map/ppermute | solution.py:448
  45.7 4.0 %collective-permute-start.14 = (bf16[128,128]{1,0:T(8,128)(2,1)S(1)}, bf16[128,128]{1,0:T(8,128)(2,1)S(1)}, u32[]{:S(2)}, u32[]{:S(2)}) collective-permute-start(bf16[128,128]{1,0:T(8,128)(2,1)S(1)} %get-tuple-element.79), channel_id=1, source_target_pairs={{0,2},{1,3},{2,0},{3,1},{4,6},{5,7},{6,4},{7,5},{8,10},{9,11},{10,... | collective-permute-start | bytes 98312 | tf_op jit(solution)/shard_map/ppermute | solution.py:448
  47.2 3.9 %collective-permute-start.15 = (bf16[128,128]{1,0:T(8,128)(2,1)S(1)}, bf16[128,128]{1,0:T(8,128)(2,1)S(1)}, u32[]{:S(2)}, u32[]{:S(2)}) collective-permute-start(bf16[128,128]{1,0:T(8,128)(2,1)S(1)} %get-tuple-element.80), channel_id=1, source_target_pairs={{0,4},{1,5},{2,6},{3,7},{4,0},{5,1},{6,2},{7,3},{8,12},{9,13},{10,... | collective-permute-start | bytes 98312 | tf_op jit(solution)/shard_map/ppermute | solution.py:448
  48.2 4.8 %collective-permute-start.16 = (bf16[128,128]{1,0:T(8,128)(2,1)S(1)}, bf16[128,128]{1,0:T(8,128)(2,1)S(1)}, u32[]{:S(2)}, u32[]{:S(2)}) collective-permute-start(bf16[128,128]{1,0:T(8,128)(2,1)S(1)} %get-tuple-element.81), channel_id=1, source_target_pairs={{0,6},{1,7},{2,4},{3,5},{4,2},{5,3},{6,0},{7,1},{8,14},{9,15},{10,... | collective-permute-start | bytes 98312 | tf_op jit(solution)/shard_map/ppermute | solution.py:448

commit v7 on v6

--- a/solution.py
+++ b/solution.py
@@ -223,7 +223,7 @@
         inverse = 1.0 / (total_ref[0:1, chunk] + total)
         inverse_ref[:, chunk] = jnp.broadcast_to(inverse, (8, tokens))
         fill_weights(raised_ref, inverse, weight_ref, rows, rows, first, 0, mass_ref)
-        early_ref[:, chunk] = raised_ref[:rows, :tokens].astype(BF16)
+        early_ref[:, chunk] = raised_ref[:rows, :tokens]
         first += tokens
     masses = jnp.sum(mass_ref[...].T, axis=0, keepdims=True)
     send_ref[rows:, :] = packed_masses(masses, lanes)
@@ -270,15 +270,28 @@
     send_ref[half:, :] = packed_masses(masses[:, half:], lanes)
 
 
+def as_line(column, dim):
+    rows = column.shape[0]
+    square = [jnp.broadcast_to(column, (rows, dim)), jnp.zeros((dim - rows, dim), F32)]
+    return jnp.concatenate(square, axis=0).T[0:1, :]
+
+
 def packed_state(peak, weight_sum, weighted):
-    rows, dim = weighted.shape
-    lines = [
-        jnp.concatenate(
-            [jnp.broadcast_to(column, (rows, dim)), jnp.zeros((dim - rows, dim), F32)], axis=0
-        ).T[0:1, :]
-        for column in (peak, weight_sum)
-    ]
-    return jnp.concatenate([weighted, *lines, jnp.zeros((6, dim), F32)], axis=0)
+    dim = weighted.shape[1]
+    lines = [as_line(peak, dim), as_line(weight_sum, dim), jnp.zeros((6, dim), F32)]
+    return jnp.concatenate([weighted, *lines], axis=0)
+
+
+def sent_state(peak, weight_sum, weighted):
+    dim = weighted.shape[1]
+    lines = []
+    for column in (peak, weight_sum):
+        rest = as_line(column, dim)
+        for _ in range(3):
+            lines.append(rest.astype(BF16).astype(F32))
+            rest = rest - lines[-1]
+    lines.append(jnp.zeros((10, dim), F32))
+    return jnp.concatenate([weighted, *lines], axis=0).astype(BF16)
 
 
 def softmax_part(scores, usable, values):
@@ -300,11 +313,13 @@
 
 def unpacked_state(state):
     dim = state.shape[1]
-    rows = state.shape[0] - 8
-    columns = [
-        jnp.broadcast_to(state[rows + at : rows + at + 1, :], (dim, dim)).T[:rows, :]
-        for at in range(2)
-    ]
+    short = state.dtype == BF16
+    rows = state.shape[0] - (16 if short else 8)
+    state = state.astype(F32)
+    lines = [state[at : at + 1, :] for at in range(rows, rows + (6 if short else 2))]
+    if short:
+        lines = [lines[at] + lines[at + 1] + lines[at + 2] for at in (0, 3)]
+    columns = [jnp.broadcast_to(line, (dim, dim)).T[:rows, :] for line in lines]
     return columns[0], columns[1], state[:rows, :]
 
 
@@ -383,7 +398,7 @@
 
 def merge_kernel(flip_ref, own_ref, recv_ref, out_ref):
     former, latter = in_order(flip_ref[0] != 0, own_ref, recv_ref)
-    out_ref[...] = packed_state(*joined(unpacked_state(former), unpacked_state(latter)))
+    out_ref[...] = sent_state(*joined(unpacked_state(former), unpacked_state(latter)))
 
 
 def last_merge_kernel(flip_ref, head_ref, own_ref, recv_ref, cent_ref, attended_ref, *pack_refs):
@@ -509,7 +524,7 @@
     tokens = heads * tok_dev
     unit_keys, raised, total = call(
         functools.partial(own_half_kernel, heads),
-        [shape((tokens, dim), BF16), shape((half, tokens), BF16), shape((8, tokens), F32)],
+        [shape((tokens, dim), BF16), shape((half, tokens), F32), shape((8, tokens), F32)],
         [*keys, own_cents],
         (),
         pass_flops * heads // 4,
@@ -520,7 +535,7 @@
     kept = [shape((part, 2 * dim), F32), shape((8, part), F32)]
     send, inverse, early = call(
         functools.partial(other_half_kernel, heads),
-        [sent, shape((8, tokens), F32), shape((part, tokens), BF16)],
+        [sent, shape((8, tokens), F32), shape((part, tokens), F32)],
         [*keys, *values, unit_keys, other_cents, total],
         [pltpu.VMEM((half, tok_dev), F32), *part_scratch],
         pass_flops * heads // 2,
@@ -594,7 +609,7 @@
         flip = ((rank >> level) & 1).reshape(1)
         (state,) = call(
             merge_kernel,
-            [shape((rows + 8, dim), F32)],
+            [shape((rows + 16, dim), BF16)],
             [flip, state, over(state, rank_basis[level])],
             scalars=1,
         )

time: 53.8 us -> 53.7 us (level)
  no operation moved by 1% of the time
where the time goes in v7:
time: 53.7 us; the launch traced here: 53.6 us
  starting transfers between devices  23.4 us (44%)
  waiting for transfers between devices  15.7 us (29%)
  Pallas kernels  12.1 us (23%)
  local copies, waits for them, and re-layouts  1.49 us (3%)
  between operations  0.92 us (2%)
    ppermute x17, starting transfers between devices, over(): return lax.ppermute(array, 'ctx', [(i, i ^ bit) for i in range(devices)])  23.4 us
    ppermute x17, waiting for transfers between devices, over(): return lax.ppermute(array, 'ctx', [(i, i ^ bit) for i in range(devices)])  15.7 us
    pallas_call x18, Pallas kernels, call(): pl.pallas_call(kernel, out_shape=tuple(outs), in_specs=in_specs, out_spec...  12.1 us
    squeeze x1, local copies, waits for them, and re-layouts, pick(): return lax.dynamic_index_in_dim(array, at, axis, keepdims=False)  1.43 us
  transfers between devices with their start and end apart: 17, of which 10 were waited for; matrix products, arithmetic and copies ran while one was open for 0% of the time, Pallas kernels for 17%

profile of v7, /device:TPU:0, one launch (start us, length us, event | category | flops | bytes accessed | tf_op | source)
XLA Modules:
  0.0 53.6 jit_solution(10928731488867718795)
XLA Ops:
  0.7 1.4 %dynamic-slice_bitcast_fusion = (bf16[512,128]{1,0:T(8,128)(2,1)S(1)}, bf16[512,128]{1,0:T(8,128)(2,1)S(1)}, bf16[512,128]{1,0:T(8,128)(2,1)S(1)}, bf16[512,128]...) fusion(bf16[4,512,128]{2,1,0:T(8,128)(2,1)} %param.8, ...), kind=kLoop, calls=%fused_computation.1 | loop fusion | bytes 2097168 | tf_op jit(solution)/shard_map/jit(dynamic_index_in_dim)/squeeze | solution.py:466
  2.1 3.0 %collective-permute-start = (bf16[512,128]{1,0:T(8,128)(2,1)S(1)}, bf16[512,128]{1,0:T(8,128)(2,1)S(1)}, u32[]{:S(2)}, u32[]{:S(2)}) collective-permute-start(bf16[512,128]{1,0:T(8,128)(2,1)S(1)} %get-tuple-element.43), channel_id=1, source_target_pairs={{0,2},{1,3},{2,0},{3,1},{4,6},{5,7},{6,4},{7,5},{8,10},{9,11},{10,... | collective-permute-start | bytes 393224 | tf_op jit(solution)/shard_map/ppermute | solution.py:463
  5.2 1.6 %collective-permute-start.1 = (bf16[512,128]{1,0:T(8,128)(2,1)S(1)}, bf16[512,128]{1,0:T(8,128)(2,1)S(1)}, u32[]{:S(2)}, u32[]{:S(2)}) collective-permute-start(bf16[512,128]{1,0:T(8,128)(2,1)S(1)} %get-tuple-element.44), channel_id=1, source_target_pairs={{0,4},{1,5},{2,6},{3,7},{4,0},{5,1},{6,2},{7,3},{8,12},{9,13},{10,... | collective-permute-start | bytes 393224 | tf_op jit(solution)/shard_map/ppermute | solution.py:463
  6.7 2.9 %collective-permute-start.5 = (bf16[512,128]{1,0:T(8,128)(2,1)S(1)}, bf16[512,128]{1,0:T(8,128)(2,1)S(1)}, u32[]{:S(2)}, u32[]{:S(2)}) collective-permute-start(bf16[512,128]{1,0:T(8,128)(2,1)S(1)} %get-tuple-element.57), channel_id=1, source_target_pairs={{0,6},{1,7},{2,4},{3,5},{4,2},{5,3},{6,0},{7,1},{8,14},{9,15},{10,... | collective-permute-start | bytes 393224 | tf_op jit(solution)/shard_map/ppermute | solution.py:463
  9.7 1.0 %shard_map.86 = (f32[512,128]{1,0:T(8,128)S(1)}, bf16[512,512]{1,0:T(8,128)(2,1)S(1)}, bf16[1024,128]{1,0:T(8,128)(2,1)S(1)}) custom-call(s32[1]{0:T(128)} %bitcast.9.base_ref.refs_2_, bf16[512,128]{1,0:T(8,128)(2,1)S(1)} %get-tuple-element.42.refs_0_.refs_5_, bf16[16,64,128]{2,1,0:T(8,128)(2,1)S(1)} %bitcast.25), custom_call_target="tpu_custom_call" | custom-call | flops 268435456 | bytes 1441796 | tf_op jit(solution)/shard_map/pallas_call | solution.py:64
  10.8 1.0 %shard_map.87 = (f32[512,128]{1,0:T(8,128)S(1)}, bf16[512,512]{1,0:T(8,128)(2,1)S(1)}) custom-call(bf16[512,128]{1,0:T(8,128)(2,1)S(1)} %collective-permute-done.key_ref.refs_1_.refs_6_, bf16[1024,128]{1,0:T(8,128)(2,1)S(1)} %get-tuple-element.50.unit_ref, f32[512,128]{1,0:T(8,128)S(1)} %get-tuple-element.51.before_ref), custom_call_target="tpu_custom_call" | custom-call | flops 268435456 | bytes 1441792 | tf_op jit(solution)/shard_map/pallas_call | solution.py:64
  11.8 1.0 %shard_map.88 = (f32[512,128]{1,0:T(8,128)S(1)}, bf16[512,512]{1,0:T(8,128)(2,1)S(1)}) custom-call(bf16[512,128]{1,0:T(8,128)(2,1)S(1)} %collective-permute-done.1.key_ref.refs_2_.refs_7_, bf16[1024,128]{1,0:T(8,128)(2,1)S(1)} %get-tuple-element.50.unit_ref, f32[512,128]{1,0:T(8,128)S(1)} %get-tuple-element.53.before_ref), custom_call_target="tpu_custom_call" | custom-call | flops 268435456 | bytes 1441792 | tf_op jit(solution)/shard_map/pallas_call | solution.py:64
  12.8 1.3 %collective-permute-done.2.key_ref.refs_3_.refs_8_ = bf16[512,128]{1,0:T(8,128)(2,1)S(1)} collective-permute-done((bf16[512,128]{1,0:T(8,128)(2,1)S(1)}, bf16[512,128]{1,0:T(8,128)(2,1)S(1)}, u32[]{:S(2)}, u32[]{:S(2)}) %collective-permute-start.2) | collective-permute-done | bytes 131104 | tf_op jit(solution)/shard_map/ppermute | solution.py:463
  16.5 3.9 %collective-permute-start.7 = (bf16[512,128]{1,0:T(8,128)(2,1)S(1)}, bf16[512,128]{1,0:T(8,128)(2,1)S(1)}, u32[]{:S(2)}, u32[]{:S(2)}) collective-permute-start(bf16[512,128]{1,0:T(8,128)(2,1)S(1)} %add_convert_fusion.own_ref), channel_id=1, source_target_pairs={{0,12},{1,13},{2,14},{3,15},{4,8},{5,9},{6,10},{7,11},{8,4},{9,5},... | collective-permute-start | bytes 393224 | tf_op jit(solution)/shard_map/ppermute | solution.py:463
  20.4 1.5 %collective-permute-start.3 = (bf16[512,128]{1,0:T(8,128)(2,1)S(1)}, bf16[512,128]{1,0:T(8,128)(2,1)S(1)}, u32[]{:S(2)}, u32[]{:S(2)}) collective-permute-start(bf16[512,128]{1,0:T(8,128)(2,1)S(1)} %get-tuple-element.47), channel_id=1, source_target_pairs={{0,2},{1,3},{2,0},{3,1},{4,6},{5,7},{6,4},{7,5},{8,10},{9,11},{10,... | collective-permute-start | bytes 393224 | tf_op jit(solution)/shard_map/ppermute | solution.py:463
  21.9 2.8 %collective-permute-done.7.recv_ref = bf16[512,128]{1,0:T(8,128)(2,1)S(1)} collective-permute-done((bf16[512,128]{1,0:T(8,128)(2,1)S(1)}, bf16[512,128]{1,0:T(8,128)(2,1)S(1)}, u32[]{:S(2)}, u32[]{:S(2)}) %collective-permute-start.7) | collective-permute-done | bytes 131104 | tf_op jit(solution)/shard_map/ppermute | solution.py:463
  25.0 1.0 %shard_map.92 = (bf16[2048,128]{1,0:T(8,128)(2,1)S(1)}, f32[512,2048]{1,0:T(8,128)S(1)}, f32[8,2048]{1,0:T(8,128)S(1)}) custom-call(bf16[512,128]{1,0:T(8,128)(2,1)S(1)} %get-tuple-element.42.refs_0_.refs_5_, bf16[512,128]{1,0:T(8,128)(2,1)S(1)} %collective-permute-done.key_ref.refs_1_.refs_6_, ...), custom_call_target="tpu_custom_call" | custom-call | flops 268435456 | bytes 5439488 | tf_op jit(solution)/shard_map/pallas_call | solution.py:64
  26.0 1.2 %collective-permute-done.4.refs_6_.refs_11_ = bf16[512,128]{1,0:T(8,128)(2,1)S(1)} collective-permute-done((bf16[512,128]{1,0:T(8,128)(2,1)S(1)}, bf16[512,128]{1,0:T(8,128)(2,1)S(1)}, u32[]{:S(2)}, u32[]{:S(2)}) %collective-permute-start.4) | collective-permute-done | bytes 131104 | tf_op jit(solution)/shard_map/ppermute | solution.py:463
  27.2 1.3 %shard_map.93 = (bf16[272,256]{1,0:T(8,128)(2,1)S(1)}, f32[8,2048]{1,0:T(8,128)S(1)}, f32[256,2048]{1,0:T(8,128)S(1)}) custom-call(bf16[512,128]{1,0:T(8,128)(2,1)S(1)} %get-tuple-element.42.refs_0_.refs_5_, bf16[512,128]{1,0:T(8,128)(2,1)S(1)} %collective-permute-done.key_ref.refs_1_.refs_6_, ...), custom_call_target="tpu_custom_call" | custom-call | flops 536870912 | bytes 4071424 | tf_op jit(solution)/shard_map/pallas_call | solution.py:64
  30.3 3.0 %collective-permute-start.11 = (bf16[272,256]{1,0:T(8,128)(2,1)S(1)}, bf16[272,256]{1,0:T(8,128)(2,1)S(1)}, u32[]{:S(2)}, u32[]{:S(2)}) collective-permute-start(bf16[272,256]{1,0:T(8,128)(2,1)S(1)} %shard_map.98), channel_id=1, source_target_pairs={{0,12},{1,13},{2,14},{3,15},{4,8},{5,9},{6,10},{7,11},{8,4},{9,5},... | collective-permute-start | bytes 417800 | tf_op jit(solution)/shard_map/ppermute | solution.py:463
  33.3 1.7 %shard_map.99 = (f32[72,128]{1,0:T(8,128)S(1)}, f32[64,128]{1,0:T(8,128)S(1)}, f32[64,256]{1,0:T(8,128)S(1)}) custom-call(s32[1]{0:T(128)} %bitcast.refs_0_.head_ref, s32[1]{0:T(128)} %bitcast.11.refs_1_, s32[1]{0:T(128)} %bitcast.9.base_ref.refs_2_, s32[8]{0:T(128)S(1)} %copy-done.4, s32[4,64]{1,0:T(4,128)S(1)} %copy-done.3, ...), custom_call_target="tpu_custom_call" | custom-call | flops 67108864 | bytes 1254444 | tf_op jit(solution)/shard_map/pallas_call | solution.py:64
  35.6 2.3 %collective-permute-done.11.recv_ref = bf16[272,256]{1,0:T(8,128)(2,1)S(1)} collective-permute-done((bf16[272,256]{1,0:T(8,128)(2,1)S(1)}, bf16[272,256]{1,0:T(8,128)(2,1)S(1)}, u32[]{:S(2)}, u32[]{:S(2)}) %collective-permute-start.11) | collective-permute-done | bytes 139296 | tf_op jit(solution)/shard_map/ppermute | solution.py:463
  38.4 1.2 %collective-permute-done.12.recv_ref = f32[72,128]{1,0:T(8,128)S(1)} collective-permute-done((f32[72,128]{1,0:T(8,128)S(1)}, f32[72,128]{1,0:T(8,128)S(1)}, u32[]{:S(2)}, u32[]{:S(2)}) %collective-permute-start.12) | collective-permute-done | bytes 36896 | tf_op jit(solution)/shard_map/ppermute | solution.py:463
  39.8 3.1 %collective-permute-start.13 = (bf16[80,128]{1,0:T(8,128)(2,1)S(1)}, bf16[80,128]{1,0:T(8,128)(2,1)S(1)}, u32[]{:S(2)}, u32[]{:S(2)}) collective-permute-start(bf16[80,128]{1,0:T(8,128)(2,1)S(1)} %shard_map.101.own_ref), channel_id=1, source_target_pairs={{0,12},{1,13},{2,14},{3,15},{4,8},{5,9},{6,10},{7,11},{8,4},{9,5},... | collective-permute-start | bytes 61448 | tf_op jit(solution)/shard_map/ppermute | solution.py:463
  43.0 2.5 %collective-permute-done.13.recv_ref = bf16[80,128]{1,0:T(8,128)(2,1)S(1)} collective-permute-done((bf16[80,128]{1,0:T(8,128)(2,1)S(1)}, bf16[80,128]{1,0:T(8,128)(2,1)S(1)}, u32[]{:S(2)}, u32[]{:S(2)}) %collective-permute-start.13) | collective-permute-done | bytes 20512 | tf_op jit(solution)/shard_map/ppermute | solution.py:463
  45.6 1.5 %collective-permute-start.14 = (bf16[128,128]{1,0:T(8,128)(2,1)S(1)}, bf16[128,128]{1,0:T(8,128)(2,1)S(1)}, u32[]{:S(2)}, u32[]{:S(2)}) collective-permute-start(bf16[128,128]{1,0:T(8,128)(2,1)S(1)} %get-tuple-element.79), channel_id=1, source_target_pairs={{0,2},{1,3},{2,0},{3,1},{4,6},{5,7},{6,4},{7,5},{8,10},{9,11},{10,... | collective-permute-start | bytes 98312 | tf_op jit(solution)/shard_map/ppermute | solution.py:463
  48.1 1.1 %collective-permute-start.16 = (bf16[128,128]{1,0:T(8,128)(2,1)S(1)}, bf16[128,128]{1,0:T(8,128)(2,1)S(1)}, u32[]{:S(2)}, u32[]{:S(2)}) collective-permute-start(bf16[128,128]{1,0:T(8,128)(2,1)S(1)} %get-tuple-element.81), channel_id=1, source_target_pairs={{0,6},{1,7},{2,4},{3,5},{4,2},{5,3},{6,0},{7,1},{8,14},{9,15},{10,... | collective-permute-start | bytes 98312 | tf_op jit(solution)/shard_map/ppermute | solution.py:463
  49.6 1.4 %collective-permute-done.15.refs_1_ = bf16[128,128]{1,0:T(8,128)(2,1)S(1)} collective-permute-done((bf16[128,128]{1,0:T(8,128)(2,1)S(1)}, bf16[128,128]{1,0:T(8,128)(2,1)S(1)}, u32[]{:S(2)}, u32[]{:S(2)}) %collective-permute-start.15) | collective-permute-done | bytes 32800 | tf_op jit(solution)/shard_map/ppermute | solution.py:463
  51.0 1.9 %collective-permute-done.16.refs_2_ = bf16[128,128]{1,0:T(8,128)(2,1)S(1)} collective-permute-done((bf16[128,128]{1,0:T(8,128)(2,1)S(1)}, bf16[128,128]{1,0:T(8,128)(2,1)S(1)}, u32[]{:S(2)}, u32[]{:S(2)}) %collective-permute-start.16) | collective-permute-done | bytes 32800 | tf_op jit(solution)/shard_map/ppermute | solution.py:463
  (41 shorter events, 7.9 us)
Async XLA Ops:
  0.6 9.0 %copy-start = (bf16[4,1024,128]{2,1,0:T(8,128)(2,1)S(1)}, bf16[4,1024,128]{2,1,0:T(8,128)(2,1)}, u32[]{:S(2)}) copy-start(bf16[4,1024,128]{2,1,0:T(8,128)(2,1)} %param.9) | copy-start | bytes 3145732
  2.1 8.6 %collective-permute-start = (bf16[512,128]{1,0:T(8,128)(2,1)S(1)}, bf16[512,128]{1,0:T(8,128)(2,1)S(1)}, u32[]{:S(2)}, u32[]{:S(2)}) collective-permute-start(bf16[512,128]{1,0:T(8,128)(2,1)S(1)} %get-tuple-element.43), channel_id=1, source_target_pairs={{0,2},{1,3},{2,0},{3,1},{4,6},{5,7},{6,4},{7,5},{8,10},{9,11},{10,... | collective-permute-start | bytes 393224 | tf_op jit(solution)/shard_map/ppermute | solution.py:463
  5.2 6.6 %collective-permute-start.1 = (bf16[512,128]{1,0:T(8,128)(2,1)S(1)}, bf16[512,128]{1,0:T(8,128)(2,1)S(1)}, u32[]{:S(2)}, u32[]{:S(2)}) collective-permute-start(bf16[512,128]{1,0:T(8,128)(2,1)S(1)} %get-tuple-element.44), channel_id=1, source_target_pairs={{0,4},{1,5},{2,6},{3,7},{4,0},{5,1},{6,2},{7,3},{8,12},{9,13},{10,... | collective-permute-start | bytes 393224 | tf_op jit(solution)/shard_map/ppermute | solution.py:463
  6.7 7.3 %collective-permute-start.2 = (bf16[512,128]{1,0:T(8,128)(2,1)S(1)}, bf16[512,128]{1,0:T(8,128)(2,1)S(1)}, u32[]{:S(2)}, u32[]{:S(2)}) collective-permute-start(bf16[512,128]{1,0:T(8,128)(2,1)S(1)} %get-tuple-element.45), channel_id=1, source_target_pairs={{0,6},{1,7},{2,4},{3,5},{4,2},{5,3},{6,0},{7,1},{8,14},{9,15},{10,... | collective-permute-start | bytes 393224 | tf_op jit(solution)/shard_map/ppermute | solution.py:463
  6.7 9.1 %collective-permute-start.5 = (bf16[512,128]{1,0:T(8,128)(2,1)S(1)}, bf16[512,128]{1,0:T(8,128)(2,1)S(1)}, u32[]{:S(2)}, u32[]{:S(2)}) collective-permute-start(bf16[512,128]{1,0:T(8,128)(2,1)S(1)} %get-tuple-element.57), channel_id=1, source_target_pairs={{0,6},{1,7},{2,4},{3,5},{4,2},{5,3},{6,0},{7,1},{8,14},{9,15},{10,... | collective-permute-start | bytes 393224 | tf_op jit(solution)/shard_map/ppermute | solution.py:463
  15.1 1.4 %collective-permute-start.6 = (bf16[512,128]{1,0:T(8,128)(2,1)S(1)}, bf16[512,128]{1,0:T(8,128)(2,1)S(1)}, u32[]{:S(2)}, u32[]{:S(2)}) collective-permute-start(bf16[512,128]{1,0:T(8,128)(2,1)S(1)} %get-tuple-element.60), channel_id=1, source_target_pairs={{0,1},{1,0},{2,3},{3,2},{4,5},{5,4},{6,7},{7,6},{8,9},{9,8},{10,11... | collective-permute-start | bytes 393224 | tf_op jit(solution)/shard_map/ppermute | solution.py:463
  16.5 8.2 %collective-permute-start.7 = (bf16[512,128]{1,0:T(8,128)(2,1)S(1)}, bf16[512,128]{1,0:T(8,128)(2,1)S(1)}, u32[]{:S(2)}, u32[]{:S(2)}) collective-permute-start(bf16[512,128]{1,0:T(8,128)(2,1)S(1)} %add_convert_fusion.own_ref), channel_id=1, source_target_pairs={{0,12},{1,13},{2,14},{3,15},{4,8},{5,9},{6,10},{7,11},{8,4},{9,5},... | collective-permute-start | bytes 393224 | tf_op jit(solution)/shard_map/ppermute | solution.py:463
  20.4 5.6 %collective-permute-start.3 = (bf16[512,128]{1,0:T(8,128)(2,1)S(1)}, bf16[512,128]{1,0:T(8,128)(2,1)S(1)}, u32[]{:S(2)}, u32[]{:S(2)}) collective-permute-start(bf16[512,128]{1,0:T(8,128)(2,1)S(1)} %get-tuple-element.47), channel_id=1, source_target_pairs={{0,2},{1,3},{2,0},{3,1},{4,6},{5,7},{6,4},{7,5},{8,10},{9,11},{10,... | collective-permute-start | bytes 393224 | tf_op jit(solution)/shard_map/ppermute | solution.py:463
  21.9 5.3 %collective-permute-start.4 = (bf16[512,128]{1,0:T(8,128)(2,1)S(1)}, bf16[512,128]{1,0:T(8,128)(2,1)S(1)}, u32[]{:S(2)}, u32[]{:S(2)}) collective-permute-start(bf16[512,128]{1,0:T(8,128)(2,1)S(1)} %get-tuple-element.48), channel_id=1, source_target_pairs={{0,4},{1,5},{2,6},{3,7},{4,0},{5,1},{6,2},{7,3},{8,12},{9,13},{10,... | collective-permute-start | bytes 393224 | tf_op jit(solution)/shard_map/ppermute | solution.py:463
  24.9 2.3 %collective-permute-start.8 = (bf16[512,128]{1,0:T(8,128)(2,1)S(1)}, bf16[512,128]{1,0:T(8,128)(2,1)S(1)}, u32[]{:S(2)}, u32[]{:S(2)}) collective-permute-start(bf16[512,128]{1,0:T(8,128)(2,1)S(1)} %shard_map.91.refs_4_), channel_id=1, source_target_pairs={{0,1},{1,0},{2,3},{3,2},{4,5},{5,4},{6,7},{7,6},{8,9},{9,8},{10,11... | collective-permute-start | bytes 393224 | tf_op jit(solution)/shard_map/ppermute | solution.py:463
  28.5 1.7 %collective-permute-start.10 = (bf16[272,256]{1,0:T(8,128)(2,1)S(1)}, bf16[272,256]{1,0:T(8,128)(2,1)S(1)}, u32[]{:S(2)}, u32[]{:S(2)}) collective-permute-start(bf16[272,256]{1,0:T(8,128)(2,1)S(1)} %get-tuple-element.72), channel_id=1, source_target_pairs={{0,1},{1,0},{2,3},{3,2},{4,5},{5,4},{6,7},{7,6},{8,9},{9,8},{10,11... | collective-permute-start | bytes 417800 | tf_op jit(solution)/shard_map/ppermute | solution.py:463
  28.6 4.7 %copy-start.1 = (bf16[8,4,8,128]{3,2,1,0:T(8,128)(2,1)S(1)}, bf16[8,4,8,128]{3,2,1,0:T(8,128)(2,1)}, u32[]{:S(2)}) copy-start(bf16[8,4,8,128]{3,2,1,0:T(8,128)(2,1)} %refs_13_.1) | copy-start | bytes 196612
  28.6 4.6 %copy-start.2 = (s32[8,4,32]{2,1,0:T(4,128)S(1)}, s32[8,4,32]{2,1,0:T(4,128)}, u32[]{:S(2)}) copy-start(s32[8,4,32]{2,1,0:T(4,128)} %refs_14_.1) | copy-start | bytes 12292
  28.6 4.6 %copy-start.3 = (s32[4,64]{1,0:T(4,128)S(1)}, s32[4,64]{1,0:T(4,128)}, u32[]{:S(2)}) copy-start(s32[4,64]{1,0:T(4,128)} %refs_4_.1) | copy-start | bytes 3076
  28.7 4.6 %copy-start.4 = (s32[8]{0:T(128)S(1)}, s32[8]{0:T(128)}, u32[]{:S(2)}) copy-start(s32[8]{0:T(128)} %refs_3_.1) | copy-start | bytes 100
  29.2 6.4 %collective-permute-start.9 = (bf16[272,256]{1,0:T(8,128)(2,1)S(1)}, bf16[272,256]{1,0:T(8,128)(2,1)S(1)}, u32[]{:S(2)}, u32[]{:S(2)}) collective-permute-start(bf16[272,256]{1,0:T(8,128)(2,1)S(1)} %shard_map.95), channel_id=1, source_target_pairs={{0,1},{1,0},{2,3},{3,2},{4,5},{5,4},{6,7},{7,6},{8,9},{9,8},{10,11... | collective-permute-start | bytes 417800 | tf_op jit(solution)/shard_map/ppermute | solution.py:463
  30.3 7.6 %collective-permute-start.11 = (bf16[272,256]{1,0:T(8,128)(2,1)S(1)}, bf16[272,256]{1,0:T(8,128)(2,1)S(1)}, u32[]{:S(2)}, u32[]{:S(2)}) collective-permute-start(bf16[272,256]{1,0:T(8,128)(2,1)S(1)} %shard_map.98), channel_id=1, source_target_pairs={{0,12},{1,13},{2,14},{3,15},{4,8},{5,9},{6,10},{7,11},{8,4},{9,5},... | collective-permute-start | bytes 417800 | tf_op jit(solution)/shard_map/ppermute | solution.py:463
  38.4 1.2 %collective-permute-start.12 = (f32[72,128]{1,0:T(8,128)S(1)}, f32[72,128]{1,0:T(8,128)S(1)}, u32[]{:S(2)}, u32[]{:S(2)}) collective-permute-start(f32[72,128]{1,0:T(8,128)S(1)} %get-tuple-element.77.own_ref), channel_id=1, source_target_pairs={{0,1},{1,0},{2,3},{3,2},{4,5},{5,4},{6,7},{7,6},{8,9},{9,8},{10,11... | collective-permute-start | bytes 110600 | tf_op jit(solution)/shard_map/ppermute | solution.py:463
  39.8 5.6 %collective-permute-start.13 = (bf16[80,128]{1,0:T(8,128)(2,1)S(1)}, bf16[80,128]{1,0:T(8,128)(2,1)S(1)}, u32[]{:S(2)}, u32[]{:S(2)}) collective-permute-start(bf16[80,128]{1,0:T(8,128)(2,1)S(1)} %shard_map.101.own_ref), channel_id=1, source_target_pairs={{0,12},{1,13},{2,14},{3,15},{4,8},{5,9},{6,10},{7,11},{8,4},{9,5},... | collective-permute-start | bytes 61448 | tf_op jit(solution)/shard_map/ppermute | solution.py:463
  45.6 4.0 %collective-permute-start.14 = (bf16[128,128]{1,0:T(8,128)(2,1)S(1)}, bf16[128,128]{1,0:T(8,128)(2,1)S(1)}, u32[]{:S(2)}, u32[]{:S(2)}) collective-permute-start(bf16[128,128]{1,0:T(8,128)(2,1)S(1)} %get-tuple-element.79), channel_id=1, source_target_pairs={{0,2},{1,3},{2,0},{3,1},{4,6},{5,7},{6,4},{7,5},{8,10},{9,11},{10,... | collective-permute-start | bytes 98312 | tf_op jit(solution)/shard_map/ppermute | solution.py:463
  47.1 3.9 %collective-permute-start.15 = (bf16[128,128]{1,0:T(8,128)(2,1)S(1)}, bf16[128,128]{1,0:T(8,128)(2,1)S(1)}, u32[]{:S(2)}, u32[]{:S(2)}) collective-permute-start(bf16[128,128]{1,0:T(8,128)(2,1)S(1)} %get-tuple-element.80), channel_id=1, source_target_pairs={{0,4},{1,5},{2,6},{3,7},{4,0},{5,1},{6,2},{7,3},{8,12},{9,13},{10,... | collective-permute-start | bytes 98312 | tf_op jit(solution)/shard_map/ppermute | solution.py:463
  48.1 4.8 %collective-permute-start.16 = (bf16[128,128]{1,0:T(8,128)(2,1)S(1)}, bf16[128,128]{1,0:T(8,128)(2,1)S(1)}, u32[]{:S(2)}, u32[]{:S(2)}) collective-permute-start(bf16[128,128]{1,0:T(8,128)(2,1)S(1)} %get-tuple-element.81), channel_id=1, source_target_pairs={{0,6},{1,7},{2,4},{3,5},{4,2},{5,3},{6,0},{7,1},{8,14},{9,15},{10,... | collective-permute-start | bytes 98312 | tf_op jit(solution)/shard_map/ppermute | solution.py:463

commit v8 on v7

--- a/solution.py
+++ b/solution.py
@@ -125,7 +125,8 @@
     key_ref,
     cent_ref,
     sums_ref,
-    keep_weight_ref,
+    keep_raised_ref,
+    inverse_ref,
     unit_ref,
     cents_ref,
     raised_ref,
@@ -137,22 +138,34 @@
             F32
         )
     unit_ref[...] = to_unit(cents_ref[...]).astype(BF16)
-    pass_chunk(key_ref, unit_ref, None, sums_ref, keep_weight_ref, raised_ref, weight_ref)
-
-
-def pass_chunk(key_ref, unit_ref, before_ref, sums_ref, keep_weight_ref, raised_ref, weight_ref):
+    pass_chunk(
+        key_ref, unit_ref, None, sums_ref, keep_raised_ref, inverse_ref, raised_ref, weight_ref
+    )
+
+
+def pass_chunk(
+    key_ref, unit_ref, before_ref, sums_ref, keep_raised_ref, inverse_ref, raised_ref, weight_ref
+):
     keys = key_ref[...]
     half = sums_ref.shape[0]
-    inverse = 1.0 / fill_raised(unit_ref, to_unit(keys).astype(BF16), raised_ref, 0, 0)
-    fill_weights(raised_ref, inverse, weight_ref, half, half, 0, 0, None)
-    fill_weights(raised_ref, inverse, keep_weight_ref, half, 0, 0, 0, None)
+    unit_keys = to_unit(keys).astype(BF16)
+    total = fill_raised(unit_ref.at[pl.ds(0, half)], unit_keys, keep_raised_ref, 0, 0)
+    total = total + fill_raised(unit_ref.at[pl.ds(half, half)], unit_keys, raised_ref, 0, 0)
+    inverse = 1.0 / total
+    inverse_ref[...] = jnp.broadcast_to(inverse, inverse_ref.shape)
+    fill_weights(raised_ref, inverse, weight_ref, half, 0, 0, 0, None)
     product(sums_ref, weight_ref, keys, before_ref)
 
 
 def keep_kernel(count, *refs):
-    key_refs, weight_refs, keep_ref = refs[:count], refs[count : 2 * count], refs[-1]
-    weights = jnp.concatenate([ref[...] for ref in weight_refs], axis=1)
-    keep_ref[...] = jnp.dot(weights, joined_rows(key_refs), preferred_element_type=F32)
+    key_refs, raised_refs, inverse_refs = refs[:count], refs[count : 2 * count], refs[2 * count : 3 * count]
+    keep_ref, weight_ref = refs[3 * count :]
+    first = 0
+    for raised_ref, inverse_ref in zip(raised_refs, inverse_refs):
+        rows, tokens = raised_ref.shape
+        fill_weights(raised_ref, inverse_ref[0:1, :], weight_ref, rows, 0, first, 0, None)
+        first += tokens
+    product(keep_ref, weight_ref, joined_rows(key_refs))
 
 
 def joined_rows(refs):
@@ -475,12 +488,13 @@
     scalar_base = base.reshape(1)
 
     pass_flops = 4 * tok_dev * clusters * dim
-    chunk_scratch = [pltpu.VMEM((clusters, tok_dev), F32), pltpu.VMEM((half, tok_dev), BF16)]
-    sums, keep_weights, unit_cents = call(
+    chunk_scratch = [pltpu.VMEM((half, tok_dev), F32), pltpu.VMEM((half, tok_dev), BF16)]
+    sums, raised, inverse, unit_cents = call(
         lambda base_ref, *refs: first_kernel(base_ref, order, *refs),
         [
             shape((half, dim), F32),
-            shape((half, tok_dev), BF16),
+            shape((half, tok_dev), F32),
+            shape((8, tok_dev), F32),
             shape((clusters, dim), BF16),
         ],
         [scalar_base, keys[0], blocks],
@@ -490,22 +504,27 @@
     )
     values = [slices[heads]] + [over(slices[heads + s], head_masks[s]) for s in range(1, heads)]
 
-    keep_weights = [keep_weights]
+    kept_raised, inverses = [raised], [inverse]
     for step in range(1, heads):
-        sums, kept = call(
+        sums, raised, inverse = call(
             pass_chunk,
-            [shape((half, dim), F32 if step < heads - 1 else BF16), shape((half, tok_dev), BF16)],
+            [
+                shape((half, dim), F32 if step < heads - 1 else BF16),
+                shape((half, tok_dev), F32),
+                shape((8, tok_dev), F32),
+            ],
             [keys[step], unit_cents, sums],
             chunk_scratch,
             pass_flops,
         )
-        keep_weights.append(kept)
+        kept_raised.append(raised)
+        inverses.append(inverse)
     send = sums
     (keep,) = call(
         functools.partial(keep_kernel, heads),
         [shape((half, dim), F32)],
-        [*keys, *keep_weights],
-        (),
+        [*keys, *kept_raised, *inverses],
+        [pltpu.VMEM((half, heads * tok_dev), BF16)],
         pass_flops * heads // 4,
     )
     keep, values[3] = lax.optimization_barrier((keep, values[3]))

time: 53.7 us -> 53.6 us (level)
  Pallas kernels: 12.1 us -> 11.5 us
    pallas_call x18, Pallas kernels: 12.1 us -> 11.5 us  [call(): pl.pallas_call(kernel, out_shape=tuple(outs), in_specs=in_specs, out_spec...]
  transfers between devices with their start and end apart: 17 -> 17, of which waited for: 10 -> 11; matrix products, arithmetic and copies ran while one was open for 0% -> 0% of each run, Pallas kernels for 17% -> 16%
where the time goes in v8:
time: 53.6 us; the launch traced here: 53.4 us
  starting transfers between devices  23.4 us (44%)
  waiting for transfers between devices  16.1 us (30%)
  Pallas kernels  11.5 us (21%)
  local copies, waits for them, and re-layouts  1.49 us (3%)
  between operations  0.92 us (2%)
    ppermute x17, starting transfers between devices, over(): return lax.ppermute(array, 'ctx', [(i, i ^ bit) for i in range(devices)])  23.4 us
    ppermute x17, waiting for transfers between devices, over(): return lax.ppermute(array, 'ctx', [(i, i ^ bit) for i in range(devices)])  16.1 us
    pallas_call x18, Pallas kernels, call(): pl.pallas_call(kernel, out_shape=tuple(outs), in_specs=in_specs, out_spec...  11.5 us
    squeeze x1, local copies, waits for them, and re-layouts, pick(): return lax.dynamic_index_in_dim(array, at, axis, keepdims=False)  1.43 us
  transfers between devices with their start and end apart: 17, of which 11 were waited for; matrix products, arithmetic and copies ran while one was open for 0% of the time, Pallas kernels for 16%

profile of v8, /device:TPU:0, one launch (start us, length us, event | category | flops | bytes accessed | tf_op | source)
XLA Modules:
  0.0 53.4 jit_solution(1740501171783013626)
XLA Ops:
  0.7 1.4 %dynamic-slice_bitcast_fusion = (bf16[512,128]{1,0:T(8,128)(2,1)S(1)}, bf16[512,128]{1,0:T(8,128)(2,1)S(1)}, bf16[512,128]{1,0:T(8,128)(2,1)S(1)}, bf16[512,128]...) fusion(bf16[4,512,128]{2,1,0:T(8,128)(2,1)} %param.8, ...), kind=kLoop, calls=%fused_computation.1 | loop fusion | bytes 2097168 | tf_op jit(solution)/shard_map/jit(dynamic_index_in_dim)/squeeze | solution.py:479
  2.1 3.0 %collective-permute-start = (bf16[512,128]{1,0:T(8,128)(2,1)S(1)}, bf16[512,128]{1,0:T(8,128)(2,1)S(1)}, u32[]{:S(2)}, u32[]{:S(2)}) collective-permute-start(bf16[512,128]{1,0:T(8,128)(2,1)S(1)} %get-tuple-element.47), channel_id=1, source_target_pairs={{0,2},{1,3},{2,0},{3,1},{4,6},{5,7},{6,4},{7,5},{8,10},{9,11},{10,... | collective-permute-start | bytes 393224 | tf_op jit(solution)/shard_map/ppermute | solution.py:476
  5.2 1.6 %collective-permute-start.1 = (bf16[512,128]{1,0:T(8,128)(2,1)S(1)}, bf16[512,128]{1,0:T(8,128)(2,1)S(1)}, u32[]{:S(2)}, u32[]{:S(2)}) collective-permute-start(bf16[512,128]{1,0:T(8,128)(2,1)S(1)} %get-tuple-element.48), channel_id=1, source_target_pairs={{0,4},{1,5},{2,6},{3,7},{4,0},{5,1},{6,2},{7,3},{8,12},{9,13},{10,... | collective-permute-start | bytes 393224 | tf_op jit(solution)/shard_map/ppermute | solution.py:476
  6.7 2.9 %collective-permute-start.5 = (bf16[512,128]{1,0:T(8,128)(2,1)S(1)}, bf16[512,128]{1,0:T(8,128)(2,1)S(1)}, u32[]{:S(2)}, u32[]{:S(2)}) collective-permute-start(bf16[512,128]{1,0:T(8,128)(2,1)S(1)} %get-tuple-element.65), channel_id=1, source_target_pairs={{0,6},{1,7},{2,4},{3,5},{4,2},{5,3},{6,0},{7,1},{8,14},{9,15},{10,... | collective-permute-start | bytes 393224 | tf_op jit(solution)/shard_map/ppermute | solution.py:476
  9.7 0.9 %shard_map.86 = (f32[512,128]{1,0:T(8,128)S(1)}, f32[512,512]{1,0:T(8,128)S(1)}, f32[8,512]{1,0:T(8,128)S(1)}, bf16[1024,128]{1,0:T(8,128)(2,1)S(1)}) custom-call(s32[1]{0:T(128)} %bitcast.9.base_ref.refs_2_, bf16[512,128]{1,0:T(8,128)(2,1)S(1)} %get-tuple-element.46.refs_0_.refs_5_, bf16[16,64,128]{2,1,0:T(8,128)(2,1)S(1)} %bitcast.25), custom_call_target="tpu_custom_call" | custom-call | flops 268435456 | bytes 1982468 | tf_op jit(solution)/shard_map/pallas_call | solution.py:64
  10.6 0.9 %shard_map.87 = (f32[512,128]{1,0:T(8,128)S(1)}, f32[512,512]{1,0:T(8,128)S(1)}, f32[8,512]{1,0:T(8,128)S(1)}) custom-call(bf16[512,128]{1,0:T(8,128)(2,1)S(1)} %collective-permute-done.key_ref.refs_1_.refs_6_, bf16[1024,128]{1,0:T(8,128)(2,1)S(1)} %get-tuple-element.54.unit_ref, f32[512,128]{1,0:T(8,128)S(1)} %get-tuple-element.55.before_ref), custom_call_target="tpu_custom_call" | custom-call | flops 268435456 | bytes 1982464 | tf_op jit(solution)/shard_map/pallas_call | solution.py:64
  12.4 1.6 %collective-permute-done.2.key_ref.refs_3_.refs_8_ = bf16[512,128]{1,0:T(8,128)(2,1)S(1)} collective-permute-done((bf16[512,128]{1,0:T(8,128)(2,1)S(1)}, bf16[512,128]{1,0:T(8,128)(2,1)S(1)}, u32[]{:S(2)}, u32[]{:S(2)}) %collective-permute-start.2) | collective-permute-done | bytes 131104 | tf_op jit(solution)/shard_map/ppermute | solution.py:476
  16.4 3.9 %collective-permute-start.7 = (bf16[512,128]{1,0:T(8,128)(2,1)S(1)}, bf16[512,128]{1,0:T(8,128)(2,1)S(1)}, u32[]{:S(2)}, u32[]{:S(2)}) collective-permute-start(bf16[512,128]{1,0:T(8,128)(2,1)S(1)} %add_convert_fusion.own_ref), channel_id=1, source_target_pairs={{0,12},{1,13},{2,14},{3,15},{4,8},{5,9},{6,10},{7,11},{8,4},{9,5},... | collective-permute-start | bytes 393224 | tf_op jit(solution)/shard_map/ppermute | solution.py:476
  20.2 1.5 %collective-permute-start.3 = (bf16[512,128]{1,0:T(8,128)(2,1)S(1)}, bf16[512,128]{1,0:T(8,128)(2,1)S(1)}, u32[]{:S(2)}, u32[]{:S(2)}) collective-permute-start(bf16[512,128]{1,0:T(8,128)(2,1)S(1)} %get-tuple-element.51), channel_id=1, source_target_pairs={{0,2},{1,3},{2,0},{3,1},{4,6},{5,7},{6,4},{7,5},{8,10},{9,11},{10,... | collective-permute-start | bytes 393224 | tf_op jit(solution)/shard_map/ppermute | solution.py:476
  21.8 2.8 %collective-permute-done.7.recv_ref = bf16[512,128]{1,0:T(8,128)(2,1)S(1)} collective-permute-done((bf16[512,128]{1,0:T(8,128)(2,1)S(1)}, bf16[512,128]{1,0:T(8,128)(2,1)S(1)}, u32[]{:S(2)}, u32[]{:S(2)}) %collective-permute-start.7) | collective-permute-done | bytes 131104 | tf_op jit(solution)/shard_map/ppermute | solution.py:476
  24.8 1.0 %shard_map.92 = (bf16[2048,128]{1,0:T(8,128)(2,1)S(1)}, f32[512,2048]{1,0:T(8,128)S(1)}, f32[8,2048]{1,0:T(8,128)S(1)}) custom-call(bf16[512,128]{1,0:T(8,128)(2,1)S(1)} %get-tuple-element.46.refs_0_.refs_5_, bf16[512,128]{1,0:T(8,128)(2,1)S(1)} %collective-permute-done.key_ref.refs_1_.refs_6_, ...), custom_call_target="tpu_custom_call" | custom-call | flops 268435456 | bytes 5439488 | tf_op jit(solution)/shard_map/pallas_call | solution.py:64
  25.8 1.2 %collective-permute-done.4.refs_6_.refs_11_ = bf16[512,128]{1,0:T(8,128)(2,1)S(1)} collective-permute-done((bf16[512,128]{1,0:T(8,128)(2,1)S(1)}, bf16[512,128]{1,0:T(8,128)(2,1)S(1)}, u32[]{:S(2)}, u32[]{:S(2)}) %collective-permute-start.4) | collective-permute-done | bytes 131104 | tf_op jit(solution)/shard_map/ppermute | solution.py:476
  27.1 1.3 %shard_map.93 = (bf16[272,256]{1,0:T(8,128)(2,1)S(1)}, f32[8,2048]{1,0:T(8,128)S(1)}, f32[256,2048]{1,0:T(8,128)S(1)}) custom-call(bf16[512,128]{1,0:T(8,128)(2,1)S(1)} %get-tuple-element.46.refs_0_.refs_5_, bf16[512,128]{1,0:T(8,128)(2,1)S(1)} %collective-permute-done.key_ref.refs_1_.refs_6_, ...), custom_call_target="tpu_custom_call" | custom-call | flops 536870912 | bytes 4071424 | tf_op jit(solution)/shard_map/pallas_call | solution.py:64
  30.1 3.0 %collective-permute-start.11 = (bf16[272,256]{1,0:T(8,128)(2,1)S(1)}, bf16[272,256]{1,0:T(8,128)(2,1)S(1)}, u32[]{:S(2)}, u32[]{:S(2)}) collective-permute-start(bf16[272,256]{1,0:T(8,128)(2,1)S(1)} %shard_map.98), channel_id=1, source_target_pairs={{0,12},{1,13},{2,14},{3,15},{4,8},{5,9},{6,10},{7,11},{8,4},{9,5},... | collective-permute-start | bytes 417800 | tf_op jit(solution)/shard_map/ppermute | solution.py:476
  33.1 1.7 %shard_map.99 = (f32[72,128]{1,0:T(8,128)S(1)}, f32[64,128]{1,0:T(8,128)S(1)}, f32[64,256]{1,0:T(8,128)S(1)}) custom-call(s32[1]{0:T(128)} %bitcast.refs_0_.head_ref, s32[1]{0:T(128)} %bitcast.11.refs_1_, s32[1]{0:T(128)} %bitcast.9.base_ref.refs_2_, s32[8]{0:T(128)S(1)} %copy-done.4, s32[4,64]{1,0:T(4,128)S(1)} %copy-done.3, ...), custom_call_target="tpu_custom_call" | custom-call | flops 67108864 | bytes 1254444 | tf_op jit(solution)/shard_map/pallas_call | solution.py:64
  35.5 2.3 %collective-permute-done.11.recv_ref = bf16[272,256]{1,0:T(8,128)(2,1)S(1)} collective-permute-done((bf16[272,256]{1,0:T(8,128)(2,1)S(1)}, bf16[272,256]{1,0:T(8,128)(2,1)S(1)}, u32[]{:S(2)}, u32[]{:S(2)}) %collective-permute-start.11) | collective-permute-done | bytes 139296 | tf_op jit(solution)/shard_map/ppermute | solution.py:476
  38.3 1.2 %collective-permute-done.12.recv_ref = f32[72,128]{1,0:T(8,128)S(1)} collective-permute-done((f32[72,128]{1,0:T(8,128)S(1)}, f32[72,128]{1,0:T(8,128)S(1)}, u32[]{:S(2)}, u32[]{:S(2)}) %collective-permute-start.12) | collective-permute-done | bytes 36896 | tf_op jit(solution)/shard_map/ppermute | solution.py:476
  39.7 3.1 %collective-permute-start.13 = (bf16[80,128]{1,0:T(8,128)(2,1)S(1)}, bf16[80,128]{1,0:T(8,128)(2,1)S(1)}, u32[]{:S(2)}, u32[]{:S(2)}) collective-permute-start(bf16[80,128]{1,0:T(8,128)(2,1)S(1)} %shard_map.101.own_ref), channel_id=1, source_target_pairs={{0,12},{1,13},{2,14},{3,15},{4,8},{5,9},{6,10},{7,11},{8,4},{9,5},... | collective-permute-start | bytes 61448 | tf_op jit(solution)/shard_map/ppermute | solution.py:476
  42.8 2.5 %collective-permute-done.13.recv_ref = bf16[80,128]{1,0:T(8,128)(2,1)S(1)} collective-permute-done((bf16[80,128]{1,0:T(8,128)(2,1)S(1)}, bf16[80,128]{1,0:T(8,128)(2,1)S(1)}, u32[]{:S(2)}, u32[]{:S(2)}) %collective-permute-start.13) | collective-permute-done | bytes 20512 | tf_op jit(solution)/shard_map/ppermute | solution.py:476
  45.5 1.5 %collective-permute-start.14 = (bf16[128,128]{1,0:T(8,128)(2,1)S(1)}, bf16[128,128]{1,0:T(8,128)(2,1)S(1)}, u32[]{:S(2)}, u32[]{:S(2)}) collective-permute-start(bf16[128,128]{1,0:T(8,128)(2,1)S(1)} %get-tuple-element.87), channel_id=1, source_target_pairs={{0,2},{1,3},{2,0},{3,1},{4,6},{5,7},{6,4},{7,5},{8,10},{9,11},{10,... | collective-permute-start | bytes 98312 | tf_op jit(solution)/shard_map/ppermute | solution.py:476
  46.9 1.0 %collective-permute-start.15 = (bf16[128,128]{1,0:T(8,128)(2,1)S(1)}, bf16[128,128]{1,0:T(8,128)(2,1)S(1)}, u32[]{:S(2)}, u32[]{:S(2)}) collective-permute-start(bf16[128,128]{1,0:T(8,128)(2,1)S(1)} %get-tuple-element.88), channel_id=1, source_target_pairs={{0,4},{1,5},{2,6},{3,7},{4,0},{5,1},{6,2},{7,3},{8,12},{9,13},{10,... | collective-permute-start | bytes 98312 | tf_op jit(solution)/shard_map/ppermute | solution.py:476
  47.9 1.1 %collective-permute-start.16 = (bf16[128,128]{1,0:T(8,128)(2,1)S(1)}, bf16[128,128]{1,0:T(8,128)(2,1)S(1)}, u32[]{:S(2)}, u32[]{:S(2)}) collective-permute-start(bf16[128,128]{1,0:T(8,128)(2,1)S(1)} %get-tuple-element.89), channel_id=1, source_target_pairs={{0,6},{1,7},{2,4},{3,5},{4,2},{5,3},{6,0},{7,1},{8,14},{9,15},{10,... | collective-permute-start | bytes 98312 | tf_op jit(solution)/shard_map/ppermute | solution.py:476
  49.5 1.4 %collective-permute-done.15.refs_1_ = bf16[128,128]{1,0:T(8,128)(2,1)S(1)} collective-permute-done((bf16[128,128]{1,0:T(8,128)(2,1)S(1)}, bf16[128,128]{1,0:T(8,128)(2,1)S(1)}, u32[]{:S(2)}, u32[]{:S(2)}) %collective-permute-start.15) | collective-permute-done | bytes 32800 | tf_op jit(solution)/shard_map/ppermute | solution.py:476
  50.9 1.9 %collective-permute-done.16.refs_2_ = bf16[128,128]{1,0:T(8,128)(2,1)S(1)} collective-permute-done((bf16[128,128]{1,0:T(8,128)(2,1)S(1)}, bf16[128,128]{1,0:T(8,128)(2,1)S(1)}, u32[]{:S(2)}, u32[]{:S(2)}) %collective-permute-start.16) | collective-permute-done | bytes 32800 | tf_op jit(solution)/shard_map/ppermute | solution.py:476
  (41 shorter events, 7.7 us)
Async XLA Ops:
  0.6 9.0 %copy-start = (bf16[4,1024,128]{2,1,0:T(8,128)(2,1)S(1)}, bf16[4,1024,128]{2,1,0:T(8,128)(2,1)}, u32[]{:S(2)}) copy-start(bf16[4,1024,128]{2,1,0:T(8,128)(2,1)} %param.9) | copy-start | bytes 3145732
  2.1 8.5 %collective-permute-start = (bf16[512,128]{1,0:T(8,128)(2,1)S(1)}, bf16[512,128]{1,0:T(8,128)(2,1)S(1)}, u32[]{:S(2)}, u32[]{:S(2)}) collective-permute-start(bf16[512,128]{1,0:T(8,128)(2,1)S(1)} %get-tuple-element.47), channel_id=1, source_target_pairs={{0,2},{1,3},{2,0},{3,1},{4,6},{5,7},{6,4},{7,5},{8,10},{9,11},{10,... | collective-permute-start | bytes 393224 | tf_op jit(solution)/shard_map/ppermute | solution.py:476
  5.2 6.4 %collective-permute-start.1 = (bf16[512,128]{1,0:T(8,128)(2,1)S(1)}, bf16[512,128]{1,0:T(8,128)(2,1)S(1)}, u32[]{:S(2)}, u32[]{:S(2)}) collective-permute-start(bf16[512,128]{1,0:T(8,128)(2,1)S(1)} %get-tuple-element.48), channel_id=1, source_target_pairs={{0,4},{1,5},{2,6},{3,7},{4,0},{5,1},{6,2},{7,3},{8,12},{9,13},{10,... | collective-permute-start | bytes 393224 | tf_op jit(solution)/shard_map/ppermute | solution.py:476
  6.7 7.3 %collective-permute-start.2 = (bf16[512,128]{1,0:T(8,128)(2,1)S(1)}, bf16[512,128]{1,0:T(8,128)(2,1)S(1)}, u32[]{:S(2)}, u32[]{:S(2)}) collective-permute-start(bf16[512,128]{1,0:T(8,128)(2,1)S(1)} %get-tuple-element.49), channel_id=1, source_target_pairs={{0,6},{1,7},{2,4},{3,5},{4,2},{5,3},{6,0},{7,1},{8,14},{9,15},{10,... | collective-permute-start | bytes 393224 | tf_op jit(solution)/shard_map/ppermute | solution.py:476
  6.7 9.0 %collective-permute-start.5 = (bf16[512,128]{1,0:T(8,128)(2,1)S(1)}, bf16[512,128]{1,0:T(8,128)(2,1)S(1)}, u32[]{:S(2)}, u32[]{:S(2)}) collective-permute-start(bf16[512,128]{1,0:T(8,128)(2,1)S(1)} %get-tuple-element.65), channel_id=1, source_target_pairs={{0,6},{1,7},{2,4},{3,5},{4,2},{5,3},{6,0},{7,1},{8,14},{9,15},{10,... | collective-permute-start | bytes 393224 | tf_op jit(solution)/shard_map/ppermute | solution.py:476
  14.9 1.4 %collective-permute-start.6 = (bf16[512,128]{1,0:T(8,128)(2,1)S(1)}, bf16[512,128]{1,0:T(8,128)(2,1)S(1)}, u32[]{:S(2)}, u32[]{:S(2)}) collective-permute-start(bf16[512,128]{1,0:T(8,128)(2,1)S(1)} %get-tuple-element.68), channel_id=1, source_target_pairs={{0,1},{1,0},{2,3},{3,2},{4,5},{5,4},{6,7},{7,6},{8,9},{9,8},{10,11... | collective-permute-start | bytes 393224 | tf_op jit(solution)/shard_map/ppermute | solution.py:476
  16.4 8.2 %collective-permute-start.7 = (bf16[512,128]{1,0:T(8,128)(2,1)S(1)}, bf16[512,128]{1,0:T(8,128)(2,1)S(1)}, u32[]{:S(2)}, u32[]{:S(2)}) collective-permute-start(bf16[512,128]{1,0:T(8,128)(2,1)S(1)} %add_convert_fusion.own_ref), channel_id=1, source_target_pairs={{0,12},{1,13},{2,14},{3,15},{4,8},{5,9},{6,10},{7,11},{8,4},{9,5},... | collective-permute-start | bytes 393224 | tf_op jit(solution)/shard_map/ppermute | solution.py:476
  20.2 5.6 %collective-permute-start.3 = (bf16[512,128]{1,0:T(8,128)(2,1)S(1)}, bf16[512,128]{1,0:T(8,128)(2,1)S(1)}, u32[]{:S(2)}, u32[]{:S(2)}) collective-permute-start(bf16[512,128]{1,0:T(8,128)(2,1)S(1)} %get-tuple-element.51), channel_id=1, source_target_pairs={{0,2},{1,3},{2,0},{3,1},{4,6},{5,7},{6,4},{7,5},{8,10},{9,11},{10,... | collective-permute-start | bytes 393224 | tf_op jit(solution)/shard_map/ppermute | solution.py:476
  21.8 5.3 %collective-permute-start.4 = (bf16[512,128]{1,0:T(8,128)(2,1)S(1)}, bf16[512,128]{1,0:T(8,128)(2,1)S(1)}, u32[]{:S(2)}, u32[]{:S(2)}) collective-permute-start(bf16[512,128]{1,0:T(8,128)(2,1)S(1)} %get-tuple-element.52), channel_id=1, source_target_pairs={{0,4},{1,5},{2,6},{3,7},{4,0},{5,1},{6,2},{7,3},{8,12},{9,13},{10,... | collective-permute-start | bytes 393224 | tf_op jit(solution)/shard_map/ppermute | solution.py:476
  24.7 2.3 %collective-permute-start.8 = (bf16[512,128]{1,0:T(8,128)(2,1)S(1)}, bf16[512,128]{1,0:T(8,128)(2,1)S(1)}, u32[]{:S(2)}, u32[]{:S(2)}) collective-permute-start(bf16[512,128]{1,0:T(8,128)(2,1)S(1)} %shard_map.91.refs_4_), channel_id=1, source_target_pairs={{0,1},{1,0},{2,3},{3,2},{4,5},{5,4},{6,7},{7,6},{8,9},{9,8},{10,11... | collective-permute-start | bytes 393224 | tf_op jit(solution)/shard_map/ppermute | solution.py:476
  28.4 1.7 %collective-permute-start.10 = (bf16[272,256]{1,0:T(8,128)(2,1)S(1)}, bf16[272,256]{1,0:T(8,128)(2,1)S(1)}, u32[]{:S(2)}, u32[]{:S(2)}) collective-permute-start(bf16[272,256]{1,0:T(8,128)(2,1)S(1)} %get-tuple-element.80), channel_id=1, source_target_pairs={{0,1},{1,0},{2,3},{3,2},{4,5},{5,4},{6,7},{7,6},{8,9},{9,8},{10,11... | collective-permute-start | bytes 417800 | tf_op jit(solution)/shard_map/ppermute | solution.py:476
  28.5 4.7 %copy-start.1 = (bf16[8,4,8,128]{3,2,1,0:T(8,128)(2,1)S(1)}, bf16[8,4,8,128]{3,2,1,0:T(8,128)(2,1)}, u32[]{:S(2)}) copy-start(bf16[8,4,8,128]{3,2,1,0:T(8,128)(2,1)} %refs_13_.1) | copy-start | bytes 196612
  28.5 4.6 %copy-start.2 = (s32[8,4,32]{2,1,0:T(4,128)S(1)}, s32[8,4,32]{2,1,0:T(4,128)}, u32[]{:S(2)}) copy-start(s32[8,4,32]{2,1,0:T(4,128)} %refs_14_.1) | copy-start | bytes 12292
  28.5 4.6 %copy-start.3 = (s32[4,64]{1,0:T(4,128)S(1)}, s32[4,64]{1,0:T(4,128)}, u32[]{:S(2)}) copy-start(s32[4,64]{1,0:T(4,128)} %refs_4_.1) | copy-start | bytes 3076
  28.5 4.6 %copy-start.4 = (s32[8]{0:T(128)S(1)}, s32[8]{0:T(128)}, u32[]{:S(2)}) copy-start(s32[8]{0:T(128)} %refs_3_.1) | copy-start | bytes 100
  29.0 6.4 %collective-permute-start.9 = (bf16[272,256]{1,0:T(8,128)(2,1)S(1)}, bf16[272,256]{1,0:T(8,128)(2,1)S(1)}, u32[]{:S(2)}, u32[]{:S(2)}) collective-permute-start(bf16[272,256]{1,0:T(8,128)(2,1)S(1)} %shard_map.95), channel_id=1, source_target_pairs={{0,1},{1,0},{2,3},{3,2},{4,5},{5,4},{6,7},{7,6},{8,9},{9,8},{10,11... | collective-permute-start | bytes 417800 | tf_op jit(solution)/shard_map/ppermute | solution.py:476
  30.1 7.6 %collective-permute-start.11 = (bf16[272,256]{1,0:T(8,128)(2,1)S(1)}, bf16[272,256]{1,0:T(8,128)(2,1)S(1)}, u32[]{:S(2)}, u32[]{:S(2)}) collective-permute-start(bf16[272,256]{1,0:T(8,128)(2,1)S(1)} %shard_map.98), channel_id=1, source_target_pairs={{0,12},{1,13},{2,14},{3,15},{4,8},{5,9},{6,10},{7,11},{8,4},{9,5},... | collective-permute-start | bytes 417800 | tf_op jit(solution)/shard_map/ppermute | solution.py:476
  38.2 1.2 %collective-permute-start.12 = (f32[72,128]{1,0:T(8,128)S(1)}, f32[72,128]{1,0:T(8,128)S(1)}, u32[]{:S(2)}, u32[]{:S(2)}) collective-permute-start(f32[72,128]{1,0:T(8,128)S(1)} %get-tuple-element.85.own_ref), channel_id=1, source_target_pairs={{0,1},{1,0},{2,3},{3,2},{4,5},{5,4},{6,7},{7,6},{8,9},{9,8},{10,11... | collective-permute-start | bytes 110600 | tf_op jit(solution)/shard_map/ppermute | solution.py:476
  39.7 5.6 %collective-permute-start.13 = (bf16[80,128]{1,0:T(8,128)(2,1)S(1)}, bf16[80,128]{1,0:T(8,128)(2,1)S(1)}, u32[]{:S(2)}, u32[]{:S(2)}) collective-permute-start(bf16[80,128]{1,0:T(8,128)(2,1)S(1)} %shard_map.101.own_ref), channel_id=1, source_target_pairs={{0,12},{1,13},{2,14},{3,15},{4,8},{5,9},{6,10},{7,11},{8,4},{9,5},... | collective-permute-start | bytes 61448 | tf_op jit(solution)/shard_map/ppermute | solution.py:476
  45.5 4.0 %collective-permute-start.14 = (bf16[128,128]{1,0:T(8,128)(2,1)S(1)}, bf16[128,128]{1,0:T(8,128)(2,1)S(1)}, u32[]{:S(2)}, u32[]{:S(2)}) collective-permute-start(bf16[128,128]{1,0:T(8,128)(2,1)S(1)} %get-tuple-element.87), channel_id=1, source_target_pairs={{0,2},{1,3},{2,0},{3,1},{4,6},{5,7},{6,4},{7,5},{8,10},{9,11},{10,... | collective-permute-start | bytes 98312 | tf_op jit(solution)/shard_map/ppermute | solution.py:476
  46.9 3.9 %collective-permute-start.15 = (bf16[128,128]{1,0:T(8,128)(2,1)S(1)}, bf16[128,128]{1,0:T(8,128)(2,1)S(1)}, u32[]{:S(2)}, u32[]{:S(2)}) collective-permute-start(bf16[128,128]{1,0:T(8,128)(2,1)S(1)} %get-tuple-element.88), channel_id=1, source_target_pairs={{0,4},{1,5},{2,6},{3,7},{4,0},{5,1},{6,2},{7,3},{8,12},{9,13},{10,... | collective-permute-start | bytes 98312 | tf_op jit(solution)/shard_map/ppermute | solution.py:476
  47.9 4.8 %collective-permute-start.16 = (bf16[128,128]{1,0:T(8,128)(2,1)S(1)}, bf16[128,128]{1,0:T(8,128)(2,1)S(1)}, u32[]{:S(2)}, u32[]{:S(2)}) collective-permute-start(bf16[128,128]{1,0:T(8,128)(2,1)S(1)} %get-tuple-element.89), channel_id=1, source_target_pairs={{0,6},{1,7},{2,4},{3,5},{4,2},{5,3},{6,0},{7,1},{8,14},{9,15},{10,... | collective-permute-start | bytes 98312 | tf_op jit(solution)/shard_map/ppermute | solution.py:476

commit v9 on v8

--- a/solution.py
+++ b/solution.py
@@ -232,11 +232,14 @@
     for key_ref in pair_refs[:count]:
         tokens = key_ref.shape[0]
         chunk = slice(first, first + tokens)
-        total = fill_raised(cent_ref, unit_ref[chunk, :], raised_ref, 0, 0)
-        inverse = 1.0 / (total_ref[0:1, chunk] + total)
+        unit_keys = unit_ref[chunk, :]
+        total = total_ref[0:1, chunk] + fill_raised(
+            cent_ref.at[pl.ds(0, rows)], unit_keys, early_ref, 0, first
+        )
+        total = total + fill_raised(cent_ref.at[pl.ds(rows, rows)], unit_keys, raised_ref, 0, 0)
+        inverse = 1.0 / total
         inverse_ref[:, chunk] = jnp.broadcast_to(inverse, (8, tokens))
-        fill_weights(raised_ref, inverse, weight_ref, rows, rows, first, 0, mass_ref)
-        early_ref[:, chunk] = raised_ref[:rows, :tokens]
+        fill_weights(raised_ref, inverse, weight_ref, rows, 0, first, 0, mass_ref)
         first += tokens
     masses = jnp.sum(mass_ref[...].T, axis=0, keepdims=True)
     send_ref[rows:, :] = packed_masses(masses, lanes)
@@ -556,7 +559,7 @@
         functools.partial(other_half_kernel, heads),
         [sent, shape((8, tokens), F32), shape((part, tokens), F32)],
         [*keys, *values, unit_keys, other_cents, total],
-        [pltpu.VMEM((half, tok_dev), F32), *part_scratch],
+        [pltpu.VMEM((part, tok_dev), F32), *part_scratch],
         pass_flops * heads // 2,
     )
     later = call(

time: 53.6 us -> 53.6 us (level)
  no operation moved by 1% of the time
where the time goes in v9:
time: 53.6 us; the launch traced here: 53.4 us
  starting transfers between devices  23.4 us (44%)
  waiting for transfers between devices  16.1 us (30%)
  Pallas kernels  11.5 us (21%)
  local copies, waits for them, and re-layouts  1.49 us (3%)
  between operations  0.92 us (2%)
    ppermute x17, starting transfers between devices, over(): return lax.ppermute(array, 'ctx', [(i, i ^ bit) for i in range(devices)])  23.4 us
    ppermute x17, waiting for transfers between devices, over(): return lax.ppermute(array, 'ctx', [(i, i ^ bit) for i in range(devices)])  16.1 us
    pallas_call x18, Pallas kernels, call(): pl.pallas_call(kernel, out_shape=tuple(outs), in_specs=in_specs, out_spec...  11.5 us
    squeeze x1, local copies, waits for them, and re-layouts, pick(): return lax.dynamic_index_in_dim(array, at, axis, keepdims=False)  1.43 us
  transfers between devices with their start and end apart: 17, of which 11 were waited for; matrix products, arithmetic and copies ran while one was open for 0% of the time, Pallas kernels for 16%

profile of v9, /device:TPU:0, one launch (start us, length us, event | category | flops | bytes accessed | tf_op | source)
XLA Modules:
  0.0 53.4 jit_solution(17451069428508603648)
XLA Ops:
  0.7 1.4 %dynamic-slice_bitcast_fusion = (bf16[512,128]{1,0:T(8,128)(2,1)S(1)}, bf16[512,128]{1,0:T(8,128)(2,1)S(1)}, bf16[512,128]{1,0:T(8,128)(2,1)S(1)}, bf16[512,128]...) fusion(bf16[4,512,128]{2,1,0:T(8,128)(2,1)} %param.8, ...), kind=kLoop, calls=%fused_computation.1 | loop fusion | bytes 2097168 | tf_op jit(solution)/shard_map/jit(dynamic_index_in_dim)/squeeze | solution.py:482
  2.1 3.0 %collective-permute-start = (bf16[512,128]{1,0:T(8,128)(2,1)S(1)}, bf16[512,128]{1,0:T(8,128)(2,1)S(1)}, u32[]{:S(2)}, u32[]{:S(2)}) collective-permute-start(bf16[512,128]{1,0:T(8,128)(2,1)S(1)} %get-tuple-element.47), channel_id=1, source_target_pairs={{0,2},{1,3},{2,0},{3,1},{4,6},{5,7},{6,4},{7,5},{8,10},{9,11},{10,... | collective-permute-start | bytes 393224 | tf_op jit(solution)/shard_map/ppermute | solution.py:479
  5.2 1.6 %collective-permute-start.1 = (bf16[512,128]{1,0:T(8,128)(2,1)S(1)}, bf16[512,128]{1,0:T(8,128)(2,1)S(1)}, u32[]{:S(2)}, u32[]{:S(2)}) collective-permute-start(bf16[512,128]{1,0:T(8,128)(2,1)S(1)} %get-tuple-element.48), channel_id=1, source_target_pairs={{0,4},{1,5},{2,6},{3,7},{4,0},{5,1},{6,2},{7,3},{8,12},{9,13},{10,... | collective-permute-start | bytes 393224 | tf_op jit(solution)/shard_map/ppermute | solution.py:479
  6.7 2.9 %collective-permute-start.5 = (bf16[512,128]{1,0:T(8,128)(2,1)S(1)}, bf16[512,128]{1,0:T(8,128)(2,1)S(1)}, u32[]{:S(2)}, u32[]{:S(2)}) collective-permute-start(bf16[512,128]{1,0:T(8,128)(2,1)S(1)} %get-tuple-element.65), channel_id=1, source_target_pairs={{0,6},{1,7},{2,4},{3,5},{4,2},{5,3},{6,0},{7,1},{8,14},{9,15},{10,... | collective-permute-start | bytes 393224 | tf_op jit(solution)/shard_map/ppermute | solution.py:479
  9.7 0.9 %shard_map.86 = (f32[512,128]{1,0:T(8,128)S(1)}, f32[512,512]{1,0:T(8,128)S(1)}, f32[8,512]{1,0:T(8,128)S(1)}, bf16[1024,128]{1,0:T(8,128)(2,1)S(1)}) custom-call(s32[1]{0:T(128)} %bitcast.9.base_ref.refs_2_, bf16[512,128]{1,0:T(8,128)(2,1)S(1)} %get-tuple-element.46.refs_0_.refs_5_, bf16[16,64,128]{2,1,0:T(8,128)(2,1)S(1)} %bitcast.25), custom_call_target="tpu_custom_call" | custom-call | flops 268435456 | bytes 1982468 | tf_op jit(solution)/shard_map/pallas_call | solution.py:64
  10.6 0.9 %shard_map.87 = (f32[512,128]{1,0:T(8,128)S(1)}, f32[512,512]{1,0:T(8,128)S(1)}, f32[8,512]{1,0:T(8,128)S(1)}) custom-call(bf16[512,128]{1,0:T(8,128)(2,1)S(1)} %collective-permute-done.key_ref.refs_1_.refs_6_, bf16[1024,128]{1,0:T(8,128)(2,1)S(1)} %get-tuple-element.54.unit_ref, f32[512,128]{1,0:T(8,128)S(1)} %get-tuple-element.55.before_ref), custom_call_target="tpu_custom_call" | custom-call | flops 268435456 | bytes 1982464 | tf_op jit(solution)/shard_map/pallas_call | solution.py:64
  12.4 1.6 %collective-permute-done.2.key_ref.refs_3_.refs_8_ = bf16[512,128]{1,0:T(8,128)(2,1)S(1)} collective-permute-done((bf16[512,128]{1,0:T(8,128)(2,1)S(1)}, bf16[512,128]{1,0:T(8,128)(2,1)S(1)}, u32[]{:S(2)}, u32[]{:S(2)}) %collective-permute-start.2) | collective-permute-done | bytes 131104 | tf_op jit(solution)/shard_map/ppermute | solution.py:479
  16.4 3.9 %collective-permute-start.7 = (bf16[512,128]{1,0:T(8,128)(2,1)S(1)}, bf16[512,128]{1,0:T(8,128)(2,1)S(1)}, u32[]{:S(2)}, u32[]{:S(2)}) collective-permute-start(bf16[512,128]{1,0:T(8,128)(2,1)S(1)} %add_convert_fusion.own_ref), channel_id=1, source_target_pairs={{0,12},{1,13},{2,14},{3,15},{4,8},{5,9},{6,10},{7,11},{8,4},{9,5},... | collective-permute-start | bytes 393224 | tf_op jit(solution)/shard_map/ppermute | solution.py:479
  20.2 1.5 %collective-permute-start.3 = (bf16[512,128]{1,0:T(8,128)(2,1)S(1)}, bf16[512,128]{1,0:T(8,128)(2,1)S(1)}, u32[]{:S(2)}, u32[]{:S(2)}) collective-permute-start(bf16[512,128]{1,0:T(8,128)(2,1)S(1)} %get-tuple-element.51), channel_id=1, source_target_pairs={{0,2},{1,3},{2,0},{3,1},{4,6},{5,7},{6,4},{7,5},{8,10},{9,11},{10,... | collective-permute-start | bytes 393224 | tf_op jit(solution)/shard_map/ppermute | solution.py:479
  21.8 2.8 %collective-permute-done.7.recv_ref = bf16[512,128]{1,0:T(8,128)(2,1)S(1)} collective-permute-done((bf16[512,128]{1,0:T(8,128)(2,1)S(1)}, bf16[512,128]{1,0:T(8,128)(2,1)S(1)}, u32[]{:S(2)}, u32[]{:S(2)}) %collective-permute-start.7) | collective-permute-done | bytes 131104 | tf_op jit(solution)/shard_map/ppermute | solution.py:479
  24.8 1.0 %shard_map.92 = (bf16[2048,128]{1,0:T(8,128)(2,1)S(1)}, f32[512,2048]{1,0:T(8,128)S(1)}, f32[8,2048]{1,0:T(8,128)S(1)}) custom-call(bf16[512,128]{1,0:T(8,128)(2,1)S(1)} %get-tuple-element.46.refs_0_.refs_5_, bf16[512,128]{1,0:T(8,128)(2,1)S(1)} %collective-permute-done.key_ref.refs_1_.refs_6_, ...), custom_call_target="tpu_custom_call" | custom-call | flops 268435456 | bytes 5439488 | tf_op jit(solution)/shard_map/pallas_call | solution.py:64
  25.8 1.2 %collective-permute-done.4.refs_6_.refs_11_ = bf16[512,128]{1,0:T(8,128)(2,1)S(1)} collective-permute-done((bf16[512,128]{1,0:T(8,128)(2,1)S(1)}, bf16[512,128]{1,0:T(8,128)(2,1)S(1)}, u32[]{:S(2)}, u32[]{:S(2)}) %collective-permute-start.4) | collective-permute-done | bytes 131104 | tf_op jit(solution)/shard_map/ppermute | solution.py:479
  27.1 1.3 %shard_map.93 = (bf16[272,256]{1,0:T(8,128)(2,1)S(1)}, f32[8,2048]{1,0:T(8,128)S(1)}, f32[256,2048]{1,0:T(8,128)S(1)}) custom-call(bf16[512,128]{1,0:T(8,128)(2,1)S(1)} %get-tuple-element.46.refs_0_.refs_5_, bf16[512,128]{1,0:T(8,128)(2,1)S(1)} %collective-permute-done.key_ref.refs_1_.refs_6_, ...), custom_call_target="tpu_custom_call" | custom-call | flops 536870912 | bytes 4071424 | tf_op jit(solution)/shard_map/pallas_call | solution.py:64
  30.1 3.0 %collective-permute-start.11 = (bf16[272,256]{1,0:T(8,128)(2,1)S(1)}, bf16[272,256]{1,0:T(8,128)(2,1)S(1)}, u32[]{:S(2)}, u32[]{:S(2)}) collective-permute-start(bf16[272,256]{1,0:T(8,128)(2,1)S(1)} %shard_map.98), channel_id=1, source_target_pairs={{0,12},{1,13},{2,14},{3,15},{4,8},{5,9},{6,10},{7,11},{8,4},{9,5},... | collective-permute-start | bytes 417800 | tf_op jit(solution)/shard_map/ppermute | solution.py:479
  33.1 1.7 %shard_map.99 = (f32[72,128]{1,0:T(8,128)S(1)}, f32[64,128]{1,0:T(8,128)S(1)}, f32[64,256]{1,0:T(8,128)S(1)}) custom-call(s32[1]{0:T(128)} %bitcast.refs_0_.head_ref, s32[1]{0:T(128)} %bitcast.11.refs_1_, s32[1]{0:T(128)} %bitcast.9.base_ref.refs_2_, s32[8]{0:T(128)S(1)} %copy-done.4, s32[4,64]{1,0:T(4,128)S(1)} %copy-done.3, ...), custom_call_target="tpu_custom_call" | custom-call | flops 67108864 | bytes 1254444 | tf_op jit(solution)/shard_map/pallas_call | solution.py:64
  35.4 2.3 %collective-permute-done.11.recv_ref = bf16[272,256]{1,0:T(8,128)(2,1)S(1)} collective-permute-done((bf16[272,256]{1,0:T(8,128)(2,1)S(1)}, bf16[272,256]{1,0:T(8,128)(2,1)S(1)}, u32[]{:S(2)}, u32[]{:S(2)}) %collective-permute-start.11) | collective-permute-done | bytes 139296 | tf_op jit(solution)/shard_map/ppermute | solution.py:479
  38.3 1.2 %collective-permute-done.12.recv_ref = f32[72,128]{1,0:T(8,128)S(1)} collective-permute-done((f32[72,128]{1,0:T(8,128)S(1)}, f32[72,128]{1,0:T(8,128)S(1)}, u32[]{:S(2)}, u32[]{:S(2)}) %collective-permute-start.12) | collective-permute-done | bytes 36896 | tf_op jit(solution)/shard_map/ppermute | solution.py:479
  39.7 3.1 %collective-permute-start.13 = (bf16[80,128]{1,0:T(8,128)(2,1)S(1)}, bf16[80,128]{1,0:T(8,128)(2,1)S(1)}, u32[]{:S(2)}, u32[]{:S(2)}) collective-permute-start(bf16[80,128]{1,0:T(8,128)(2,1)S(1)} %shard_map.101.own_ref), channel_id=1, source_target_pairs={{0,12},{1,13},{2,14},{3,15},{4,8},{5,9},{6,10},{7,11},{8,4},{9,5},... | collective-permute-start | bytes 61448 | tf_op jit(solution)/shard_map/ppermute | solution.py:479
  42.8 2.5 %collective-permute-done.13.recv_ref = bf16[80,128]{1,0:T(8,128)(2,1)S(1)} collective-permute-done((bf16[80,128]{1,0:T(8,128)(2,1)S(1)}, bf16[80,128]{1,0:T(8,128)(2,1)S(1)}, u32[]{:S(2)}, u32[]{:S(2)}) %collective-permute-start.13) | collective-permute-done | bytes 20512 | tf_op jit(solution)/shard_map/ppermute | solution.py:479
  45.5 1.5 %collective-permute-start.14 = (bf16[128,128]{1,0:T(8,128)(2,1)S(1)}, bf16[128,128]{1,0:T(8,128)(2,1)S(1)}, u32[]{:S(2)}, u32[]{:S(2)}) collective-permute-start(bf16[128,128]{1,0:T(8,128)(2,1)S(1)} %get-tuple-element.87), channel_id=1, source_target_pairs={{0,2},{1,3},{2,0},{3,1},{4,6},{5,7},{6,4},{7,5},{8,10},{9,11},{10,... | collective-permute-start | bytes 98312 | tf_op jit(solution)/shard_map/ppermute | solution.py:479
  46.9 1.0 %collective-permute-start.15 = (bf16[128,128]{1,0:T(8,128)(2,1)S(1)}, bf16[128,128]{1,0:T(8,128)(2,1)S(1)}, u32[]{:S(2)}, u32[]{:S(2)}) collective-permute-start(bf16[128,128]{1,0:T(8,128)(2,1)S(1)} %get-tuple-element.88), channel_id=1, source_target_pairs={{0,4},{1,5},{2,6},{3,7},{4,0},{5,1},{6,2},{7,3},{8,12},{9,13},{10,... | collective-permute-start | bytes 98312 | tf_op jit(solution)/shard_map/ppermute | solution.py:479
  47.9 1.1 %collective-permute-start.16 = (bf16[128,128]{1,0:T(8,128)(2,1)S(1)}, bf16[128,128]{1,0:T(8,128)(2,1)S(1)}, u32[]{:S(2)}, u32[]{:S(2)}) collective-permute-start(bf16[128,128]{1,0:T(8,128)(2,1)S(1)} %get-tuple-element.89), channel_id=1, source_target_pairs={{0,6},{1,7},{2,4},{3,5},{4,2},{5,3},{6,0},{7,1},{8,14},{9,15},{10,... | collective-permute-start | bytes 98312 | tf_op jit(solution)/shard_map/ppermute | solution.py:479
  49.4 1.4 %collective-permute-done.15.refs_1_ = bf16[128,128]{1,0:T(8,128)(2,1)S(1)} collective-permute-done((bf16[128,128]{1,0:T(8,128)(2,1)S(1)}, bf16[128,128]{1,0:T(8,128)(2,1)S(1)}, u32[]{:S(2)}, u32[]{:S(2)}) %collective-permute-start.15) | collective-permute-done | bytes 32800 | tf_op jit(solution)/shard_map/ppermute | solution.py:479
  50.9 1.9 %collective-permute-done.16.refs_2_ = bf16[128,128]{1,0:T(8,128)(2,1)S(1)} collective-permute-done((bf16[128,128]{1,0:T(8,128)(2,1)S(1)}, bf16[128,128]{1,0:T(8,128)(2,1)S(1)}, u32[]{:S(2)}, u32[]{:S(2)}) %collective-permute-start.16) | collective-permute-done | bytes 32800 | tf_op jit(solution)/shard_map/ppermute | solution.py:479
  (41 shorter events, 7.7 us)
Async XLA Ops:
  0.6 9.0 %copy-start = (bf16[4,1024,128]{2,1,0:T(8,128)(2,1)S(1)}, bf16[4,1024,128]{2,1,0:T(8,128)(2,1)}, u32[]{:S(2)}) copy-start(bf16[4,1024,128]{2,1,0:T(8,128)(2,1)} %param.9) | copy-start | bytes 3145732
  2.1 8.5 %collective-permute-start = (bf16[512,128]{1,0:T(8,128)(2,1)S(1)}, bf16[512,128]{1,0:T(8,128)(2,1)S(1)}, u32[]{:S(2)}, u32[]{:S(2)}) collective-permute-start(bf16[512,128]{1,0:T(8,128)(2,1)S(1)} %get-tuple-element.47), channel_id=1, source_target_pairs={{0,2},{1,3},{2,0},{3,1},{4,6},{5,7},{6,4},{7,5},{8,10},{9,11},{10,... | collective-permute-start | bytes 393224 | tf_op jit(solution)/shard_map/ppermute | solution.py:479
  5.2 6.4 %collective-permute-start.1 = (bf16[512,128]{1,0:T(8,128)(2,1)S(1)}, bf16[512,128]{1,0:T(8,128)(2,1)S(1)}, u32[]{:S(2)}, u32[]{:S(2)}) collective-permute-start(bf16[512,128]{1,0:T(8,128)(2,1)S(1)} %get-tuple-element.48), channel_id=1, source_target_pairs={{0,4},{1,5},{2,6},{3,7},{4,0},{5,1},{6,2},{7,3},{8,12},{9,13},{10,... | collective-permute-start | bytes 393224 | tf_op jit(solution)/shard_map/ppermute | solution.py:479
  6.7 7.3 %collective-permute-start.2 = (bf16[512,128]{1,0:T(8,128)(2,1)S(1)}, bf16[512,128]{1,0:T(8,128)(2,1)S(1)}, u32[]{:S(2)}, u32[]{:S(2)}) collective-permute-start(bf16[512,128]{1,0:T(8,128)(2,1)S(1)} %get-tuple-element.49), channel_id=1, source_target_pairs={{0,6},{1,7},{2,4},{3,5},{4,2},{5,3},{6,0},{7,1},{8,14},{9,15},{10,... | collective-permute-start | bytes 393224 | tf_op jit(solution)/shard_map/ppermute | solution.py:479
  6.7 9.0 %collective-permute-start.5 = (bf16[512,128]{1,0:T(8,128)(2,1)S(1)}, bf16[512,128]{1,0:T(8,128)(2,1)S(1)}, u32[]{:S(2)}, u32[]{:S(2)}) collective-permute-start(bf16[512,128]{1,0:T(8,128)(2,1)S(1)} %get-tuple-element.65), channel_id=1, source_target_pairs={{0,6},{1,7},{2,4},{3,5},{4,2},{5,3},{6,0},{7,1},{8,14},{9,15},{10,... | collective-permute-start | bytes 393224 | tf_op jit(solution)/shard_map/ppermute | solution.py:479
  14.9 1.4 %collective-permute-start.6 = (bf16[512,128]{1,0:T(8,128)(2,1)S(1)}, bf16[512,128]{1,0:T(8,128)(2,1)S(1)}, u32[]{:S(2)}, u32[]{:S(2)}) collective-permute-start(bf16[512,128]{1,0:T(8,128)(2,1)S(1)} %get-tuple-element.68), channel_id=1, source_target_pairs={{0,1},{1,0},{2,3},{3,2},{4,5},{5,4},{6,7},{7,6},{8,9},{9,8},{10,11... | collective-permute-start | bytes 393224 | tf_op jit(solution)/shard_map/ppermute | solution.py:479
  16.4 8.2 %collective-permute-start.7 = (bf16[512,128]{1,0:T(8,128)(2,1)S(1)}, bf16[512,128]{1,0:T(8,128)(2,1)S(1)}, u32[]{:S(2)}, u32[]{:S(2)}) collective-permute-start(bf16[512,128]{1,0:T(8,128)(2,1)S(1)} %add_convert_fusion.own_ref), channel_id=1, source_target_pairs={{0,12},{1,13},{2,14},{3,15},{4,8},{5,9},{6,10},{7,11},{8,4},{9,5},... | collective-permute-start | bytes 393224 | tf_op jit(solution)/shard_map/ppermute | solution.py:479
  20.2 5.6 %collective-permute-start.3 = (bf16[512,128]{1,0:T(8,128)(2,1)S(1)}, bf16[512,128]{1,0:T(8,128)(2,1)S(1)}, u32[]{:S(2)}, u32[]{:S(2)}) collective-permute-start(bf16[512,128]{1,0:T(8,128)(2,1)S(1)} %get-tuple-element.51), channel_id=1, source_target_pairs={{0,2},{1,3},{2,0},{3,1},{4,6},{5,7},{6,4},{7,5},{8,10},{9,11},{10,... | collective-permute-start | bytes 393224 | tf_op jit(solution)/shard_map/ppermute | solution.py:479
  21.8 5.3 %collective-permute-start.4 = (bf16[512,128]{1,0:T(8,128)(2,1)S(1)}, bf16[512,128]{1,0:T(8,128)(2,1)S(1)}, u32[]{:S(2)}, u32[]{:S(2)}) collective-permute-start(bf16[512,128]{1,0:T(8,128)(2,1)S(1)} %get-tuple-element.52), channel_id=1, source_target_pairs={{0,4},{1,5},{2,6},{3,7},{4,0},{5,1},{6,2},{7,3},{8,12},{9,13},{10,... | collective-permute-start | bytes 393224 | tf_op jit(solution)/shard_map/ppermute | solution.py:479
  24.7 2.3 %collective-permute-start.8 = (bf16[512,128]{1,0:T(8,128)(2,1)S(1)}, bf16[512,128]{1,0:T(8,128)(2,1)S(1)}, u32[]{:S(2)}, u32[]{:S(2)}) collective-permute-start(bf16[512,128]{1,0:T(8,128)(2,1)S(1)} %shard_map.91.refs_4_), channel_id=1, source_target_pairs={{0,1},{1,0},{2,3},{3,2},{4,5},{5,4},{6,7},{7,6},{8,9},{9,8},{10,11... | collective-permute-start | bytes 393224 | tf_op jit(solution)/shard_map/ppermute | solution.py:479
  28.4 1.7 %collective-permute-start.10 = (bf16[272,256]{1,0:T(8,128)(2,1)S(1)}, bf16[272,256]{1,0:T(8,128)(2,1)S(1)}, u32[]{:S(2)}, u32[]{:S(2)}) collective-permute-start(bf16[272,256]{1,0:T(8,128)(2,1)S(1)} %get-tuple-element.80), channel_id=1, source_target_pairs={{0,1},{1,0},{2,3},{3,2},{4,5},{5,4},{6,7},{7,6},{8,9},{9,8},{10,11... | collective-permute-start | bytes 417800 | tf_op jit(solution)/shard_map/ppermute | solution.py:479
  28.5 4.7 %copy-start.1 = (bf16[8,4,8,128]{3,2,1,0:T(8,128)(2,1)S(1)}, bf16[8,4,8,128]{3,2,1,0:T(8,128)(2,1)}, u32[]{:S(2)}) copy-start(bf16[8,4,8,128]{3,2,1,0:T(8,128)(2,1)} %refs_13_.1) | copy-start | bytes 196612
  28.5 4.6 %copy-start.2 = (s32[8,4,32]{2,1,0:T(4,128)S(1)}, s32[8,4,32]{2,1,0:T(4,128)}, u32[]{:S(2)}) copy-start(s32[8,4,32]{2,1,0:T(4,128)} %refs_14_.1) | copy-start | bytes 12292
  28.5 4.6 %copy-start.3 = (s32[4,64]{1,0:T(4,128)S(1)}, s32[4,64]{1,0:T(4,128)}, u32[]{:S(2)}) copy-start(s32[4,64]{1,0:T(4,128)} %refs_4_.1) | copy-start | bytes 3076
  28.5 4.6 %copy-start.4 = (s32[8]{0:T(128)S(1)}, s32[8]{0:T(128)}, u32[]{:S(2)}) copy-start(s32[8]{0:T(128)} %refs_3_.1) | copy-start | bytes 100
  29.0 6.4 %collective-permute-start.9 = (bf16[272,256]{1,0:T(8,128)(2,1)S(1)}, bf16[272,256]{1,0:T(8,128)(2,1)S(1)}, u32[]{:S(2)}, u32[]{:S(2)}) collective-permute-start(bf16[272,256]{1,0:T(8,128)(2,1)S(1)} %shard_map.95), channel_id=1, source_target_pairs={{0,1},{1,0},{2,3},{3,2},{4,5},{5,4},{6,7},{7,6},{8,9},{9,8},{10,11... | collective-permute-start | bytes 417800 | tf_op jit(solution)/shard_map/ppermute | solution.py:479
  30.1 7.6 %collective-permute-start.11 = (bf16[272,256]{1,0:T(8,128)(2,1)S(1)}, bf16[272,256]{1,0:T(8,128)(2,1)S(1)}, u32[]{:S(2)}, u32[]{:S(2)}) collective-permute-start(bf16[272,256]{1,0:T(8,128)(2,1)S(1)} %shard_map.98), channel_id=1, source_target_pairs={{0,12},{1,13},{2,14},{3,15},{4,8},{5,9},{6,10},{7,11},{8,4},{9,5},... | collective-permute-start | bytes 417800 | tf_op jit(solution)/shard_map/ppermute | solution.py:479
  38.2 1.2 %collective-permute-start.12 = (f32[72,128]{1,0:T(8,128)S(1)}, f32[72,128]{1,0:T(8,128)S(1)}, u32[]{:S(2)}, u32[]{:S(2)}) collective-permute-start(f32[72,128]{1,0:T(8,128)S(1)} %get-tuple-element.85.own_ref), channel_id=1, source_target_pairs={{0,1},{1,0},{2,3},{3,2},{4,5},{5,4},{6,7},{7,6},{8,9},{9,8},{10,11... | collective-permute-start | bytes 110600 | tf_op jit(solution)/shard_map/ppermute | solution.py:479
  39.7 5.6 %collective-permute-start.13 = (bf16[80,128]{1,0:T(8,128)(2,1)S(1)}, bf16[80,128]{1,0:T(8,128)(2,1)S(1)}, u32[]{:S(2)}, u32[]{:S(2)}) collective-permute-start(bf16[80,128]{1,0:T(8,128)(2,1)S(1)} %shard_map.101.own_ref), channel_id=1, source_target_pairs={{0,12},{1,13},{2,14},{3,15},{4,8},{5,9},{6,10},{7,11},{8,4},{9,5},... | collective-permute-start | bytes 61448 | tf_op jit(solution)/shard_map/ppermute | solution.py:479
  45.5 4.0 %collective-permute-start.14 = (bf16[128,128]{1,0:T(8,128)(2,1)S(1)}, bf16[128,128]{1,0:T(8,128)(2,1)S(1)}, u32[]{:S(2)}, u32[]{:S(2)}) collective-permute-start(bf16[128,128]{1,0:T(8,128)(2,1)S(1)} %get-tuple-element.87), channel_id=1, source_target_pairs={{0,2},{1,3},{2,0},{3,1},{4,6},{5,7},{6,4},{7,5},{8,10},{9,11},{10,... | collective-permute-start | bytes 98312 | tf_op jit(solution)/shard_map/ppermute | solution.py:479
  46.9 3.9 %collective-permute-start.15 = (bf16[128,128]{1,0:T(8,128)(2,1)S(1)}, bf16[128,128]{1,0:T(8,128)(2,1)S(1)}, u32[]{:S(2)}, u32[]{:S(2)}) collective-permute-start(bf16[128,128]{1,0:T(8,128)(2,1)S(1)} %get-tuple-element.88), channel_id=1, source_target_pairs={{0,4},{1,5},{2,6},{3,7},{4,0},{5,1},{6,2},{7,3},{8,12},{9,13},{10,... | collective-permute-start | bytes 98312 | tf_op jit(solution)/shard_map/ppermute | solution.py:479
  47.9 4.8 %collective-permute-start.16 = (bf16[128,128]{1,0:T(8,128)(2,1)S(1)}, bf16[128,128]{1,0:T(8,128)(2,1)S(1)}, u32[]{:S(2)}, u32[]{:S(2)}) collective-permute-start(bf16[128,128]{1,0:T(8,128)(2,1)S(1)} %get-tuple-element.89), channel_id=1, source_target_pairs={{0,6},{1,7},{2,4},{3,5},{4,2},{5,3},{6,0},{7,1},{8,14},{9,15},{10,... | collective-permute-start | bytes 98312 | tf_op jit(solution)/shard_map/ppermute | solution.py:479
